TPU v7x, 128 devices: a whole 4x4x4 slice. The times are simulated.
128 devices in a mesh: row: 4 (over z), col: 32 (over y, x, core).
Axes of the slice: x: 4, y: 4, z: 4, core: 2. Of those that a mesh axis runs over, the one named last changes fastest.
Arguments:
- samples: bfloat16 [16, 4, 32, 8, 4096], P(None, 'row', 'col'), may hold values from -6 to 6
- ard_weight: float32 [4096], replicated, may hold values from 8.544922e-05 to 0.000769043, as said below
- nugget: bfloat16 [16, 4, 32, 8], P(None, 'row', 'col'), may hold values from 0.29882812 to 3
Outputs:
- factored: float32 [16, 4, 256, 2, 32, 256], P(None, 'row', None, None, 'col')
Inputs may be any that keep to these rules, and one draw needn't show every extreme that they name: `ard_weight`: each weight is positive.
All inputs are finite; a program needn't handle non-finite values.
Results may differ from a plain program's by a relative error of at most 0.00046.
Values may be sent and summed in bfloat16 or wider, within the bound.
No kernel may reach another device: no remote copies, remote signals or barrier semaphores. Data moves between devices by JAX's collectives and lax.ppermute only.
A program may use at most 128 MiB of HBM per device.

v0:
```python
import jax
import jax.numpy as jnp
from jax import lax
from jax.sharding import PartitionSpec as P


def spread(value, axis, source):
    kept = jnp.where(lax.axis_index(axis) == source, value, 0).astype(value.dtype)
    return lax.psum(kept, axis)


def weighted_norms(row_side, ard_weight):
    widened = row_side.astype(jnp.float32)
    return jnp.sum(widened * widened * ard_weight, axis=1)


def weighted_parts(row_side, ard_weight):
    widened = row_side.astype(jnp.float32)
    scaled = (widened * ard_weight).astype(jnp.bfloat16)
    sq_norms = jnp.sum(widened * widened * ard_weight, axis=1)
    return (scaled, sq_norms)


def kernel_block(row_side, row_norms, col_scaled, col_norms):
    cross_term = lax.dot_general(
        row_side, col_scaled, (((1,), (1,)), ((), ())), preferred_element_type=jnp.float32
    )
    return jnp.exp(-0.5 * (row_norms[:, None] + col_norms[None, :] - 2.0 * cross_term))


def solve_panel(corner, blocks):
    tile_width = corner.shape[0]
    stacked = blocks.reshape(-1, tile_width)
    solved = jax.scipy.linalg.solve_triangular(corner, stacked.T, lower=True).T
    return solved.reshape(blocks.shape)


def local(samples, ard_weight, nugget):
    row_count = lax.axis_size("row")
    col_count = lax.axis_size("col")
    row_index = lax.axis_index("row")
    col_index = lax.axis_index("col")
    row_tiles = samples.shape[0]
    features = samples.shape[4]
    tile_width = samples.shape[3] * col_count
    stride = col_count // row_count
    col_tiles = row_tiles // stride
    pick_index = col_index // row_count
    root_row = col_index % row_count
    gathered, nugget_rows = (
        lax.all_gather(samples, "col", axis=2, tiled=True),
        lax.all_gather(nugget, "col", axis=2, tiled=True),
    )
    row_data = gathered.reshape(row_tiles * tile_width, features)
    row_norms = weighted_norms(row_data, ard_weight)
    chosen = lax.dynamic_index_in_dim(
        gathered.reshape(col_tiles, stride, tile_width, features), pick_index, 1, keepdims=False
    )
    col_data = spread(chosen, "row", root_row).reshape(col_tiles * tile_width, features)
    col_scaled, col_norms = weighted_parts(col_data, ard_weight)
    kernel = kernel_block(row_data, row_norms, col_scaled, col_norms).reshape(
        row_tiles, tile_width, col_tiles, tile_width
    )
    tile_rows = lax.broadcasted_iota(jnp.int32, (row_tiles, col_tiles), 0)
    tile_cols = lax.broadcasted_iota(jnp.int32, (row_tiles, col_tiles), 1)
    diag_hit = (tile_rows == tile_cols * stride + pick_index) & (row_index == root_row)
    identity = lax.broadcasted_iota(jnp.int32, (tile_width, tile_width), 0) == lax.broadcasted_iota(
        jnp.int32, (tile_width, tile_width), 1
    )
    row_nugget = nugget_rows.reshape(row_tiles, tile_width).astype(jnp.float32)
    on_diag = diag_hit[:, None, :, None] & identity[None, :, None, :]
    kernel = kernel + jnp.where(on_diag, row_nugget[:, :, None, None], 0.0)
    first_rows = (lax.iota(jnp.int32, row_tiles) == 0) & (row_index == 0)
    first_cols = (lax.iota(jnp.int32, col_tiles) == 0) & (col_index == 0)
    own_corner = jnp.linalg.cholesky(kernel[0, :, 0, :])
    corner = spread(own_corner, "row", 0)
    solved = solve_panel(corner, kernel[:, :, 0, :])
    local_panel = jnp.where(first_rows[:, None, None], corner, solved)
    panel_rows = spread(local_panel, "col", 0)
    picked = lax.dynamic_index_in_dim(
        panel_rows.reshape(col_tiles, stride, tile_width, tile_width), pick_index, 1, keepdims=False
    )
    panel_cols = spread(picked, "row", root_row)
    update = lax.dot_general(
        panel_rows.reshape(-1, tile_width),
        panel_cols.reshape(-1, tile_width),
        (((1,), (1,)), ((), ())),
        precision=lax.Precision.HIGHEST,
        preferred_element_type=jnp.float32,
    )
    trailing = kernel - update.reshape(row_tiles, tile_width, col_tiles, tile_width)
    result = jnp.where(first_rows[:, None, None, None], kernel, trailing)
    result = jnp.where(first_cols[None, None, :, None], panel_rows[:, :, None, :], result)
    return result.reshape(row_tiles, 1, tile_width, col_tiles, 1, tile_width)


def solution(mesh):
    placed = (P(None, "row", "col", None, None), P(), P(None, "row", "col", None))
    return jax.shard_map(
        local,
        mesh=mesh,
        in_specs=placed,
        out_specs=P(None, "row", None, None, "col", None),
        check_vma=False,
    )
```

profile of v0, /device:TPU:0, one launch (start us, length us, event | category | flops | bytes accessed | tf_op | source)
XLA Modules:
  0.0 585.8 jit_solution(12798804643579031588)
XLA Ops:
  6.5 0.0 all-gather.2.cloned.1.call-start
  6.5 0.7 all-gather.2.cloned.1.call-update
  7.3 0.0 all-reduce.6.cloned.1.call-start
  7.3 118.5 %all-gather.2.cloned.1.call-done = bf16[16,1,32,8,4096]{4,3,2,1,0:T(8,128)(2,1)} async-done(((bf16[16,1,1,8,4096]{4,3,2,1,0:T(8,128)(2,1)}), bf16[16,1,32,8,4096]{4,3,2,1,0:T(8,128)(2,1)}) %all-gather.2.cloned.1.call-update) | async-done | bytes 33554448 | tf_op jit(solution)/shard_map/all_gather | solution.py:51
  125.8 4.5 select_bitcast_fusion
  130.3 0.0 copy-start.4
  130.3 0.0 copy-start.3
  130.3 0.0 all-reduce.6.cloned.1.call-update
  130.3 0.0 all-reduce.8.cloned.1.call-start
  130.4 0.6 copy-done.4
  131.0 23.8 %all_gather.7 = bf16[16,1,32,8]{0,3,1,2:T(8,128)(2,1)S(1)} all-gather(bf16[16,1,1,8]{0,3,1,2:T(8,128)(2,1)S(1)} %bitcast.93), channel_id=1, replica_groups=mesh['row'=4,'col'=32] {'col'}, dimensions={2}, use_global_device_ids=true | all-gather | bytes 8448 | tf_op jit(solution)/shard_map/all_gather | solution.py:52
  154.7 0.1 copy.20
  154.9 0.0 copy-done.3
  154.9 12.6 %multiply_reduce_fusion = f32[16,32,8]{2,1,0:T(8,128)S(1)} fusion(bf16[16,1,32,8,4096]{4,3,2,1,0:T(8,128)(2,1)} %all-gather.2.cloned.1.call-done, f32[4096]{0:T(1024)S(1)} %copy-done.3), kind=kLoop, calls=%fused_computation.2 | loop fusion | flops 67104768 | bytes 33587200 | tf_op jit(solution)/shard_map/reduce_sum | solution.py:14
  167.4 0.1 add.70
  167.6 55.4 %all-reduce.6.cloned.1.call-done = bf16[2,256,4096]{2,1,0:T(8,128)(2,1)} async-done(((bf16[2,256,4096]{2,1,0:T(8,128)(2,1)}), bf16[2,256,4096]{2,1,0:T(8,128)(2,1)}) %all-reduce.6.cloned.1.call-update) | async-done | bytes 4194320 | tf_op jit(solution)/shard_map/psum | solution.py:9
  222.9 4.1 fusion.1
  227.1 22.8 %fusion.6 = f32[4096,512]{0,1:T(8,128)S(1)} fusion(bf16[512,4096]{1,0:T(8,128)(2,1)S(1)} %bitcast.91, bf16[4096,4096]{1,0:T(8,128)(2,1)} %bitcast.83, f32[512]{0:T(512)S(1)} %bitcast.94, f32[4096]{0:T(1024)S(1)} %add.70), kind=kOutput, calls=%fused_computation.13 | convolution fusion | flops 17188257792 | bytes 46155776 | tf_op jit(solution)/shard_map/dot_general | solution.py:25
  249.9 3.9 copy.35
  253.8 5.4 copy_add_fusion
  259.1 0.0 copy-start
  259.2 3.4 copy-done
  262.6 0.1 copy.22
  262.7 1.0 fusion.15
  263.7 11.9 %cholesky.50 = f32[128,128]{1,0:T(8,128)S(1)} custom-call(f32[128,128]{1,0:T(8,128)S(1)} %cholesky.118), custom_call_target="Cholesky" | custom-call | tf_op jit(solution)/shard_map/jit(cholesky)/cholesky | solution.py:75
  275.6 9.8 %custom-call.15 = f32[1,128,128]{1,2,0:T(8,128)S(1)} custom-call(f32[1,128,128]{2,1,0:T(8,128)S(1)} %get-tuple-element.28), custom_call_target="InvertDiagBlocksLowerTriangular" | custom-call | tf_op jit(solution)/shard_map/jit(cholesky)/cholesky | solution.py:75
  285.5 0.2 constant_dynamic-update-slice_fusion
  285.7 0.3 convolution_subtract_fusion.1
  285.9 11.7 %cholesky.105 = f32[128,128]{1,0:T(8,128)S(1)} custom-call(f32[128,128]{1,0:T(8,128)S(1)} %convolution_subtract_fusion.1), custom_call_target="Cholesky" | custom-call | tf_op jit(solution)/shard_map/jit(cholesky)/cholesky | solution.py:75
  297.7 0.7 compare_reduce_fusion
  299.7 0.7 select_select_fusion.1
  300.4 0.0 all-reduce.8.cloned.1.call-update
  300.4 0.0 all-reduce.10.cloned.1.call-start
  300.5 4.5 slice.67
  305.0 5.6 copy.23
  310.6 5.6 copy.24
  316.2 26.0 %all-reduce.8.cloned.1.call-done = f32[256,256]{1,0:T(8,128)} async-done(((f32[256,256]{1,0:T(8,128)}), f32[256,256]{1,0:T(8,128)}) %all-reduce.8.cloned.1.call-update) | async-done | bytes 262160 | tf_op jit(solution)/shard_map/psum | solution.py:9
  342.2 1.0 fusion.16
  343.2 0.1 triangular_solve.42
  343.2 3.9 while.1
  343.2 0.6 fusion.31
  343.8 1.3 bitcast_dynamic-update-slice_fusion.2
  345.2 0.6 fusion.31
  345.8 1.3 bitcast_dynamic-update-slice_fusion.2
  347.1 19.7 %custom-call.16 = f32[2,128,128]{1,2,0:T(8,128)S(1)} custom-call(f32[2,128,128]{2,1,0:T(8,128)S(1)} %get-tuple-element.12), custom_call_target="InvertDiagBlocksLowerTriangular" | custom-call | tf_op jit(solution)/shard_map/jit(_solve_triangular)/triangular_solve | solution.py:34
  366.8 0.0 copy-start.1
  366.8 3.6 fusion.11
  370.5 0.0 copy-done.1
  370.5 1.9 convolution_subtract_fusion
  372.4 1.9 fusion.18
  374.4 2.4 maximum_bitcast_fusion
  376.8 0.0 copy-start.2
  376.8 5.6 copy.32
  382.4 0.0 copy-done.2
  382.4 4.6 select_select_fusion
  387.1 0.0 all-reduce.10.cloned.1.call-update
  387.1 0.0 all-reduce.12.cloned.1.call-start
  387.2 111.9 %all-reduce.10.cloned.1.call-done = f32[16,256,256]{2,1,0:T(8,128)} async-done(((f32[16,256,256]{2,1,0:T(8,128)}), f32[16,256,256]{2,1,0:T(8,128)}) %all-reduce.10.cloned.1.call-update) | async-done | bytes 4194320 | tf_op jit(solution)/shard_map/psum | solution.py:9
  499.1 1.9 fusion.13
  500.9 0.0 all-reduce.12.cloned.1.call-update
  501.0 5.6 copy.26
  506.6 37.6 %all-reduce.12.cloned.1.call-done = f32[2,256,256]{2,1,0:T(8,128)} async-done(((f32[2,256,256]{2,1,0:T(8,128)}), f32[2,256,256]{2,1,0:T(8,128)}) %all-reduce.12.cloned.1.call-update) | async-done | bytes 524304 | tf_op jit(solution)/shard_map/psum | solution.py:9
  544.2 14.3 %fusion.4 = f32[16,1,256,2,1,256]{2,5,3,0,4,1:T(8,128)} fusion(f32[16,256,2,256]{1,3,2,0:T(8,128)} %copy-done, f32[16,256,256]{1,2,0:T(8,128)} %copy.26, pred[16]{0:T(512)(128)(4,1)S(1)} %compare_and_fusion, pred[2]{0:T(512)(128)(4,1)S(1)} %compare_and_fusion.1, f32[16,256,256]{2,1,0:T(8,128)} %all-reduce.10.cloned.1.call-done, ...), kind=kOutput, calls=%fused_computation.10 | convolution fusion | flops 6448742400 | bytes 25690130 | tf_op jit(solution)/shard_map/dot_general | solution.py:84
  558.5 20.5 %copy.29 = f32[16,1,256,2,1,256]{5,4,3,2,1,0:T(1,128)} copy(f32[16,1,256,2,1,256]{2,5,3,0,4,1:T(8,128)} %fusion.4) | data formatting | bytes 16777216 | tf_op jit(solution)/shard_map/reshape | solution.py:94
  (16 shorter events, 0.2 us)
Async XLA Ops:
  6.5 119.3 %all-gather.2.cloned.1.call-start = ((), (), s32[]{:S(2)}) async-start(), calls=%async_computation | async-start | bytes 34603008 | tf_op jit(solution)/shard_map/all_gather | solution.py:51
  7.3 215.7 %all-reduce.6.cloned.1.call-start = ((), (), s32[]{:S(2)}) async-start(), calls=%async_computation.1 | async-start | bytes 8388608 | tf_op jit(solution)/shard_map/psum | solution.py:9
  130.3 0.7 copy-start.4
  130.3 24.6 %copy-start.3 = (f32[4096]{0:T(1024)S(1)}, f32[4096]{0:T(1024)}, u32[]{:S(2)}) copy-start(f32[4096]{0:T(1024)} %param.4) | copy-start | bytes 49156
  130.3 211.9 %all-reduce.8.cloned.1.call-start = ((), (), s32[]{:S(2)}) async-start(), calls=%async_computation.2 | async-start | bytes 524288 | tf_op jit(solution)/shard_map/psum | solution.py:9
  259.1 3.4 copy-start
  300.4 198.6 %all-reduce.10.cloned.1.call-start = ((), (), s32[]{:S(2)}) async-start(), calls=%async_computation.3 | async-start | bytes 8388608 | tf_op jit(solution)/shard_map/psum | solution.py:9
  366.8 3.7 copy-start.1
  376.8 5.6 copy-start.2
  387.1 157.1 %all-reduce.12.cloned.1.call-start = ((), (), s32[]{:S(2)}) async-start(), calls=%async_computation.4 | async-start | bytes 1048576 | tf_op jit(solution)/shard_map/psum | solution.py:9
Sparse Core Ops, SparseCore 0:
  9.7 116.0 all-gather.1
  130.4 92.4 all-reduce.5
  300.5 41.6 all-reduce.7
  387.2 111.7 all-reduce.9
  501.2 42.8 all-reduce.11
where the time goes:
time: 593 us; the launch traced here: 586 us
  waiting for transfers between devices  350 us (59%)
  other arithmetic  92.1 us (16%)
  local copies, waits for them, and re-layouts  59.6 us (10%)
  matrix products  45.1 us (8%)
  blocking collectives  23.8 us (4%)
  between operations  14.9 us (3%)
    psum x4, waiting for transfers between devices, spread(): return lax.psum(kept, axis)  231 us
    all_gather x1, waiting for transfers between devices, local(): lax.all_gather(samples, 'col', axis=2, tiled=True)  118 us
    another operation x6, other arithmetic, local(): own_corner = jnp.linalg.cholesky(kernel[0, :, 0, :])  34.2 us
    all_gather x1, blocking collectives, local(): lax.all_gather(nugget, 'col', axis=2, tiled=True)  23.8 us
    dot_general x1, matrix products, kernel_block(): lax.dot_general(row_side, col_scaled, (((1,), (1,)), ((), ())), preferred...  22.8 us
    another operation x3, other arithmetic, solve_panel(): solved = jax.scipy.linalg.solve_triangular(corner, stacked.T, lower=True).T  20.6 us
    reshape x1, local copies, waits for them, and re-layouts, local(): return result.reshape(row_tiles, 1, tile_width, col_tiles, 1, tile_width)  20.5 us
    dot_general x1, matrix products, local(): lax.dot_general(panel_rows.reshape(-1, tile_width), panel_cols.reshape(-1...  14.3 us
  transfers between devices with their start and end apart: 5, of which 5 were waited for; matrix products, arithmetic and copies ran while one was open for 6% of the time, Pallas kernels for 0%

commit v1 on v0

v1 whole, which is shorter than its diff:
```python
import functools

import jax
import jax.numpy as jnp
from jax import lax
from jax.experimental import pallas as pl
from jax.experimental.pallas import tpu as pltpu
from jax.sharding import PartitionSpec as P

NB = 256
HIGH = lax.Precision.HIGHEST
NT = (((1,), (1,)), ((), ()))
NN = (((1,), (0,)), ((), ()))


def dot_high(left, right, dims=NN):
    return lax.dot_general(left, right, dims, precision=HIGH, preferred_element_type=jnp.float32)


def eliminate(block):
    size = block.shape[0]
    height = 32
    rows = lax.broadcasted_iota(jnp.int32, (size, size), 0)
    cols = lax.broadcasted_iota(jnp.int32, (size, size), 1)
    eye = (rows == cols).astype(jnp.float32)
    whole = jnp.concatenate([block, eye], axis=1)
    parts = [whole[g * height : (g + 1) * height] for g in range(size // height)]
    inner = lax.broadcasted_iota(jnp.int32, (height, 1), 0)
    for j in range(size):
        first, at = divmod(j, height)
        pivot_row = parts[first][at : at + 1, :]
        pivot_row = pivot_row * (1.0 / pivot_row[:, j : j + 1])
        for g in range(first, size // height):
            factor = parts[g][:, j : j + 1]
            if g == first:
                factor = jnp.where(inner > at, factor, 0.0)
            parts[g] = parts[g] - factor * pivot_row
    whole = jnp.concatenate(parts, axis=0)
    pivots = jnp.sum(whole[:, :size] * eye, axis=1, keepdims=True)
    root = lax.rsqrt(pivots)
    root = root * (1.5 - 0.5 * pivots * root * root)
    return whole[:, size:] * root


def corner_kernel(a_ref, l_ref, x_ref):
    half = NB // 2
    rows = lax.broadcasted_iota(jnp.int32, (half, half), 0)
    cols = lax.broadcasted_iota(jnp.int32, (half, half), 1)
    lower = rows >= cols
    zero = jnp.zeros((half, half), jnp.float32)
    a11, a21, a22 = a_ref[:half, :half], a_ref[half:, :half], a_ref[half:, half:]
    x11 = eliminate(a11)
    l21 = dot_high(a21, x11, NT)
    l_ref[:half, :half] = jnp.where(lower, dot_high(a11, x11, NT), 0.0)
    l_ref[:half, half:] = zero
    l_ref[half:, :half] = l21
    s22 = a22 - dot_high(l21, l21, NT)
    x22 = eliminate(s22)
    l_ref[half:, half:] = jnp.where(lower, dot_high(s22, x22, NT), 0.0)
    x_ref[:half, :half] = x11
    x_ref[:half, half:] = zero
    x_ref[half:, :half] = -dot_high(x22, dot_high(l21, x11))
    x_ref[half:, half:] = x22


def factor_corner(corner_kernel_tile):
    shape = jax.ShapeDtypeStruct((NB, NB), jnp.float32)
    return pl.pallas_call(corner_kernel, out_shape=(shape, shape))(corner_kernel_tile)


def halves(value):
    high = value.astype(jnp.bfloat16)
    low = (value - high.astype(jnp.float32)).astype(jnp.bfloat16)
    return high, low


def main_kernel(tiles, rows_dev, where_ref, rows_ref, norm_ref, w_ref, wn_ref, nug_ref, inv_ref, q_ref, l_ref, o_ref):
    step = pl.program_id(0)
    row, col = where_ref[0], where_ref[1]
    eye = lax.broadcasted_iota(jnp.int32, (NB, NB), 0) == lax.broadcasted_iota(jnp.int32, (NB, NB), 1)
    for n in range(tiles):
        tile = (step * tiles + n) * rows_dev + row
        cross = lax.dot_general(
            rows_ref[n * NB : (n + 1) * NB, :], w_ref[...], NT, preferred_element_type=jnp.float32
        )
        norms = norm_ref[n * NB : (n + 1) * NB, :]
        kern = jnp.exp(-0.5 * (norms + wn_ref[...] - 2.0 * cross))
        left = kern[:, :NB] + jnp.where(eye & (tile == 0), nug_ref[:, :NB], 0.0)
        high, low = halves(left)
        panel = lax.dot_general(
            jnp.concatenate([high, high, low], axis=1), inv_ref[...], NN, preferred_element_type=jnp.float32
        )
        high, low = halves(panel)
        update = lax.dot_general(
            jnp.concatenate([high, high, low], axis=1), q_ref[...], NN, preferred_element_type=jnp.float32
        )
        first_tile = tile == 0
        for u in range(2):
            part = slice(NB * (u + 1), NB * (u + 2))
            own = kern[:, part] + jnp.where(eye & (tile == col + 32 * u), nug_ref[:, part], 0.0)
            result = jnp.where(first_tile, own, own - update[:, NB * u : NB * (u + 1)])
            if u == 0:
                result = jnp.where(col == 0, jnp.where(first_tile, l_ref[...], panel), result)
            for half in range(2):
                o_ref[pl.ds(n * NB * 4 + 2 * u + half, NB, stride=4), :] = result[:, 128 * half : 128 * (half + 1)]


def stacked(value):
    high = lax.reduce_precision(value, 8, 7)
    low = (value - high).astype(jnp.bfloat16)
    high = high.astype(jnp.bfloat16)
    return jnp.concatenate([high, low, high], axis=0)


def local(samples, ard_weight, nugget):
    row_count = lax.axis_size("row")
    col_count = lax.axis_size("col")
    row_index = lax.axis_index("row")
    col_index = lax.axis_index("col")
    row_tiles, _, _, sub, features = samples.shape
    quarter = features // row_count
    gathered = lax.all_gather(samples, "col", axis=2, tiled=True)

    own = samples.reshape(row_tiles, sub, features)
    widened = own.astype(jnp.float32)
    own_norms = jnp.sum(widened * widened * ard_weight, axis=2)
    n_high = lax.reduce_precision(own_norms, 8, 7)
    n_mid = lax.reduce_precision(own_norms - n_high, 8, 7)
    n_low = own_norms - n_high - n_mid
    pieces = jnp.stack([n_high, n_mid, n_low]).astype(jnp.bfloat16).transpose(0, 2, 1)

    cut = own.reshape(row_tiles, sub, row_count, quarter).transpose(2, 0, 1, 3)
    extra = jnp.broadcast_to(nugget.reshape(1, row_tiles, sub, 1), (row_count, row_tiles, sub, 128))
    sent = lax.all_to_all(jnp.concatenate([cut, extra], axis=3), "row", 0, 0)
    wide = quarter + 128
    fold = row_tiles // 2
    sent = sent.reshape(row_count, 2, fold, sub, wide)
    first = jnp.broadcast_to(sent[0, 0, 0][None, None], (col_count, 1, sub, wide))
    sent = sent.transpose(2, 0, 1, 3, 4).reshape(col_count, 2, sub, wide)
    sent = jnp.concatenate([first, sent], axis=1)
    tags = jnp.concatenate(
        [sent[..., quarter : quarter + 64],
         jnp.broadcast_to(pieces[None], (col_count, 3, sub, row_tiles)),
         sent[..., quarter + 80 :]], axis=3)
    sent = jnp.concatenate([sent[..., :quarter], tags], axis=3)
    got = lax.all_to_all(sent, "col", 0, 0)
    part = got[..., :quarter].transpose(1, 0, 2, 3).reshape(3 * NB, quarter)
    nug = got[..., quarter].astype(jnp.float32).transpose(1, 0, 2).reshape(1, 3 * NB)
    norm_bits = got[..., quarter + 64 : quarter + 80].astype(jnp.float32)
    row_norms = (norm_bits[:, 0] + norm_bits[:, 1]) + norm_bits[:, 2]
    row_norms = row_norms.transpose(2, 0, 1).reshape(row_tiles * NB, 1)

    up = [(i, (i + 1) % row_count) for i in range(row_count)]
    down = [(i, (i - 1) % row_count) for i in range(row_count)]
    mid = part.shape[0] // 2
    below = lax.ppermute(part, "row", up)
    above = lax.ppermute(part, "row", down)
    across = jnp.concatenate(
        [lax.ppermute(below[:mid], "row", up), lax.ppermute(above[mid:], "row", down)], axis=0
    )
    w_raw = jnp.zeros((3 * NB, features), jnp.bfloat16)
    for shift, value in enumerate((part, below, across, above)):
        at = lax.rem(row_index - shift + row_count, row_count) * quarter
        w_raw = lax.dynamic_update_slice(w_raw, value, (0, at))

    w_wide = w_raw.astype(jnp.float32)
    w_scaled = (w_wide * ard_weight).astype(jnp.bfloat16)
    w_norms = jnp.sum(w_wide * w_wide * ard_weight, axis=1)
    cross0 = lax.dot_general(w_raw, w_scaled[:NB], NT, preferred_element_type=jnp.float32)
    kern0 = jnp.exp(-0.5 * (w_norms[:, None] + w_norms[None, :NB] - 2.0 * cross0))
    tile0 = kern0[:NB] + jnp.diag(nug[0, :NB])
    corner, inverse = factor_corner(0.5 * (tile0 + tile0.T))
    q_panel = dot_high(inverse, kern0[NB:], NT)

    rows_data = gathered.reshape(row_tiles * NB, features)
    tiles = 2
    steps = row_tiles // tiles
    position = jnp.stack([row_index, col_index]).astype(jnp.int32)
    vmem = pl.BlockSpec(memory_space=pltpu.VMEM)
    flops = 2 * row_tiles * NB * 3 * NB * features
    result = pl.pallas_call(
        functools.partial(main_kernel, tiles, 4),
        out_shape=jax.ShapeDtypeStruct((row_tiles * NB * 4, 128), jnp.float32),
        grid_spec=pltpu.PrefetchScalarGridSpec(
            num_scalar_prefetch=1,
            grid=(steps,),
            in_specs=[
                pl.BlockSpec((tiles * NB, features), lambda i, _: (i, 0)),
                pl.BlockSpec((tiles * NB, 1), lambda i, _: (i, 0)),
                vmem, vmem, vmem, vmem, vmem, vmem,
            ],
            out_specs=pl.BlockSpec((tiles * NB * 4, 128), lambda i, _: (i, 0)),
        ),
        compiler_params=pltpu.CompilerParams(vmem_limit_bytes=48 * 2**20),
        cost_estimate=pl.CostEstimate(flops=flops, bytes_accessed=48 * 2**20, transcendentals=0),
    )(position, rows_data, row_norms, w_scaled, w_norms.reshape(1, -1), nug, stacked(inverse.T), stacked(q_panel), corner)
    return result.reshape(row_tiles, 1, NB, 2, 1, NB)


def solution(mesh):
    placed = (P(None, "row", "col", None, None), P(), P(None, "row", "col", None))
    return jax.shard_map(
        local,
        mesh=mesh,
        in_specs=placed,
        out_specs=P(None, "row", None, None, "col", None),
        check_vma=False,
    )
```

time: 593 us -> 228 us (0.38)
  waiting for transfers between devices: 350 us -> 61.4 us
  other arithmetic: 92.1 us -> 8.32 us
  Pallas kernels: 0 us -> 64.4 us
  matrix products: 45.1 us -> 3.43 us
  local copies, waits for them, and re-layouts: 59.6 us -> 19 us
  blocking collectives: 23.8 us -> 43.4 us
  starting transfers between devices: 0.17 us -> 11.9 us
    psum x4 -> x0, waiting for transfers between devices: 231 us -> none  [spread(): return lax.psum(kept, axis)]
    all_gather x1, waiting for transfers between devices: 118 us -> 0.02 us  [local(): gathered = lax.all_gather(samples, 'col', axis=2, tiled=True)]
    pallas_call x0 -> x2, Pallas kernels: none -> 64.4 us  [the longest x1 39.8 us: local(): pl.pallas_call(functools.partial(main_kernel, tiles, 4), out_shape=jax.Sh...]
    another operation x9 -> x2, other arithmetic: 54.8 us -> 0.09 us  [the longest x1 0.07 us: local(): position = jnp.stack([row_index, col_index]).astype(jnp.int32)]
    ppermute x0 -> x4, waiting for transfers between devices: none -> 44.6 us  [the longest x1 33.5 us: local(): below = lax.ppermute(part, 'row', up)]
    all_to_all x0 -> x1, blocking collectives: none -> 43.4 us  [local(): got = lax.all_to_all(sent, 'col', 0, 0)]
    dot_general x2, matrix products: 37.1 us -> 3.43 us  [the longest x1 1.86 us: local(): lax.dot_general(w_raw, w_scaled[:NB], NT, preferred_element_type=jnp.floa...]
    reshape x2 -> x4, local copies, waits for them, and re-layouts: 26.1 us -> 0.77 us  [the longest x1 0.59 us: local(): row_norms = row_norms.transpose(2, 0, 1).reshape(row_tiles * NB, 1)]
  transfers between devices with their start and end apart: 5 -> 6, of which waited for: 5 -> 4; matrix products, arithmetic and copies ran while one was open for 6% -> 13% of each run, Pallas kernels for 0% -> 11%
where the time goes in v1:
time: 228 us; the launch traced here: 226 us
  Pallas kernels  64.4 us (28%)
  waiting for transfers between devices  61.4 us (27%)
  blocking collectives  43.4 us (19%)
  local copies, waits for them, and re-layouts  19 us (8%)
  between operations  13.7 us (6%)
  starting transfers between devices  11.9 us (5%)
  other arithmetic  8.32 us (4%)
  matrix products  3.43 us (2%)
    all_to_all x1, blocking collectives, local(): got = lax.all_to_all(sent, 'col', 0, 0)  43.4 us
    pallas_call x1, Pallas kernels, local(): pl.pallas_call(functools.partial(main_kernel, tiles, 4), out_shape=jax.Sh...  39.8 us
    ppermute x1, waiting for transfers between devices, local(): below = lax.ppermute(part, 'row', up)  33.5 us
    pallas_call x1, Pallas kernels, factor_corner(): pl.pallas_call(corner_kernel, out_shape=(shape, shape))(corner_kernel_tile)  24.6 us
    all_to_all x1, waiting for transfers between devices, local(): sent = lax.all_to_all(jnp.concatenate([cut, extra], axis=3), 'row', 0, 0)  16 us
    ppermute x1, waiting for transfers between devices, local(): lax.ppermute(below[:mid], 'row', up)  9.77 us
    all_to_all x1, starting transfers between devices, local(): sent = lax.all_to_all(jnp.concatenate([cut, extra], axis=3), 'row', 0, 0)  5.39 us
  transfers between devices with their start and end apart: 6, of which 4 were waited for; matrix products, arithmetic and copies ran while one was open for 13% of the time, Pallas kernels for 11%

profile of v1, /device:TPU:0, one launch (start us, length us, event | category | flops | bytes accessed | tf_op | source)
XLA Modules:
  0.0 225.6 jit_solution(14681762381219159911)
XLA Ops:
  6.5 0.0 all-gather.2.cloned.1.call-start
  6.5 0.7 all-gather.2.cloned.1.call-update
  7.3 1.9 reshape_reshape.3
  9.1 0.0 copy-done.7
  9.1 0.1 copy.34
  9.2 0.2 broadcast_in_dim.49
  9.4 0.6 pad_maximum_fusion
  10.0 0.0 copy-start.1
  10.0 0.0 copy-start.5
  10.0 1.1 copy.35
  11.2 5.4 %all-to-all-start = ((bf16[4,16,8,1152]{3,2,1,0:T(8,128)(2,1)}), bf16[4,16,8,1152]{3,2,1,0:T(8,128)(2,1)S(1)}, u32[]{:S(2)}, u32[]{:S(2)}) async-start(bf16[4,16,8,1152]{3,2,1,0:T(8,128)(2,1)} %copy.35), calls=%async_computation | async-start | bytes 2359296 | tf_op jit(solution)/shard_map/all_to_all | solution.py:134
  16.5 0.0 copy-done.1
  16.5 0.0 copy-done.5
  16.6 0.4 fusion.5
  16.9 0.1 copy.37
  17.0 16.0 %all-to-all-done = bf16[4,16,8,1152]{3,2,1,0:T(8,128)(2,1)S(1)} async-done(((bf16[4,16,8,1152]{3,2,1,0:T(8,128)(2,1)}), bf16[4,16,8,1152]{3,2,1,0:T(8,128)(2,1)S(1)}, u32[]{:S(2)}, u32[]{:S(2)}) %all-to-all-start) | async-done | bytes 1179680 | tf_op jit(solution)/shard_map/all_to_all | solution.py:134
  33.0 0.1 copy.36
  33.2 0.8 pad_maximum_fusion.3
  34.0 0.2 slice_maximum_fusion
  34.2 0.7 broadcast_in_dim.52
  34.9 2.2 concatenate.21
  37.1 43.4 %all_to_all.10 = bf16[32,3,8,1152]{3,2,1,0:T(8,128)(2,1)S(1)} all-to-all(bf16[32,3,8,1152]{3,2,1,0:T(8,128)(2,1)S(1)} %concatenate.21), channel_id=1, replica_groups=mesh['row'=4,'col'=32] {'col'}, dimensions={0} | all-to-all | bytes 3538944 | tf_op jit(solution)/shard_map/all_to_all | solution.py:146
  80.5 0.2 slice_bitcast_fusion
  80.7 0.1 copy.39
  80.8 0.0 copy-start.3
  80.8 0.1 collective-permute-start
  80.9 3.2 %collective-permute-start.2 = (bf16[768,1024]{1,0:T(8,128)(2,1)S(1)}, bf16[768,1024]{1,0:T(8,128)(2,1)}, u32[]{:S(2)}, u32[]{:S(2)}) collective-permute-start(bf16[768,1024]{1,0:T(8,128)(2,1)S(1)} %bitcast.52), channel_id=1, source_target_pairs={{0,96},{32,0},{64,32},{96,64},{1,97},{33,1},{65,33},{97,65},{2,98}... | collective-permute-start | bytes 4718600 | tf_op jit(solution)/shard_map/ppermute | solution.py:157
  84.2 0.1 pad_add_fusion.where_ref
  84.3 0.2 copy.48
  84.5 33.5 %collective-permute-done = bf16[768,1024]{1,0:T(8,128)(2,1)} collective-permute-done((bf16[768,1024]{1,0:T(8,128)(2,1)S(1)}, bf16[768,1024]{1,0:T(8,128)(2,1)}, u32[]{:S(2)}, u32[]{:S(2)}) %collective-permute-start) | collective-permute-done | bytes 1572896 | tf_op jit(solution)/shard_map/ppermute | solution.py:156
  118.0 2.1 slice.74
  120.2 0.0 collective-permute-start.1
  120.2 0.0 collective-permute-done.2
  120.2 2.1 slice.75
  122.2 3.2 %collective-permute-start.3 = (bf16[384,1024]{1,0:T(8,128)(2,1)}, bf16[384,1024]{1,0:T(8,128)(2,1)}, u32[]{:S(2)}, u32[]{:S(2)}) collective-permute-start(bf16[384,1024]{1,0:T(8,128)(2,1)} %slice.75), channel_id=1, source_target_pairs={{0,96},{32,0},{64,32},{96,64},{1,97},{33,1},{65,33},{97,65},{2,98}... | collective-permute-start | bytes 2359304 | tf_op jit(solution)/shard_map/ppermute | solution.py:159
  125.5 0.0 copy-done.3
  125.5 0.1 copy.41
  125.5 0.1 reshape.79.nug_ref
  125.6 0.1 slice_convert_fusion
  125.8 0.3 copy.38
  126.1 0.6 reshape.83.norm_ref
  126.7 0.0 copy-start.4
  126.7 0.8 broadcast_in_dim.53
  127.5 0.6 copy-done.4
  128.1 0.2 constant_dynamic-update-slice_fusion.2
  128.3 1.6 constant_dynamic-update-slice_fusion.1
  129.9 9.8 %collective-permute-done.1 = bf16[384,1024]{1,0:T(8,128)(2,1)} collective-permute-done((bf16[384,1024]{1,0:T(8,128)(2,1)}, bf16[384,1024]{1,0:T(8,128)(2,1)}, u32[]{:S(2)}, u32[]{:S(2)}) %collective-permute-start.1) | collective-permute-done | bytes 786464 | tf_op jit(solution)/shard_map/ppermute | solution.py:159
  139.7 1.3 collective-permute-done.3
  141.0 1.6 maximum_dynamic-update-slice_fusion
  142.6 0.0 copy-start.6
  142.6 1.6 constant_dynamic-update-slice_fusion
  144.2 0.0 copy-done.6
  144.2 3.7 %fusion.2 = (f32[768]{0:T(1024)S(1)}, bf16[768,4096]{1,0:T(8,128)(2,1)S(1)}) fusion(bf16[768,4096]{1,0:T(8,128)(2,1)S(1)} %constant_dynamic-update-slice_fusion, f32[4096]{0:T(1024)S(1)} %copy-done.6), kind=kLoop, calls=%fused_computation.4 | loop fusion | flops 18873600 | bytes 12602368 | tf_op jit(solution)/shard_map/reduce_sum | solution.py:168
  148.0 0.0 copy-start.2
  148.0 1.9 multiply_exponential_fusion
  149.9 0.7 copy-done.2
  150.6 0.1 copy.43
  150.7 0.8 fusion.15.a_ref
  151.5 24.6 %shard_map.37 = (f32[256,256]{1,0:T(8,128)}, f32[256,256]{1,0:T(8,128)}) custom-call(f32[256,256]{1,0:T(8,128)} %fusion.15.a_ref), custom_call_target="tpu_custom_call" | custom-call | tf_op jit(solution)/shard_map/pallas_call | solution.py:68
  176.1 1.1 copy.44
  177.3 1.6 fusion.9
  178.9 0.1 pad_maximum_fusion.1.q_ref
  178.9 0.0 all-gather.2.cloned.1.call-done
  179.0 39.8 %shard_map.38 = f32[16384,128]{1,0:T(8,128)} custom-call(s32[2]{0:T(128)S(1)} %pad_add_fusion.where_ref, bf16[4096,4096]{1,0:T(8,128)(2,1)} %bitcast.60, f32[4096,1]{1,0:T(8,128)S(1)} %reshape.83.norm_ref, bf16[768,4096]{1,0:T(8,128)(2,1)} %copy-done.2, f32[1,768]{1,0:T(1,128)S(1)} %reshape.74.wn_ref, f32[1,768]{1,0:T(1,128)S(1)} %reshape.79.nug_ref, ...), custom_call_target="tpu_custom_call" | custom-call | flops 25769803776 | bytes 50331648 | tf_op jit(solution)/shard_map/pallas_call | solution.py:181
  (16 shorter events, 0.2 us)
Async XLA Ops:
  6.5 2.6 %copy-start.7 = (bf16[16,1,1,8]{0,3,2,1:T(8,128)(2,1)S(1)}, bf16[16,1,1,8]{0,3,2,1:T(8,128)(2,1)}, u32[]{:S(2)}) copy-start(bf16[16,1,1,8]{0,3,2,1:T(8,128)(2,1)} %param.5) | copy-start | bytes 772
  6.5 172.4 %all-gather.2.cloned.1.call-start = ((), (), s32[]{:S(2)}) async-start(), calls=%async_computation.2 | async-start | bytes 34603008 | tf_op jit(solution)/shard_map/all_gather | solution.py:122
  10.0 6.6 %copy-start.1 = (bf16[16,1,1,8,4096]{4,3,2,1,0:T(8,128)(2,1)S(1)}, bf16[16,1,1,8,4096]{4,3,2,1,0:T(8,128)(2,1)}, u32[]{:S(2)}) copy-start(bf16[16,1,1,8,4096]{4,3,2,1,0:T(8,128)(2,1)} %param.3) | copy-start | bytes 3145732
  10.0 6.5 %copy-start.5 = (f32[4096]{0:T(1024)S(1)}, f32[4096]{0:T(1024)}, u32[]{:S(2)}) copy-start(f32[4096]{0:T(1024)} %param.4) | copy-start | bytes 49156
  11.2 21.9 %all-to-all-start = ((bf16[4,16,8,1152]{3,2,1,0:T(8,128)(2,1)}), bf16[4,16,8,1152]{3,2,1,0:T(8,128)(2,1)S(1)}, u32[]{:S(2)}, u32[]{:S(2)}) async-start(bf16[4,16,8,1152]{3,2,1,0:T(8,128)(2,1)} %copy.35), calls=%async_computation | async-start | bytes 2359296 | tf_op jit(solution)/shard_map/all_to_all | solution.py:134
  80.8 44.6 %copy-start.3 = (bf16[3,32,8,1024]{3,2,1,0:T(8,128)(2,1)}, bf16[3,32,8,1024]{3,2,1,0:T(8,128)(2,1)S(1)}, u32[]{:S(2)}) copy-start(bf16[3,32,8,1024]{3,2,1,0:T(8,128)(2,1)S(1)} %copy.39) | copy-start | bytes 4718596
  80.8 37.2 %collective-permute-start = (bf16[768,1024]{1,0:T(8,128)(2,1)S(1)}, bf16[768,1024]{1,0:T(8,128)(2,1)}, u32[]{:S(2)}, u32[]{:S(2)}) collective-permute-start(bf16[768,1024]{1,0:T(8,128)(2,1)S(1)} %bitcast.51), channel_id=1, source_target_pairs={{0,32},{32,64},{64,96},{96,0},{1,33},{33,65},{65,97},{97,1},{2,34}... | collective-permute-start | bytes 4718600 | tf_op jit(solution)/shard_map/ppermute | solution.py:156
  80.9 39.2 %collective-permute-start.2 = (bf16[768,1024]{1,0:T(8,128)(2,1)S(1)}, bf16[768,1024]{1,0:T(8,128)(2,1)}, u32[]{:S(2)}, u32[]{:S(2)}) collective-permute-start(bf16[768,1024]{1,0:T(8,128)(2,1)S(1)} %bitcast.52), channel_id=1, source_target_pairs={{0,96},{32,0},{64,32},{96,64},{1,97},{33,1},{65,33},{97,65},{2,98}... | collective-permute-start | bytes 4718600 | tf_op jit(solution)/shard_map/ppermute | solution.py:157
  120.2 19.5 %collective-permute-start.1 = (bf16[384,1024]{1,0:T(8,128)(2,1)}, bf16[384,1024]{1,0:T(8,128)(2,1)}, u32[]{:S(2)}, u32[]{:S(2)}) collective-permute-start(bf16[384,1024]{1,0:T(8,128)(2,1)} %slice.74), channel_id=1, source_target_pairs={{0,32},{32,64},{64,96},{96,0},{1,33},{33,65},{65,97},{97,1},{2,34}... | collective-permute-start | bytes 2359304 | tf_op jit(solution)/shard_map/ppermute | solution.py:159
  122.2 18.8 %collective-permute-start.3 = (bf16[384,1024]{1,0:T(8,128)(2,1)}, bf16[384,1024]{1,0:T(8,128)(2,1)}, u32[]{:S(2)}, u32[]{:S(2)}) collective-permute-start(bf16[384,1024]{1,0:T(8,128)(2,1)} %slice.75), channel_id=1, source_target_pairs={{0,96},{32,0},{64,32},{96,64},{1,97},{33,1},{65,33},{97,65},{2,98}... | collective-permute-start | bytes 2359304 | tf_op jit(solution)/shard_map/ppermute | solution.py:159
  126.7 1.4 copy-start.4
  142.6 1.6 copy-start.6
  148.0 2.6 %copy-start.2 = (bf16[768,4096]{1,0:T(8,128)(2,1)}, bf16[768,4096]{1,0:T(8,128)(2,1)S(1)}, u32[]{:S(2)}) copy-start(bf16[768,4096]{1,0:T(8,128)(2,1)S(1)} %get-tuple-element.10.w_ref) | copy-start | bytes 18874372
  176.1 2.9 %copy-start = (f32[256,256]{1,0:T(8,128)S(1)}, f32[256,256]{1,0:T(8,128)}, u32[]{:S(2)}) copy-start(f32[256,256]{1,0:T(8,128)} %get-tuple-element.8.l_ref) | copy-start | bytes 786436
Sparse Core Ops, SparseCore 0:
  9.7 127.9 all-gather.1

commit v2 on v1

v2 whole, which is shorter than its diff:
```python
import functools

import jax
import jax.numpy as jnp
from jax import lax
from jax.experimental import pallas as pl
from jax.experimental.pallas import tpu as pltpu
from jax.sharding import PartitionSpec as P

NB = 256
HIGH = lax.Precision.HIGHEST
NT = (((1,), (1,)), ((), ()))
NN = (((1,), (0,)), ((), ()))
RING = (0, 3, 1, 2)


def dot_high(left, right, dims=NN):
    return lax.dot_general(left, right, dims, precision=HIGH, preferred_element_type=jnp.float32)


def eliminate(block):
    size = block.shape[0]
    height = 32
    rows = lax.broadcasted_iota(jnp.int32, (size, size), 0)
    cols = lax.broadcasted_iota(jnp.int32, (size, size), 1)
    eye = (rows == cols).astype(jnp.float32)
    whole = jnp.concatenate([block, eye], axis=1)
    parts = [whole[g * height : (g + 1) * height] for g in range(size // height)]
    inner = lax.broadcasted_iota(jnp.int32, (height, 1), 0)
    for j in range(0, size, 2):
        first, at = divmod(j, height)
        row0 = parts[first][at : at + 1, :]
        row1 = parts[first][at + 1 : at + 2, :]
        a, b = row0[:, j : j + 1], row0[:, j + 1 : j + 2]
        c, d = row1[:, j : j + 1], row1[:, j + 1 : j + 2]
        inv_a = 1.0 / a
        scale = c * inv_a
        inv_d = 1.0 / (d - scale * b)
        row1 = row1 - scale * row0
        for g in range(first, size // height):
            f0 = parts[g][:, j : j + 1] * inv_a
            f1 = (parts[g][:, j + 1 : j + 2] - f0 * b) * inv_d
            if g == first:
                f0 = jnp.where(inner > at, f0, 0.0)
                f1 = jnp.where(inner > at + 1, f1, 0.0)
            parts[g] = parts[g] - f0 * row0 - f1 * row1
    whole = jnp.concatenate(parts, axis=0)
    pivots = jnp.sum(whole[:, :size] * eye, axis=1, keepdims=True)
    root = lax.rsqrt(pivots)
    root = root * (1.5 - 0.5 * pivots * root * root)
    return whole[:, size:] * root


def corner_kernel(a_ref, l_ref, x_ref):
    half = NB // 2
    rows = lax.broadcasted_iota(jnp.int32, (half, half), 0)
    cols = lax.broadcasted_iota(jnp.int32, (half, half), 1)
    lower = rows >= cols
    zero = jnp.zeros((half, half), jnp.float32)
    a11, a21, a22 = a_ref[:half, :half], a_ref[half:, :half], a_ref[half:, half:]
    x11 = eliminate(a11)
    l21 = dot_high(a21, x11, NT)
    l_ref[:half, :half] = jnp.where(lower, dot_high(a11, x11, NT), 0.0)
    l_ref[:half, half:] = zero
    l_ref[half:, :half] = l21
    s22 = a22 - dot_high(l21, l21, NT)
    x22 = eliminate(s22)
    l_ref[half:, half:] = jnp.where(lower, dot_high(s22, x22, NT), 0.0)
    x_ref[:half, :half] = x11
    x_ref[:half, half:] = zero
    x_ref[half:, :half] = -dot_high(x22, dot_high(l21, x11))
    x_ref[half:, half:] = x22


def factor_corner(tile):
    shape = jax.ShapeDtypeStruct((NB, NB), jnp.float32)
    return pl.pallas_call(
        corner_kernel,
        out_shape=(shape, shape),
        cost_estimate=pl.CostEstimate(flops=10**10, bytes_accessed=2**20, transcendentals=0),
    )(tile)


def halves(value):
    high = value.astype(jnp.bfloat16)
    low = (value - high.astype(jnp.float32)).astype(jnp.bfloat16)
    return high, low


def main_kernel(cuts, a_count, where_ref, norm_ref, grow_ref, *refs):
    count = len(cuts)
    pieces = refs[:count]
    w0_ref, wc_ref, wn_ref, nug_ref, gcol_ref, inv_ref, q_ref, l_ref = refs[count : count + 8]
    own_ref, sib_ref, rows_buf, w_buf, row_sem, w_sem = refs[count + 8 :]
    step = pl.program_id(0)
    row, col = where_ref[0], where_ref[1]

    def w_copy(n):
        if n == 0:
            return pltpu.make_async_copy(w0_ref, w_buf.at[0], w_sem.at[0])
        return pltpu.make_async_copy(wc_ref.at[n - 1], w_buf.at[n], w_sem.at[n])

    def row_copy(n):
        index, start, size = cuts[n]
        return pltpu.make_async_copy(pieces[n], rows_buf.at[index, pl.ds(start, size)], row_sem.at[n])

    @pl.when(step == 0)
    def _():
        for n in range(count):
            if cuts[n][0] == 0:
                row_copy(n).start()
        for n in range(5):
            w_copy(n).start()
        for n in range(count):
            if cuts[n][0] != 0:
                row_copy(n).start()

    for n in range(count):
        @pl.when(step == cuts[n][0])
        def _(n=n):
            row_copy(n).wait()

    def wait_w(n):
        @pl.when(step == 0)
        def _():
            w_copy(n).wait()

    norms = norm_ref[...]
    grow = grow_ref[...]

    def kern(n):
        part = slice(NB * n, NB * (n + 1))
        wait_w(n)
        cross = lax.dot_general(rows_buf[step], w_buf[n], NT, preferred_element_type=jnp.float32)
        value = jnp.exp(-0.5 * (norms + wn_ref[:, part] - 2.0 * cross))
        return value + jnp.where(grow == gcol_ref[:, part], nug_ref[:, part], 0.0)

    high, low = halves(kern(0))
    panel = lax.dot_general(
        jnp.concatenate([high, high, low], axis=1), inv_ref[...], NN, preferred_element_type=jnp.float32
    )
    high, low = halves(panel)
    triple = jnp.concatenate([high, high, low], axis=1)
    for n in range(1, 5):
        out_ref = own_ref if n < 3 else sib_ref
        owner = col if n < 3 else col + 1 - 2 * lax.rem(col, 2)
        u = (n - 1) % 2
        own = kern(n)
        update = lax.dot_general(
            triple, q_ref[:, NB * (n - 1) : NB * n], NN, preferred_element_type=jnp.float32
        )
        result = jnp.where(grow < NB, own, own - update)
        if u == 0:
            result = jnp.where(owner == 0, panel, result)
        for half in range(2):
            out_ref[0, pl.ds(2 * u + half, NB, stride=4), :] = result[:, 128 * half : 128 * (half + 1)]
        if u == 0:
            @pl.when((owner == 0) & (row == 0) & (step < a_count))
            def _(out_ref=out_ref):
                for d in range(4):
                    chip = where_ref[2 + 4 * step + d]
                    start = pl.multiple_of(chip * 16 + lax.rem(col, 2) * 8, 8)
                    tile = l_ref[pl.ds(start, 8), :]
                    for half in range(2):
                        out_ref[0, pl.ds(d * 64 * 4 + half, 8, stride=4), :] = tile[:, 128 * half : 128 * (half + 1)]


def run_main(pieces, cuts, a_count, where, norms, grow, rest):
    steps = max(cut[0] for cut in cuts) + 1
    shape = jax.ShapeDtypeStruct((steps, NB * 4, 128), jnp.float32)
    vmem = pl.BlockSpec(memory_space=pltpu.VMEM)
    hbm = pl.BlockSpec(memory_space=pl.ANY)
    features = pieces[0].shape[-1]
    column = pl.BlockSpec((NB, 1), lambda i, _: (i, 0))
    out = pl.BlockSpec((1, NB * 4, 128), lambda i, _: (i, 0, 0))
    return pl.pallas_call(
        functools.partial(main_kernel, cuts, a_count),
        out_shape=(shape, shape),
        grid_spec=pltpu.PrefetchScalarGridSpec(
            num_scalar_prefetch=1,
            grid=(steps,),
            in_specs=[column, column] + [hbm] * (len(pieces) + 2) + [vmem] * 6,
            out_specs=(out, out),
            scratch_shapes=[
                pltpu.VMEM((steps, NB, features), jnp.bfloat16),
                pltpu.VMEM((5, NB, features), jnp.bfloat16),
                pltpu.SemaphoreType.DMA((len(pieces),)),
                pltpu.SemaphoreType.DMA((5,)),
            ],
        ),
        compiler_params=pltpu.CompilerParams(vmem_limit_bytes=50 * 2**20),
        cost_estimate=pl.CostEstimate(
            flops=2 * steps * NB * 5 * NB * features, bytes_accessed=steps * 4 * 2**20, transcendentals=0
        ),
    )(where, norms, grow, *pieces, *rest)


def place_kernel(plan, where_ref, *refs):
    count = len(plan)
    sources, out_ref, sem = refs[:count], refs[-2], refs[-1]
    core = lax.rem(where_ref[1], 2)
    copies = []
    for source, (mine, kinds) in zip(sources, plan):
        side = core if mine else 1 - core
        for i, (is_a, first) in enumerate(kinds):
            for d in range(4):
                chip = where_ref[2 + 4 * first + d]
                copies.append(pltpu.make_async_copy(
                    source.at[i, d], out_ref.at[pl.ds(0 if is_a else 8, 8), chip, side], sem.at[len(copies)]))
    for copy in copies:
        copy.start()
    for copy in copies:
        copy.wait()


def place(sources, plan, where, before, shape):
    hbm = pl.BlockSpec(memory_space=pl.ANY)
    total = sum(4 * len(kinds) for _, kinds in plan)
    args = [where] + list(sources) + ([] if before is None else [before])
    return pl.pallas_call(
        functools.partial(place_kernel, plan),
        out_shape=jax.ShapeDtypeStruct(shape, jnp.float32),
        in_specs=[pl.BlockSpec(memory_space=pltpu.SMEM)] + [hbm] * (len(args) - 1),
        out_specs=hbm,
        scratch_shapes=[pltpu.SemaphoreType.DMA((total,))],
        input_output_aliases={} if before is None else {len(args) - 1: 0},
        cost_estimate=pl.CostEstimate(flops=0, bytes_accessed=total * 2**18, transcendentals=0),
    )(*args)


def stacked(value):
    high = lax.reduce_precision(value, 8, 7)
    low = (value - high).astype(jnp.bfloat16)
    high = high.astype(jnp.bfloat16)
    return jnp.concatenate([high, low, high], axis=0)


def rolled(value, axis, shift):
    double = jnp.concatenate([value, value], axis=axis)
    turned = lax.dynamic_slice_in_dim(double, shift, 4, axis)
    return jnp.concatenate([lax.slice_in_dim(turned, d, d + 1, axis=axis) for d in RING], axis=axis)


def x_move(step):
    return [(y * 8 + x * 2 + k, y * 8 + (x + step) % 4 * 2 + k) for y in range(4) for x in range(4) for k in range(2)]


def y_move(step):
    return [(y * 8 + x * 2 + k, (y + step) % 4 * 8 + x * 2 + k) for y in range(4) for x in range(4) for k in range(2)]


def local(samples, ard_weight, nugget):
    row_count = lax.axis_size("row")
    col_count = lax.axis_size("col")
    row_index = lax.axis_index("row")
    col_index = lax.axis_index("col")
    core = col_index % 2
    chip_x, chip_y = col_index // 2 % 4, col_index // 8
    row_tiles, _, _, sub, features = samples.shape
    quarter = features // row_count
    eighth = quarter // 2
    fold = row_tiles // 2
    own = samples.reshape(row_tiles, sub, features)
    sibling = [(i, i ^ 1) for i in range(col_count)]

    def swap(value):
        return lax.ppermute(value, "col", sibling)

    def ring(value, moves, cut):
        up, down = moves(1), moves(-1)
        below = lax.ppermute(value, "col", up)
        above = lax.ppermute(value, "col", down)
        far0 = lax.ppermute(below[:cut], "col", up)
        far1 = lax.ppermute(above[cut:], "col", down)
        return below, above, far0, far1

    part_a, part_b = own[:fold], own[fold:]
    line_a = ring(part_a, x_move, fold // 2)
    line_b = ring(part_b, y_move, fold // 2)
    four_a = jnp.concatenate([part_a, *line_a], axis=0).reshape(4, fold * sub, features)
    four_b = jnp.concatenate([part_b, *line_b], axis=0).reshape(4, fold * sub, features)
    grid_a = ring(four_a, y_move, 2)
    grid_b = ring(four_b, x_move, 2)

    widened = own.astype(jnp.float32)
    own_norms = jnp.sum(widened * widened * ard_weight, axis=2)
    n_high = lax.reduce_precision(own_norms, 8, 7)
    n_mid = lax.reduce_precision(own_norms - n_high, 8, 7)
    n_low = own_norms - n_high - n_mid
    bits = jnp.stack([n_high, n_mid, n_low]).astype(jnp.bfloat16).transpose(2, 0, 1).reshape(sub, 3 * row_tiles)

    cut = own.reshape(row_tiles, sub, row_count, quarter).transpose(2, 0, 1, 3)
    extra = jnp.broadcast_to(nugget.reshape(1, row_tiles, sub, 1), (row_count, row_tiles, sub, 128))
    sent = lax.all_to_all(jnp.concatenate([cut, extra], axis=3), "row", 0, 0)
    sent = sent.reshape(row_count, 2, fold, sub, quarter + 128).transpose(2, 0, 1, 3, 4)
    sent = sent.reshape(col_count, 2, sub, quarter + 128)
    body = sent[..., :quarter]
    tags = sent[..., quarter]
    first = body[0, 0]
    first = jnp.broadcast_to(
        jnp.stack([first[:, :eighth], first[:, eighth:]])[None], (col_count // 2, 2, sub, eighth)
    ).reshape(col_count, sub, eighth)
    tail = jnp.concatenate(
        [jnp.broadcast_to(tags[0, 0][None, :, None], (col_count, sub, 1)),
         tags[:, 0, :, None], tags[:, 1, :, None],
         jnp.zeros((col_count, sub, 61), jnp.bfloat16),
         jnp.broadcast_to(bits[None], (col_count, sub, 3 * row_tiles)),
         jnp.zeros((col_count, sub, 64 - 3 * row_tiles), jnp.bfloat16)], axis=2)
    got = lax.all_to_all(jnp.concatenate([body[:, 0], body[:, 1], first, tail], axis=2), "col", 0, 0)
    got = got.reshape(NB, -1)
    tags = got[:, 2 * quarter + eighth :].astype(jnp.float32)
    nug_own = tags[:, :3].T
    norm_bits = tags[:, 64 : 64 + 3 * row_tiles].reshape(NB, 3, row_tiles)
    norms = ((norm_bits[:, 0] + norm_bits[:, 1]) + norm_bits[:, 2]).T
    nug_sib = swap(nug_own)
    nug = jnp.concatenate([nug_own, nug_sib[1:]], axis=0).reshape(1, 5 * NB)

    up = [(i, (i + 1) % row_count) for i in range(row_count)]
    down = [(i, (i - 1) % row_count) for i in range(row_count)]
    homes = [lax.rem(row_index + 4 - d, row_count) for d in (0, 1, 3, 2)]

    zero_piece = got[:, 2 * quarter : 2 * quarter + eighth]
    below = lax.ppermute(zero_piece, "row", up)
    above = lax.ppermute(zero_piece, "row", down)
    far = jnp.concatenate(
        [lax.ppermute(below[: NB // 2], "row", up), lax.ppermute(above[NB // 2 :], "row", down)], axis=0)
    half0 = jnp.zeros((NB, 4 * eighth), jnp.bfloat16)
    for home, value in zip(homes, (zero_piece, below, above, far)):
        half0 = lax.dynamic_update_slice(half0, value, (0, home * eighth))
    half1 = swap(half0)
    even = jnp.where(core == 0, half0, half1).reshape(NB, 4, 1, eighth)
    odd = jnp.where(core == 0, half1, half0).reshape(NB, 4, 1, eighth)
    raw0 = jnp.concatenate([even, odd], axis=2).reshape(NB, features)
    wide0 = raw0.astype(jnp.float32)
    scaled0 = (wide0 * ard_weight).astype(jnp.bfloat16)
    norms0 = jnp.sum(wide0 * wide0 * ard_weight, axis=1)
    cross = lax.dot_general(raw0, scaled0, NT, preferred_element_type=jnp.float32)
    tile0 = jnp.exp(-0.5 * (norms0[:, None] + norms0[None, :] - 2.0 * cross)) + jnp.diag(nug[0, :NB])
    corner, inverse = factor_corner(0.5 * (tile0 + tile0.T))

    piece = got[:, : 2 * quarter].reshape(NB, 2, quarter).transpose(1, 0, 2)
    below = lax.ppermute(piece, "row", up)
    above = lax.ppermute(piece, "row", down)
    far = jnp.concatenate(
        [lax.ppermute(below[:1], "row", up), lax.ppermute(above[1:], "row", down)], axis=0)
    scaled_c = jnp.zeros((4, NB, features), jnp.bfloat16)
    norms_c = jnp.zeros((4, NB), jnp.float32)
    cross_c = jnp.zeros((4 * NB, NB), jnp.float32)
    for home, value in zip(homes, (piece, below, above, far)):
        raw = jnp.concatenate([value, swap(value)], axis=0)
        weight = lax.dynamic_slice_in_dim(ard_weight, home * quarter, quarter)
        wide = raw.astype(jnp.float32)
        scaled_c = lax.dynamic_update_slice(
            scaled_c, (wide * weight).astype(jnp.bfloat16), (0, 0, home * quarter))
        norms_c = norms_c + jnp.sum(wide * wide * weight, axis=2)
        against = lax.dynamic_slice_in_dim(scaled0, home * quarter, quarter, 1)
        cross_c = cross_c + lax.dot_general(
            raw.reshape(4 * NB, quarter), against, NT, preferred_element_type=jnp.float32)
    norms_c = norms_c.reshape(-1)
    kern_c = jnp.exp(-0.5 * (norms_c[:, None] + norms0[None, :] - 2.0 * cross_c))
    q_panel = stacked(dot_high(inverse, kern_c, NT))
    inverse3 = stacked(inverse.T)

    norms = norms.reshape(row_tiles, 4, 4, 2, sub)
    norms = lax.dynamic_index_in_dim(norms, core, 3, keepdims=False)
    norms = rolled(rolled(norms, 1, chip_y), 2, chip_x)
    ring_of = jnp.array(RING, jnp.int32)
    ys = lax.rem(chip_y + ring_of, 4)
    xs = lax.rem(chip_x + ring_of, 4)
    chips = ys[:, None] * 4 + xs[None, :]
    grow = (lax.iota(jnp.int32, row_tiles)[:, None, None, None] * row_count + row_index) * NB
    grow = grow + chips[None, :, :, None] * 16 + core * 8 + lax.iota(jnp.int32, sub)

    def arrange(value, order):
        a = value[:fold].transpose(1, 2, 0, 3).reshape(4, NB)
        b = value[fold:].transpose(2, 1, 0, 3).reshape(4, NB)
        return jnp.concatenate([a[order], b[order]]).reshape(-1, 1)

    near, last = slice(0, 3), slice(3, 4)

    def where_of(order):
        head = jnp.stack([row_index, col_index])
        lines = jnp.concatenate([chips[order], chips.T[order]]).reshape(-1)
        return jnp.concatenate([head, lines]).astype(jnp.int32)

    tile_j = jnp.stack([0 * col_index, col_index, col_index + 32, col_index ^ 1, (col_index ^ 1) + 32])
    gcol = (tile_j[:, None] * NB + lax.iota(jnp.int32, NB)).astype(jnp.int32).reshape(1, 5 * NB)
    wn = jnp.concatenate([norms0, norms_c]).reshape(1, -1)
    rest = (scaled0, scaled_c, wn, nug, gcol, inverse3, q_panel, corner)

    def flat(value):
        return value.reshape(-1, features)

    near_pieces = [flat(v) for v in (four_a, grid_a[0], grid_a[1], four_b, grid_b[0], grid_b[1])]
    near_cuts = tuple((i, 0, NB) for i in range(6))
    own1, sib1 = run_main(
        near_pieces, near_cuts, 3, where_of(near), arrange(norms, near), arrange(grow, near), rest)
    last_pieces = [flat(v) for v in (grid_a[2], grid_a[3], grid_b[2], grid_b[3])]
    last_cuts = ((0, 0, 128), (0, 128, 128), (1, 0, 128), (1, 128, 128))
    own2, sib2 = run_main(
        last_pieces, last_cuts, 1, where_of(last), arrange(norms, last), arrange(grow, last), rest)
    shape = (row_tiles, 16, 2, 4 * sub, 128)
    kinds1 = tuple((i < 3, i) for i in range(6))
    kinds2 = tuple((i < 1, i) for i in range(2))

    def lines(value):
        return value.reshape(-1, 4, fold, 4 * sub, 128)

    out = place((lines(own1), lines(swap(sib1))), ((True, kinds1), (False, kinds1)), where_of(near), None, shape)
    out = place((lines(own2), lines(swap(sib2))), ((True, kinds2), (False, kinds2)), where_of(last), out, shape)
    return out.reshape(row_tiles, 1, NB, 2, 1, NB)


def solution(mesh):
    placed = (P(None, "row", "col", None, None), P(), P(None, "row", "col", None))
    return jax.shard_map(
        local,
        mesh=mesh,
        in_specs=placed,
        out_specs=P(None, "row", None, None, "col", None),
        check_vma=False,
    )
```

time: 228 us -> 620 us (2.72); the launches traced: 226 us -> 608 us
  Pallas kernels: 64.4 us -> 349 us
  local copies, waits for them, and re-layouts: 19 us -> 90.5 us
  blocking collectives: 43.4 us -> 0 us
  starting transfers between devices: 11.9 us -> 51.2 us
  waiting for transfers between devices: 61.4 us -> 80.8 us
  other arithmetic: 8.32 us -> 26.5 us
  between operations: 13.7 us -> 1.68 us
    pallas_call x2 -> x5, Pallas kernels: 64.4 us -> 349 us  [the longest x2 258 us: place(): pl.pallas_call(functools.partial(place_kernel, plan), out_shape=jax.Shape...]
    all_to_all x1 -> x0, blocking collectives: 43.4 us -> none  [local(): got = lax.all_to_all(sent, 'col', 0, 0)]
    ppermute x4 -> x32, starting transfers between devices: 6.53 us -> 41.8 us  [the longest x4 12.8 us: ring(): far1 = lax.ppermute(above[cut:], 'col', down)]
    slice x5 -> x52, local copies, waits for them, and re-layouts: 4.21 us -> 31.6 us  [the longest x4 8.07 us: ring(): far1 = lax.ppermute(above[cut:], 'col', down)]
    ppermute x4 -> x32, waiting for transfers between devices: 44.6 us -> 64.3 us  [the longest x4 29.8 us: ring(): above = lax.ppermute(value, 'col', down)]
    unnamed x17 -> x86, local copies, waits for them, and re-layouts: 1.61 us -> 20.2 us
    all_to_all x0 -> x1, waiting for transfers between devices: none -> 16.6 us  [local(): lax.all_to_all(jnp.concatenate([body[:, 0], body[:, 1], first, tail], axi...]
    all_to_all x1, waiting for transfers between devices: 16 us -> 0.01 us  [local(): sent = lax.all_to_all(jnp.concatenate([cut, extra], axis=3), 'row', 0, 0)]
  transfers between devices with their start and end apart: 6 -> 34, of which waited for: 4 -> 9; matrix products, arithmetic and copies ran while one was open for 13% -> 19% of each run, Pallas kernels for 11% -> 40%
where the time goes in v2:
time: 620 us; the launch traced here: 608 us
  Pallas kernels  349 us (56%)
  local copies, waits for them, and re-layouts  90.5 us (15%)
  waiting for transfers between devices  80.8 us (13%)
  starting transfers between devices  51.2 us (8%)
  other arithmetic  26.5 us (4%)
  matrix products  7.59 us (1%)
    pallas_call x2, Pallas kernels, place(): pl.pallas_call(functools.partial(place_kernel, plan), out_shape=jax.Shape...  258 us
    pallas_call x2, Pallas kernels, run_main(): pl.pallas_call(functools.partial(main_kernel, cuts, a_count), out_shape=(...  60.3 us
    pallas_call x1, Pallas kernels, factor_corner(): pl.pallas_call(corner_kernel, out_shape=(shape, shape), cost_estimate=pl....  30.9 us
    ppermute x4, waiting for transfers between devices, ring(): above = lax.ppermute(value, 'col', down)  29.8 us
    unnamed x86, local copies, waits for them, and re-layouts  20.2 us
    all_to_all x1, waiting for transfers between devices, local(): lax.all_to_all(jnp.concatenate([body[:, 0], body[:, 1], first, tail], axi...  16.6 us
    ppermute x4, waiting for transfers between devices, ring(): far0 = lax.ppermute(below[:cut], 'col', up)  14.1 us
    ppermute x1, waiting for transfers between devices, local(): lax.ppermute(below[:NB // 2], 'row', up)  13.5 us
  transfers between devices with their start and end apart: 34, of which 9 were waited for; matrix products, arithmetic and copies ran while one was open for 19% of the time, Pallas kernels for 40%

profile of v2, /device:TPU:0, one launch (start us, length us, event | category | flops | bytes accessed | tf_op | source)
XLA Modules:
  0.0 607.8 jit_solution(16899893880318033725)
XLA Ops:
  0.0 2.4 slice_bitcast_fusion.2
  2.4 1.6 collective-permute-start
  4.0 1.7 collective-permute-start.1
  5.7 1.7 collective-permute-start.8
  7.3 1.6 collective-permute-start.9
  11.7 5.4 all-to-all-start
  22.0 1.7 slice.305
  23.7 3.0 collective-permute-start.3
  26.7 1.7 slice.308
  28.7 1.7 slice.309
  30.4 2.9 collective-permute-start.11
  33.3 1.9 constant_dynamic-update-slice_fusion.3
  35.2 1.9 constant_dynamic-update-slice_fusion.2
  37.0 1.9 constant_dynamic-update-slice_fusion.8
  38.9 1.9 constant_dynamic-update-slice_fusion.7
  42.6 1.9 concatenate.95
  44.5 4.0 all-to-all-start.1
  48.5 1.7 constant_dynamic-update-slice_fusion
  50.2 1.7 constant_dynamic-update-slice_fusion.6
  51.8 1.7 constant_dynamic-update-slice_fusion.5
  53.5 16.6 %all-to-all-done.1 = bf16[32,8,2688]{2,1,0:T(8,128)(2,1)S(1)} async-done(((bf16[32,8,2688]{2,1,0:T(8,128)(2,1)}), bf16[32,8,2688]{2,1,0:T(8,128)(2,1)S(1)}, u32[]{:S(2)}, u32[]{:S(2)}) %all-to-all-start.1) | async-done | bytes 1376288 | tf_op jit(solution)/shard_map/all_to_all | solution.py:309
  71.9 2.1 collective-permute-start.16
  75.5 1.3 copy.166
  76.8 1.5 copy.167
  79.2 2.5 collective-permute-start.24
  87.6 3.3 collective-permute-start.19
  94.5 13.5 %collective-permute-done.18 = bf16[128,512]{1,0:T(8,128)(2,1)S(1)} collective-permute-done((bf16[128,512]{1,0:T(8,128)(2,1)S(1)}, bf16[128,512]{1,0:T(8,128)(2,1)S(1)}, u32[]{:S(2)}, u32[]{:S(2)}) %collective-permute-start.18) | collective-permute-done | bytes 131104 | tf_op jit(solution)/shard_map/ppermute | solution.py:326
  110.5 1.9 slice.316
  112.6 1.9 slice.317
  114.5 3.0 collective-permute-start.27
  117.5 2.3 constant_dynamic-update-slice_fusion.11
  119.8 2.3 constant_dynamic-update-slice_fusion.13
  122.1 1.8 fusion.2
  125.0 3.4 pad_maximum_fusion.1
  128.9 4.6 broadcast_select_fusion.1
  133.6 1.5 copy.163
  135.1 2.3 copy.164
  137.3 1.5 fusion.28
  138.8 5.3 copy.165
  144.1 6.7 %reshape.359 = f32[256,4096]{1,0:T(8,128)} reshape(f32[256,4,2,512]{3,2,1,0:T(2,128)} %copy.165) | data formatting | bytes 8388608 | tf_op jit(solution)/shard_map/convert_element_type | solution.py:334
  150.9 4.0 multiply_convert_fusion.1.refs_4_.refs_6_
  155.5 1.6 fusion.41
  158.3 1.8 fusion.40.a_ref
  160.1 30.9 %shard_map.46 = (f32[256,256]{1,0:T(8,128)}, f32[256,256]{1,0:T(8,128)}) custom-call(f32[256,256]{1,0:T(8,128)} %fusion.40.a_ref), custom_call_target="tpu_custom_call" | custom-call | flops 10000000000 | bytes 1048576 | tf_op jit(solution)/shard_map/pallas_call | solution.py:77
  192.2 2.6 fusion.33
  194.8 3.3 collective-permute-start.6
  200.5 3.3 collective-permute-start.14
  205.8 1.7 constant_dynamic-update-slice_fusion.12
  215.1 28.3 %collective-permute-done.6 = bf16[4,64,4096]{2,1,0:T(8,128)(2,1)} collective-permute-done((bf16[4,64,4096]{2,1,0:T(8,128)(2,1)}, bf16[4,64,4096]{2,1,0:T(8,128)(2,1)}, u32[]{:S(2)}, u32[]{:S(2)}) %collective-permute-start.6) | collective-permute-done | bytes 2097184 | tf_op jit(solution)/shard_map/ppermute | solution.py:272
  243.5 3.3 collective-permute-done.12
  246.8 1.5 collective-permute-done.14
  248.3 42.6 %shard_map.48 = (f32[6,1024,128]{2,1,0:T(8,128)}, f32[6,1024,128]{2,1,0:T(8,128)}) custom-call(s32[26]{0:T(128)S(1)} %copy-done.4, f32[1536,1]{1,0:T(8,128)S(1)} %bitcast.173, s32[1536,1]{1,0:T(8,128)S(1)} %bitcast.172, bf16[256,4096]{1,0:T(8,128)(2,1)} %bitcast.56.refs_0_, bf16[256,4096]{1,0:T(8,128)(2,1)} %bitcast.57.refs_1_, ...), custom_call_target="tpu_custom_call" | custom-call | flops 16106127360 | bytes 25165824 | tf_op jit(solution)/shard_map/pallas_call | solution.py:176
  292.4 2.4 slice.307
  294.8 3.2 collective-permute-start.7
  298.1 2.3 slice.310
  300.4 2.3 slice.311
  302.7 3.8 collective-permute-start.15
  311.7 7.6 %collective-permute-done.5 = bf16[2,64,4096]{2,1,0:T(8,128)(2,1)} collective-permute-done((bf16[2,64,4096]{2,1,0:T(8,128)(2,1)S(1)}, bf16[2,64,4096]{2,1,0:T(8,128)(2,1)}, u32[]{:S(2)}, u32[]{:S(2)}) %collective-permute-start.5) | collective-permute-done | bytes 1048608 | tf_op jit(solution)/shard_map/ppermute | solution.py:273
  319.3 1.9 collective-permute-done.7
  321.2 6.6 %collective-permute-done.13 = bf16[2,64,4096]{2,1,0:T(8,128)(2,1)} collective-permute-done((bf16[2,64,4096]{2,1,0:T(8,128)(2,1)}, bf16[2,64,4096]{2,1,0:T(8,128)(2,1)}, u32[]{:S(2)}, u32[]{:S(2)}) %collective-permute-start.13) | collective-permute-done | bytes 1048608 | tf_op jit(solution)/shard_map/ppermute | solution.py:273
  327.7 1.6 collective-permute-done.15
  329.3 17.7 %shard_map.47 = (f32[2,1024,128]{2,1,0:T(8,128)S(1)}, f32[2,1024,128]{2,1,0:T(8,128)S(1)}) custom-call(s32[10]{0:T(128)S(1)} %pad_add_fusion.2.where_ref, f32[512,1]{1,0:T(8,128)S(1)} %bitcast.175, s32[512,1]{1,0:T(8,128)S(1)} %bitcast.174, bf16[128,4096]{1,0:T(8,128)(2,1)} %bitcast.32.refs_0_, bf16[128,4096]{1,0:T(8,128)(2,1)} %bitcast.33.refs_1_, ...), custom_call_target="tpu_custom_call" | custom-call | flops 5368709120 | bytes 8388608 | tf_op jit(solution)/shard_map/pallas_call | solution.py:176
  348.0 192.8 %shard_map.49.refs_2_ = f32[16,16,2,32,128]{4,3,2,1,0:T(8,128)} custom-call(s32[26]{0:T(128)} %pad_add_fusion.3.where_ref, f32[6,4,8,32,128]{4,3,2,1,0:T(8,128)} %bitcast.202, f32[6,4,8,32,128]{4,3,2,1,0:T(8,128)} %bitcast.63.refs_1_), custom_call_target="tpu_custom_call" | custom-call | bytes 12582912 | tf_op jit(solution)/shard_map/pallas_call | solution.py:220
  541.9 65.4 %shard_map.50 = f32[16,16,2,32,128]{4,3,2,1,0:T(8,128)} custom-call(s32[10]{0:T(128)} %copy-done.5, f32[2,4,8,32,128]{4,3,2,1,0:T(8,128)} %bitcast.171, f32[2,4,8,32,128]{4,3,2,1,0:T(8,128)} %bitcast.205, f32[16,16,2,32,128]{4,3,2,1,0:T(8,128)} %shard_map.49.refs_2_), custom_call_target="tpu_custom_call", output_to_operand_aliasing={{}: (3, {})} | custom-call | bytes 4194304 | tf_op jit(solution)/shard_map/pallas_call | solution.py:220
  (255 shorter events, 50.9 us)
Async XLA Ops:
  0.0 8.9 %copy-start.10 = (bf16[16,1,1,8,4096]{4,3,2,1,0:T(8,128)(2,1)S(1)}, bf16[16,1,1,8,4096]{4,3,2,1,0:T(8,128)(2,1)}, u32[]{:S(2)}) copy-start(bf16[16,1,1,8,4096]{4,3,2,1,0:T(8,128)(2,1)} %param.4) | copy-start | bytes 3145732
  0.0 9.7 %copy-start.28 = (bf16[16,1,1,8]{0,3,2,1:T(8,128)(2,1)S(1)}, bf16[16,1,1,8]{0,3,2,1:T(8,128)(2,1)}, u32[]{:S(2)}) copy-start(bf16[16,1,1,8]{0,3,2,1:T(8,128)(2,1)} %param.6) | copy-start | bytes 772
  2.4 18.2 %collective-permute-start = (bf16[8,8,4096]{2,1,0:T(8,128)(2,1)}, bf16[8,8,4096]{2,1,0:T(8,128)(2,1)}, u32[]{:S(2)}, u32[]{:S(2)}) collective-permute-start(bf16[8,8,4096]{2,1,0:T(8,128)(2,1)} %get-tuple-element.26), channel_id=1, source_target_pairs={{0,2},{1,3},{2,4},{3,5},{4,6},{5,7},{6,0},{7,1},{8,10},{9,11},{10,... | collective-permute-start | bytes 1572872 | tf_op jit(solution)/shard_map/ppermute | solution.py:271
  4.0 18.0 %collective-permute-start.1 = (bf16[8,8,4096]{2,1,0:T(8,128)(2,1)}, bf16[8,8,4096]{2,1,0:T(8,128)(2,1)}, u32[]{:S(2)}, u32[]{:S(2)}) collective-permute-start(bf16[8,8,4096]{2,1,0:T(8,128)(2,1)} %get-tuple-element.26), channel_id=1, source_target_pairs={{0,6},{1,7},{2,0},{3,1},{4,2},{5,3},{6,4},{7,5},{8,14},{9,15},{10,... | collective-permute-start | bytes 1572872 | tf_op jit(solution)/shard_map/ppermute | solution.py:272
  5.7 21.0 %collective-permute-start.8 = (bf16[8,8,4096]{2,1,0:T(8,128)(2,1)}, bf16[8,8,4096]{2,1,0:T(8,128)(2,1)}, u32[]{:S(2)}, u32[]{:S(2)}) collective-permute-start(bf16[8,8,4096]{2,1,0:T(8,128)(2,1)} %get-tuple-element.25), channel_id=1, source_target_pairs={{0,8},{1,9},{2,10},{3,11},{4,12},{5,13},{6,14},{7,15},{8,16},{9,17... | collective-permute-start | bytes 1572872 | tf_op jit(solution)/shard_map/ppermute | solution.py:271
  7.3 21.4 %collective-permute-start.9 = (bf16[8,8,4096]{2,1,0:T(8,128)(2,1)}, bf16[8,8,4096]{2,1,0:T(8,128)(2,1)}, u32[]{:S(2)}, u32[]{:S(2)}) collective-permute-start(bf16[8,8,4096]{2,1,0:T(8,128)(2,1)} %get-tuple-element.25), channel_id=1, source_target_pairs={{0,24},{1,25},{2,26},{3,27},{4,28},{5,29},{6,30},{7,31},{8,0},{9,1... | collective-permute-start | bytes 1572872 | tf_op jit(solution)/shard_map/ppermute | solution.py:272
  10.6 6.5 %copy-start.18 = (f32[4096]{0:T(1024)S(1)}, f32[4096]{0:T(1024)}, u32[]{:S(2)}) copy-start(f32[4096]{0:T(1024)} %param.5) | copy-start | bytes 49156
  11.7 29.8 %all-to-all-start = ((bf16[4,16,8,1152]{3,2,1,0:T(8,128)(2,1)}), bf16[4,16,8,1152]{3,2,1,0:T(8,128)(2,1)S(1)}, u32[]{:S(2)}, u32[]{:S(2)}) async-start(bf16[4,16,8,1152]{3,2,1,0:T(8,128)(2,1)} %copy.147), calls=%async_computation | async-start | bytes 2359296 | tf_op jit(solution)/shard_map/all_to_all | solution.py:294
  17.1 1.7 copy-start.29
  18.9 1.8 copy-start.26
  18.9 1.8 copy-start.27
  19.2 1.5 copy-start.19
  19.2 1.5 copy-start.20
  20.7 190.0 %copy-start.24 = (f32[1024]{0:T(1024)}, f32[1024]{0:T(1024)S(1)}, u32[]{:S(2)}) copy-start(f32[1024]{0:T(1024)S(1)} %get-tuple-element.39) | copy-start | bytes 12292
  21.7 19.1 %collective-permute-start.2 = (bf16[4,8,4096]{2,1,0:T(8,128)(2,1)S(1)}, bf16[4,8,4096]{2,1,0:T(8,128)(2,1)S(1)}, u32[]{:S(2)}, u32[]{:S(2)}) collective-permute-start(bf16[4,8,4096]{2,1,0:T(8,128)(2,1)S(1)} %slice.304), channel_id=1, source_target_pairs={{0,2},{1,3},{2,4},{3,5},{4,6},{5,7},{6,0},{7,1},{8,10},{9,11},{10,... | collective-permute-start | bytes 786440 | tf_op jit(solution)/shard_map/ppermute | solution.py:273
  23.7 24.8 %collective-permute-start.3 = (bf16[4,8,4096]{2,1,0:T(8,128)(2,1)}, bf16[4,8,4096]{2,1,0:T(8,128)(2,1)}, u32[]{:S(2)}, u32[]{:S(2)}) collective-permute-start(bf16[4,8,4096]{2,1,0:T(8,128)(2,1)} %slice.305), channel_id=1, source_target_pairs={{0,6},{1,7},{2,0},{3,1},{4,2},{5,3},{6,4},{7,5},{8,14},{9,15},{10,... | collective-permute-start | bytes 786440 | tf_op jit(solution)/shard_map/ppermute | solution.py:274
  28.4 21.8 %collective-permute-start.10 = (bf16[4,8,4096]{2,1,0:T(8,128)(2,1)}, bf16[4,8,4096]{2,1,0:T(8,128)(2,1)}, u32[]{:S(2)}, u32[]{:S(2)}) collective-permute-start(bf16[4,8,4096]{2,1,0:T(8,128)(2,1)} %slice.308), channel_id=1, source_target_pairs={{0,8},{1,9},{2,10},{3,11},{4,12},{5,13},{6,14},{7,15},{8,16},{9,17... | collective-permute-start | bytes 786440 | tf_op jit(solution)/shard_map/ppermute | solution.py:273
  30.4 21.4 %collective-permute-start.11 = (bf16[4,8,4096]{2,1,0:T(8,128)(2,1)}, bf16[4,8,4096]{2,1,0:T(8,128)(2,1)}, u32[]{:S(2)}, u32[]{:S(2)}) collective-permute-start(bf16[4,8,4096]{2,1,0:T(8,128)(2,1)} %slice.309), channel_id=1, source_target_pairs={{0,24},{1,25},{2,26},{3,27},{4,28},{5,29},{6,30},{7,31},{8,0},{9,1... | collective-permute-start | bytes 786440 | tf_op jit(solution)/shard_map/ppermute | solution.py:274
  44.5 25.6 %all-to-all-start.1 = ((bf16[32,8,2688]{2,1,0:T(8,128)(2,1)}), bf16[32,8,2688]{2,1,0:T(8,128)(2,1)S(1)}, u32[]{:S(2)}, u32[]{:S(2)}) async-start(bf16[32,8,2688]{2,1,0:T(8,128)(2,1)} %concatenate.95), calls=%async_computation.1 | async-start | bytes 2752512 | tf_op jit(solution)/shard_map/all_to_all | solution.py:309
  70.1 6.7 %copy-start.14 = (bf16[32,8,2688]{2,1,0:T(8,128)(2,1)}, bf16[32,8,2688]{2,1,0:T(8,128)(2,1)S(1)}, u32[]{:S(2)}) copy-start(bf16[32,8,2688]{2,1,0:T(8,128)(2,1)S(1)} %all-to-all-done.1) | copy-start | bytes 4128772
  71.9 13.7 %collective-permute-start.16 = (bf16[256,512]{1,0:T(8,128)(2,1)}, bf16[256,512]{1,0:T(8,128)(2,1)}, u32[]{:S(2)}, u32[]{:S(2)}) collective-permute-start(bf16[256,512]{1,0:T(8,128)(2,1)} %slice.312), channel_id=1, source_target_pairs={{0,32},{32,64},{64,96},{96,0},{1,33},{33,65},{65,97},{97,1},{2,34}... | collective-permute-start | bytes 786440 | tf_op jit(solution)/shard_map/ppermute | solution.py:323
  74.0 12.6 %collective-permute-start.17 = (bf16[256,512]{1,0:T(8,128)(2,1)}, bf16[256,512]{1,0:T(8,128)(2,1)}, u32[]{:S(2)}, u32[]{:S(2)}) collective-permute-start(bf16[256,512]{1,0:T(8,128)(2,1)} %slice.312), channel_id=1, source_target_pairs={{0,96},{32,0},{64,32},{96,64},{1,97},{33,1},{65,33},{97,65},{2,98}... | collective-permute-start | bytes 786440 | tf_op jit(solution)/shard_map/ppermute | solution.py:324
  78.3 43.8 %collective-permute-start.21 = (bf16[2,256,1024]{2,1,0:T(8,128)(2,1)S(1)}, bf16[2,256,1024]{2,1,0:T(8,128)(2,1)}, u32[]{:S(2)}, u32[]{:S(2)}) collective-permute-start(bf16[2,256,1024]{2,1,0:T(8,128)(2,1)S(1)} %bitcast.184), channel_id=1, source_target_pairs={{0,1},{1,0},{2,3},{3,2},{4,5},{5,4},{6,7},{7,6},{8,9},{9,8},{10,11... | collective-permute-start | bytes 3145736 | tf_op jit(solution)/shard_map/ppermute | solution.py:267
  78.4 32.2 %collective-permute-start.22 = (bf16[2,256,1024]{2,1,0:T(8,128)(2,1)S(1)}, bf16[2,256,1024]{2,1,0:T(8,128)(2,1)}, u32[]{:S(2)}, u32[]{:S(2)}) collective-permute-start(bf16[2,256,1024]{2,1,0:T(8,128)(2,1)S(1)} %bitcast.185), channel_id=1, source_target_pairs={{0,32},{32,64},{64,96},{96,0},{1,33},{33,65},{65,97},{97,1},{2,34}... | collective-permute-start | bytes 3145736 | tf_op jit(solution)/shard_map/ppermute | solution.py:342
  79.2 33.5 %collective-permute-start.24 = (bf16[2,256,1024]{2,1,0:T(8,128)(2,1)S(1)}, bf16[2,256,1024]{2,1,0:T(8,128)(2,1)}, u32[]{:S(2)}, u32[]{:S(2)}) collective-permute-start(bf16[2,256,1024]{2,1,0:T(8,128)(2,1)S(1)} %bitcast.186), channel_id=1, source_target_pairs={{0,96},{32,0},{64,32},{96,64},{1,97},{33,1},{65,33},{97,65},{2,98}... | collective-permute-start | bytes 3145736 | tf_op jit(solution)/shard_map/ppermute | solution.py:343
  83.1 10.7 %copy-start.22 = (f32[4,4,8,8]{2,3,1,0:T(8,128)}, f32[4,4,8,8]{2,3,1,0:T(8,128)S(1)}, u32[]{:S(2)}) copy-start(f32[4,4,8,8]{2,3,1,0:T(8,128)S(1)} %get-tuple-element.33) | copy-start | bytes 12292
  86.5 21.4 %collective-permute-start.18 = (bf16[128,512]{1,0:T(8,128)(2,1)S(1)}, bf16[128,512]{1,0:T(8,128)(2,1)S(1)}, u32[]{:S(2)}, u32[]{:S(2)}) collective-permute-start(bf16[128,512]{1,0:T(8,128)(2,1)S(1)} %slice.313), channel_id=1, source_target_pairs={{0,32},{32,64},{64,96},{96,0},{1,33},{33,65},{65,97},{97,1},{2,34}... | collective-permute-start | bytes 393224 | tf_op jit(solution)/shard_map/ppermute | solution.py:326
  87.6 20.4 %collective-permute-start.19 = (bf16[128,512]{1,0:T(8,128)(2,1)S(1)}, bf16[128,512]{1,0:T(8,128)(2,1)S(1)}, u32[]{:S(2)}, u32[]{:S(2)}) collective-permute-start(bf16[128,512]{1,0:T(8,128)(2,1)S(1)} %slice.314), channel_id=1, source_target_pairs={{0,96},{32,0},{64,32},{96,64},{1,97},{33,1},{65,33},{97,65},{2,98}... | collective-permute-start | bytes 393224 | tf_op jit(solution)/shard_map/ppermute | solution.py:326
  108.0 2.2 collective-permute-start.29
  108.8 19.6 %collective-permute-start.20 = (bf16[256,2048]{0,1:T(8,128)(2,1)}, bf16[256,2048]{0,1:T(8,128)(2,1)}, u32[]{:S(2)}, u32[]{:S(2)}) collective-permute-start(bf16[256,2048]{0,1:T(8,128)(2,1)} %constant_dynamic-update-slice_fusion.17), channel_id=1, source_target_pairs={{0,1},{1,0},{2,3},{3,2},{4,5},{5,4},{6,7},{7,6},{8,9},{9,8},{10,11... | collective-permute-start | bytes 3145736 | tf_op jit(solution)/shard_map/ppermute | solution.py:267
  110.2 104.9 %collective-permute-start.4 = (bf16[4,64,4096]{2,1,0:T(8,128)(2,1)}, bf16[4,64,4096]{2,1,0:T(8,128)(2,1)}, u32[]{:S(2)}, u32[]{:S(2)}) collective-permute-start(bf16[4,64,4096]{2,1,0:T(8,128)(2,1)} %bitcast.31), channel_id=1, source_target_pairs={{0,8},{1,9},{2,10},{3,11},{4,12},{5,13},{6,14},{7,15},{8,16},{9,17... | collective-permute-start | bytes 6291464 | tf_op jit(solution)/shard_map/ppermute | solution.py:271
  112.4 82.4 %collective-permute-start.26 = (bf16[1,256,1024]{2,1,0:T(8,128)(2,1)}, bf16[1,256,1024]{2,1,0:T(8,128)(2,1)S(1)}, u32[]{:S(2)}, u32[]{:S(2)}) collective-permute-start(bf16[1,256,1024]{2,1,0:T(8,128)(2,1)} %slice.316), channel_id=1, source_target_pairs={{0,32},{32,64},{64,96},{96,0},{1,33},{33,65},{65,97},{97,1},{2,34}... | collective-permute-start | bytes 1572872 | tf_op jit(solution)/shard_map/ppermute | solution.py:345
  114.5 83.6 %collective-permute-start.27 = (bf16[1,256,1024]{2,1,0:T(8,128)(2,1)}, bf16[1,256,1024]{2,1,0:T(8,128)(2,1)}, u32[]{:S(2)}, u32[]{:S(2)}) collective-permute-start(bf16[1,256,1024]{2,1,0:T(8,128)(2,1)} %slice.317), channel_id=1, source_target_pairs={{0,96},{32,0},{64,32},{96,64},{1,97},{33,1},{65,33},{97,65},{2,98}... | collective-permute-start | bytes 1572872 | tf_op jit(solution)/shard_map/ppermute | solution.py:345
  122.1 78.4 %collective-permute-start.23 = (bf16[2,256,1024]{2,1,0:T(8,128)(2,1)}, bf16[2,256,1024]{2,1,0:T(8,128)(2,1)}, u32[]{:S(2)}, u32[]{:S(2)}) collective-permute-start(bf16[2,256,1024]{2,1,0:T(8,128)(2,1)} %collective-permute-done.22), channel_id=1, source_target_pairs={{0,1},{1,0},{2,3},{3,2},{4,5},{5,4},{6,7},{7,6},{8,9},{9,8},{10,11... | collective-permute-start | bytes 3145736 | tf_op jit(solution)/shard_map/ppermute | solution.py:267
  128.4 5.1 copy-start.12
  128.4 77.3 %collective-permute-start.25 = (bf16[2,256,1024]{2,1,0:T(8,128)(2,1)}, bf16[2,256,1024]{2,1,0:T(8,128)(2,1)}, u32[]{:S(2)}, u32[]{:S(2)}) collective-permute-start(bf16[2,256,1024]{2,1,0:T(8,128)(2,1)} %collective-permute-done.24), channel_id=1, source_target_pairs={{0,1},{1,0},{2,3},{3,2},{4,5},{5,4},{6,7},{7,6},{8,9},{9,8},{10,11... | collective-permute-start | bytes 3145736 | tf_op jit(solution)/shard_map/ppermute | solution.py:267
  150.9 4.0 copy-start.11
  192.2 6.0 copy-start.23
  192.2 16.7 %slice-start = ((s8[8388608]{0:T(1024)(128)(4,1)}), s8[4194304]{0:T(1024)(128)(4,1)S(1)}, s32[]{:S(2)}) async-start(s8[8388608]{0:T(1024)(128)(4,1)} %bitcast.189), calls=%async_computation.2 | async-start | bytes 8388608
  194.8 9.0 %copy-start.8 = (bf16[4,256,1024]{2,1,0:T(8,128)(2,1)S(1)}, bf16[4,256,1024]{2,1,0:T(8,128)(2,1)}, u32[]{:S(2)}) copy-start(bf16[4,256,1024]{2,1,0:T(8,128)(2,1)} %constant_dynamic-update-slice_fusion.11) | copy-start | bytes 6291460
  194.8 48.7 %collective-permute-start.6 = (bf16[4,64,4096]{2,1,0:T(8,128)(2,1)}, bf16[4,64,4096]{2,1,0:T(8,128)(2,1)}, u32[]{:S(2)}, u32[]{:S(2)}) collective-permute-start(bf16[4,64,4096]{2,1,0:T(8,128)(2,1)} %bitcast.31), channel_id=1, source_target_pairs={{0,24},{1,25},{2,26},{3,27},{4,28},{5,29},{6,30},{7,31},{8,0},{9,1... | collective-permute-start | bytes 6291464 | tf_op jit(solution)/shard_map/ppermute | solution.py:272
  198.1 48.7 %collective-permute-start.12 = (bf16[4,64,4096]{2,1,0:T(8,128)(2,1)S(1)}, bf16[4,64,4096]{2,1,0:T(8,128)(2,1)}, u32[]{:S(2)}, u32[]{:S(2)}) collective-permute-start(bf16[4,64,4096]{2,1,0:T(8,128)(2,1)S(1)} %bitcast.209), channel_id=1, source_target_pairs={{0,2},{1,3},{2,4},{3,5},{4,6},{5,7},{6,0},{7,1},{8,10},{9,11},{10,... | collective-permute-start | bytes 6291464 | tf_op jit(solution)/shard_map/ppermute | solution.py:271
  200.4 5.4 copy-start.9
  200.5 47.8 %collective-permute-start.14 = (bf16[4,64,4096]{2,1,0:T(8,128)(2,1)S(1)}, bf16[4,64,4096]{2,1,0:T(8,128)(2,1)}, u32[]{:S(2)}, u32[]{:S(2)}) collective-permute-start(bf16[4,64,4096]{2,1,0:T(8,128)(2,1)S(1)} %bitcast.210), channel_id=1, source_target_pairs={{0,6},{1,7},{2,0},{3,1},{4,2},{5,3},{6,4},{7,5},{8,14},{9,15},{10,... | collective-permute-start | bytes 6291464 | tf_op jit(solution)/shard_map/ppermute | solution.py:272
  205.1 3.8 slice-start.1
  205.7 2.4 copy-start.15
  205.7 4.8 collective-permute-start.28
  211.3 37.0 %copy-start.2 = (f32[1,1280]{1,0:T(1,128)}, f32[1,1280]{1,0:T(1,128)S(1)}, u32[]{:S(2)}) copy-start(f32[1,1280]{1,0:T(1,128)S(1)} %reshape.341.refs_6_.refs_8_) | copy-start | bytes 15364
  213.0 1.2 copy-start.25
  214.3 34.0 %copy-start = (bf16[768,1024]{1,0:T(8,128)(2,1)}, bf16[768,1024]{1,0:T(8,128)(2,1)S(1)}, u32[]{:S(2)}) copy-start(bf16[768,1024]{1,0:T(8,128)(2,1)S(1)} %pad_maximum_fusion.2.refs_10_.refs_12_) | copy-start | bytes 4718596
  214.3 34.0 %copy-start.4 = (s32[26]{0:T(128)S(1)}, s32[26]{0:T(128)}, u32[]{:S(2)}) copy-start(s32[26]{0:T(128)} %pad_add_fusion.3.where_ref) | copy-start | bytes 316
  214.3 34.0 %copy-start.6 = (f32[256,256]{1,0:T(8,128)S(1)}, f32[256,256]{1,0:T(8,128)}, u32[]{:S(2)}) copy-start(f32[256,256]{1,0:T(8,128)} %get-tuple-element.12.refs_11_.refs_13_) | copy-start | bytes 786436
  215.1 33.2 %copy-start.13 = (bf16[4,256,4096]{2,1,0:T(8,128)(2,1)}, bf16[4,256,4096]{2,1,0:T(8,128)(2,1)S(1)}, u32[]{:S(2)}) copy-start(bf16[4,256,4096]{2,1,0:T(8,128)(2,1)S(1)} %fusion.13.refs_5_.refs_7_) | copy-start | bytes 25165828
  291.0 57.1 %collective-permute-start.31 = (f32[6,1024,128]{2,1,0:T(8,128)}, f32[6,1024,128]{2,1,0:T(8,128)}, u32[]{:S(2)}, u32[]{:S(2)}) collective-permute-start(f32[6,1024,128]{2,1,0:T(8,128)} %get-tuple-element.16), channel_id=1, source_target_pairs={{0,1},{1,0},{2,3},{3,2},{4,5},{5,4},{6,7},{7,6},{8,9},{9,8},{10,11... | collective-permute-start | bytes 9437192 | tf_op jit(solution)/shard_map/ppermute | solution.py:267
  292.4 26.9 %collective-permute-start.5 = (bf16[2,64,4096]{2,1,0:T(8,128)(2,1)S(1)}, bf16[2,64,4096]{2,1,0:T(8,128)(2,1)}, u32[]{:S(2)}, u32[]{:S(2)}) collective-permute-start(bf16[2,64,4096]{2,1,0:T(8,128)(2,1)S(1)} %slice.306), channel_id=1, source_target_pairs={{0,8},{1,9},{2,10},{3,11},{4,12},{5,13},{6,14},{7,15},{8,16},{9,17... | collective-permute-start | bytes 3145736 | tf_op jit(solution)/shard_map/ppermute | solution.py:273
  294.8 34.5 %copy-start.3 = (f32[1,1280]{1,0:T(1,128)S(1)}, f32[1,1280]{1,0:T(1,128)}, u32[]{:S(2)}) copy-start(f32[1,1280]{1,0:T(1,128)} %copy-done.2) | copy-start | bytes 15364
  294.8 34.5 %copy-start.7 = (f32[256,256]{1,0:T(8,128)S(1)}, f32[256,256]{1,0:T(8,128)}, u32[]{:S(2)}) copy-start(f32[256,256]{1,0:T(8,128)} %get-tuple-element.12.refs_11_.refs_13_) | copy-start | bytes 786436
  294.8 26.3 %collective-permute-start.7 = (bf16[2,64,4096]{2,1,0:T(8,128)(2,1)}, bf16[2,64,4096]{2,1,0:T(8,128)(2,1)}, u32[]{:S(2)}, u32[]{:S(2)}) collective-permute-start(bf16[2,64,4096]{2,1,0:T(8,128)(2,1)} %slice.307), channel_id=1, source_target_pairs={{0,24},{1,25},{2,26},{3,27},{4,28},{5,29},{6,30},{7,31},{8,0},{9,1... | collective-permute-start | bytes 3145736 | tf_op jit(solution)/shard_map/ppermute | solution.py:274
  300.4 27.4 %collective-permute-start.13 = (bf16[2,64,4096]{2,1,0:T(8,128)(2,1)}, bf16[2,64,4096]{2,1,0:T(8,128)(2,1)}, u32[]{:S(2)}, u32[]{:S(2)}) collective-permute-start(bf16[2,64,4096]{2,1,0:T(8,128)(2,1)} %slice.310), channel_id=1, source_target_pairs={{0,2},{1,3},{2,4},{3,5},{4,6},{5,7},{6,0},{7,1},{8,10},{9,11},{10,... | collective-permute-start | bytes 3145736 | tf_op jit(solution)/shard_map/ppermute | solution.py:273
  302.7 26.6 %collective-permute-start.15 = (bf16[2,64,4096]{2,1,0:T(8,128)(2,1)}, bf16[2,64,4096]{2,1,0:T(8,128)(2,1)}, u32[]{:S(2)}, u32[]{:S(2)}) collective-permute-start(bf16[2,64,4096]{2,1,0:T(8,128)(2,1)} %slice.311), channel_id=1, source_target_pairs={{0,6},{1,7},{2,0},{3,1},{4,2},{5,3},{6,4},{7,5},{8,14},{9,15},{10,... | collective-permute-start | bytes 3145736 | tf_op jit(solution)/shard_map/ppermute | solution.py:274
  309.8 37.3 %copy-start.5 = (s32[10]{0:T(128)}, s32[10]{0:T(128)S(1)}, u32[]{:S(2)}) copy-start(s32[10]{0:T(128)S(1)} %pad_add_fusion.2.where_ref) | copy-start | bytes 124
  347.0 1.0 copy-start.1
  348.0 192.8 %collective-permute-start.30 = (f32[2,1024,128]{2,1,0:T(8,128)S(1)}, f32[2,1024,128]{2,1,0:T(8,128)S(1)}, u32[]{:S(2)}, u32[]{:S(2)}) collective-permute-start(f32[2,1024,128]{2,1,0:T(8,128)S(1)} %get-tuple-element.14), channel_id=1, source_target_pairs={{0,1},{1,0},{2,3},{3,2},{4,5},{5,4},{6,7},{7,6},{8,9},{9,8},{10,11... | collective-permute-start | bytes 3145736 | tf_op jit(solution)/shard_map/ppermute | solution.py:267
  540.8 1.0 copy-start.17
  (2 other events, 1.6 us)

commit v3 on v1

v3 whole, which is shorter than its diff:
```python
import functools

import jax
import jax.numpy as jnp
from jax import lax
from jax.experimental import pallas as pl
from jax.experimental.pallas import tpu as pltpu
from jax.sharding import PartitionSpec as P

NB = 256
HIGH = lax.Precision.HIGHEST
NT = (((1,), (1,)), ((), ()))
NN = (((1,), (0,)), ((), ()))
GRANT = 62 * 2**20
SMALL = pl.CostEstimate(flops=1, bytes_accessed=1, transcendentals=0)
VMEM = pl.BlockSpec(memory_space=pltpu.VMEM)
HBM = pl.BlockSpec(memory_space=pl.ANY)
SMEM = pl.BlockSpec(memory_space=pltpu.SMEM)


def dot_high(left, right, dims=NN):
    return lax.dot_general(left, right, dims, precision=HIGH, preferred_element_type=jnp.float32)


def dot_fast(left, right, dims):
    return lax.dot_general(left, right, dims, preferred_element_type=jnp.float32)


def halves(value):
    high = value.astype(jnp.bfloat16)
    low = (value - high.astype(jnp.float32)).astype(jnp.bfloat16)
    return high, low


def as_row(column):
    return jnp.broadcast_to(column, (column.shape[0], 128)).T[0:1, :]


def eliminate(block):
    size = block.shape[0]
    height = 32
    rows = lax.broadcasted_iota(jnp.int32, (size, size), 0)
    cols = lax.broadcasted_iota(jnp.int32, (size, size), 1)
    eye = (rows == cols).astype(jnp.float32)
    whole = jnp.concatenate([block, eye], axis=1)
    parts = [whole[g * height : (g + 1) * height] for g in range(size // height)]
    inner = lax.broadcasted_iota(jnp.int32, (height, 1), 0)
    for j in range(size):
        first, at = divmod(j, height)
        pivot_row = parts[first][at : at + 1, :]
        pivot_row = pivot_row * (1.0 / pivot_row[:, j : j + 1])
        for g in range(first, size // height):
            factor = parts[g][:, j : j + 1]
            if g == first:
                factor = jnp.where(inner > at, factor, 0.0)
            parts[g] = parts[g] - factor * pivot_row
    whole = jnp.concatenate(parts, axis=0)
    pivots = jnp.sum(whole[:, :size] * eye, axis=1, keepdims=True)
    root = lax.rsqrt(pivots)
    root = root * (1.5 - 0.5 * pivots * root * root)
    return whole[:, size:] * root


def store_factor(a_ref, l_ref, x_ref):
    half = NB // 2
    rows = lax.broadcasted_iota(jnp.int32, (half, half), 0)
    cols = lax.broadcasted_iota(jnp.int32, (half, half), 1)
    lower = rows >= cols
    zero = jnp.zeros((half, half), jnp.float32)
    a11, a21, a22 = a_ref[:half, :half], a_ref[half:, :half], a_ref[half:, half:]
    x11 = eliminate(a11)
    l21 = dot_high(a21, x11, NT)
    l_ref[:half, :half] = jnp.where(lower, dot_high(a11, x11, NT), 0.0)
    l_ref[:half, half:] = zero
    l_ref[half:, :half] = l21
    s22 = a22 - dot_high(l21, l21, NT)
    x22 = eliminate(s22)
    l_ref[half:, half:] = jnp.where(lower, dot_high(s22, x22, NT), 0.0)
    x_ref[:half, :half] = x11
    x_ref[:half, half:] = zero
    x_ref[half:, :half] = -dot_high(x22, dot_high(l21, x11))
    x_ref[half:, half:] = x22


def store_triple(out_ref, value):
    high, low = halves(value)
    size = value.shape[0]
    out_ref[:size, :] = high
    out_ref[size : 2 * size, :] = low
    out_ref[2 * size :, :] = high


def spots(where_ref, quarter):
    row = where_ref[0]
    return [pl.multiple_of(lax.rem(row + 4 - d, 4) * quarter, quarter) for d in (0, 1, 3, 2)]


def bring(sem, pairs):
    copies = [pltpu.make_async_copy(source, target, sem.at[n]) for n, (source, target) in enumerate(pairs)]
    for copy in copies:
        copy.start()
    for copy in copies:
        copy.wait()


def corner_kernel(where_ref, own_ref, below_ref, above_ref, far0_ref, far1_ref, weight_ref, nug_ref,
                  scaled_ref, norm_ref, l_ref, x_ref, x3_ref, raw_ref, a_ref, sem):
    quarter = own_ref.shape[1]
    own, below, above, far = spots(where_ref, quarter)
    bring(sem, (
        (own_ref, raw_ref.at[:, pl.ds(own, quarter)]),
        (below_ref, raw_ref.at[:, pl.ds(below, quarter)]),
        (above_ref, raw_ref.at[:, pl.ds(above, quarter)]),
        (far0_ref, raw_ref.at[: NB // 2, pl.ds(far, quarter)]),
        (far1_ref, raw_ref.at[NB // 2 :, pl.ds(far, quarter)]),
    ))
    norms = jnp.zeros((NB, 1), jnp.float32)
    cross = jnp.zeros((NB, NB), jnp.float32)
    for j in range(4):
        part = slice(j * quarter, (j + 1) * quarter)
        raw = raw_ref[:, part]
        wide = raw.astype(jnp.float32)
        product = wide * weight_ref[:, part]
        scaled = product.astype(jnp.bfloat16)
        scaled_ref[:, part] = scaled
        norms += jnp.sum(wide * wide * weight_ref[:, part], axis=1, keepdims=True)
        cross += dot_fast(raw, scaled, NT)
    row_norms = as_row(norms)
    norm_ref[...] = row_norms
    eye = lax.broadcasted_iota(jnp.int32, (NB, NB), 0) == lax.broadcasted_iota(jnp.int32, (NB, NB), 1)
    tile = jnp.exp(-0.5 * (norms + row_norms - 2.0 * cross)) + jnp.where(eye, nug_ref[...], 0.0)
    a_ref[...] = 0.5 * (tile + tile.T)
    store_factor(a_ref, l_ref, x_ref)
    store_triple(x3_ref, x_ref[...].T)


def column_kernel(where_ref, own_ref, below_ref, above_ref, far0_ref, far1_ref, weight_ref, scaled0_ref, norm0_ref,
                  x_ref, scaled_ref, norm_ref, q_ref, raw_ref, zero_ref, sem):
    quarter = own_ref.shape[1] // 2
    own, below, above, far = spots(where_ref, quarter)
    pairs = [(scaled0_ref, zero_ref)]
    for u in range(2):
        rows = slice(u * NB, (u + 1) * NB)
        part = slice(u * quarter, (u + 1) * quarter)
        pairs += [
            (own_ref.at[:, part], raw_ref.at[rows, pl.ds(own, quarter)]),
            (below_ref.at[:, part], raw_ref.at[rows, pl.ds(below, quarter)]),
            (above_ref.at[:, part], raw_ref.at[rows, pl.ds(above, quarter)]),
            (far0_ref.at[:, part], raw_ref.at[u * NB : u * NB + NB // 2, pl.ds(far, quarter)]),
            (far1_ref.at[:, part], raw_ref.at[u * NB + NB // 2 : (u + 1) * NB, pl.ds(far, quarter)]),
        ]
    bring(sem, pairs)
    norms = jnp.zeros((2 * NB, 1), jnp.float32)
    cross = jnp.zeros((2 * NB, NB), jnp.float32)
    for j in range(4):
        part = slice(j * quarter, (j + 1) * quarter)
        raw = raw_ref[:, part]
        wide = raw.astype(jnp.float32)
        scaled_ref[:, part] = (wide * weight_ref[:, part]).astype(jnp.bfloat16)
        norms += jnp.sum(wide * wide * weight_ref[:, part], axis=1, keepdims=True)
        cross += dot_fast(raw, zero_ref[:, part], NT)
    norm_ref[...] = as_row(norms)
    kern = jnp.exp(-0.5 * (norms + norm0_ref[...] - 2.0 * cross))
    store_triple(q_ref, dot_high(x_ref[...], kern, NT))


def main_kernel(tiles, rows_dev, where_ref, rows_ref, norm_ref, w0_ref, wc_ref, wn_ref, nug_ref, inv_ref, q_ref, l_ref, o_ref):
    step = pl.program_id(0)
    row, col = where_ref[0], where_ref[1]
    eye = lax.broadcasted_iota(jnp.int32, (NB, NB), 0) == lax.broadcasted_iota(jnp.int32, (NB, NB), 1)
    for n in range(tiles):
        tile = (step * tiles + n) * rows_dev + row
        data = rows_ref[n * NB : (n + 1) * NB, :]
        cross = jnp.concatenate([dot_fast(data, w0_ref[...], NT), dot_fast(data, wc_ref[...], NT)], axis=1)
        norms = norm_ref[n * NB : (n + 1) * NB, :]
        kern = jnp.exp(-0.5 * (norms + wn_ref[...] - 2.0 * cross))
        left = kern[:, :NB] + jnp.where(eye & (tile == 0), nug_ref[:, :NB], 0.0)
        high, low = halves(left)
        panel = lax.dot_general(
            jnp.concatenate([high, high, low], axis=1), inv_ref[...], NN, preferred_element_type=jnp.float32
        )
        high, low = halves(panel)
        update = lax.dot_general(
            jnp.concatenate([high, high, low], axis=1), q_ref[...], NN, preferred_element_type=jnp.float32
        )
        first_tile = tile == 0
        for u in range(2):
            part = slice(NB * (u + 1), NB * (u + 2))
            own = kern[:, part] + jnp.where(eye & (tile == col + 32 * u), nug_ref[:, part], 0.0)
            result = jnp.where(first_tile, own, own - update[:, NB * u : NB * (u + 1)])
            if u == 0:
                result = jnp.where(col == 0, jnp.where(first_tile, l_ref[...], panel), result)
            for half in range(2):
                o_ref[pl.ds(n * NB * 4 + 2 * u + half, NB, stride=4), :] = result[:, 128 * half : 128 * (half + 1)]


def local(samples, ard_weight, nugget):
    row_count = lax.axis_size("row")
    col_count = lax.axis_size("col")
    row_index = lax.axis_index("row")
    col_index = lax.axis_index("col")
    row_tiles, _, _, sub, features = samples.shape
    quarter = features // row_count
    fold = row_tiles // 2
    own = samples.reshape(row_tiles, sub, features)
    weight_row = ard_weight.reshape(1, features)
    f32, bf16 = jnp.float32, jnp.bfloat16
    shape = jax.ShapeDtypeStruct

    gathered = lax.all_gather(samples, "col", axis=2, tiled=True)

    widened = own.astype(f32)
    own_norms = jnp.sum(widened * widened * ard_weight, axis=2)
    n_high = lax.reduce_precision(own_norms, 8, 7)
    n_mid = lax.reduce_precision(own_norms - n_high, 8, 7)
    n_low = own_norms - n_high - n_mid
    bits = jnp.stack([n_high, n_mid, n_low]).astype(bf16).transpose(2, 0, 1).reshape(sub, 3 * row_tiles)

    cut = own.reshape(row_tiles, sub, row_count, quarter).transpose(2, 0, 1, 3)
    extra = jnp.broadcast_to(nugget.reshape(1, row_tiles, sub, 1), (row_count, row_tiles, sub, 128))
    sent = lax.all_to_all(jnp.concatenate([cut, extra], axis=3), "row", 0, 0)
    sent = sent.reshape(row_count, 2, fold, sub, quarter + 128).transpose(2, 0, 1, 3, 4)
    sent = sent.reshape(col_count, 2, sub, quarter + 128)
    body = sent[..., :quarter]
    tags = sent[..., quarter]
    tail = jnp.concatenate(
        [jnp.broadcast_to(tags[0, 0][None, :, None], (col_count, sub, 1)),
         tags[:, 0, :, None], tags[:, 1, :, None],
         jnp.zeros((col_count, sub, 61), bf16),
         jnp.broadcast_to(bits[None], (col_count, sub, 3 * row_tiles)),
         jnp.zeros((col_count, sub, 64 - 3 * row_tiles), bf16)], axis=2)
    first = jnp.broadcast_to(body[0, 0][None], (col_count, sub, quarter))
    got = lax.all_to_all(jnp.concatenate([body[:, 0], body[:, 1], first, tail], axis=2), "col", 0, 0)
    got = got.reshape(NB, -1)
    tags = got[:, 3 * quarter :].astype(f32)
    nug = tags[:, :3].T.reshape(1, 3 * NB)
    norm_bits = tags[:, 64 : 64 + 3 * row_tiles].reshape(NB, 3, row_tiles)
    norms = ((norm_bits[:, 0] + norm_bits[:, 1]) + norm_bits[:, 2]).T

    up = [(i, (i + 1) % row_count) for i in range(row_count)]
    down = [(i, (i - 1) % row_count) for i in range(row_count)]

    where = jnp.stack([row_index, col_index]).astype(jnp.int32)
    norms = norms.reshape(-1, 1)

    zero = got[:, 2 * quarter : 3 * quarter]
    below0, above0 = lax.ppermute(zero, "row", up), lax.ppermute(zero, "row", down)
    zero_far = (below0, above0, lax.ppermute(below0[: NB // 2], "row", up),
                lax.ppermute(above0[NB // 2 :], "row", down))
    zero_far, got = lax.optimization_barrier((zero_far, got))
    cols = got[:, : 2 * quarter]
    below, above = lax.ppermute(cols, "row", up), lax.ppermute(cols, "row", down)
    scaled0, norms0, corner, inverse, inverse3 = pl.pallas_call(
        corner_kernel,
        out_shape=(shape((NB, features), bf16), shape((1, NB), f32), shape((NB, NB), f32), shape((NB, NB), f32),
                   shape((3 * NB, NB), bf16)),
        in_specs=[SMEM] + [HBM] * 5 + [VMEM] * 2,
        out_specs=(VMEM,) * 5,
        scratch_shapes=[pltpu.VMEM((NB, features), bf16), pltpu.VMEM((NB, NB), f32), pltpu.SemaphoreType.DMA((5,))],
        cost_estimate=SMALL,
        compiler_params=pltpu.CompilerParams(vmem_limit_bytes=GRANT),
    )(where, zero, *zero_far, weight_row, nug[:, :NB])
    corner, below, above = lax.optimization_barrier((corner, below, above))
    cols_far = (below, above, lax.ppermute(below[: NB // 2], "row", up), lax.ppermute(above[NB // 2 :], "row", down))
    scaled, norms_c, q_panel = pl.pallas_call(
        column_kernel,
        out_shape=(shape((2 * NB, features), bf16), shape((1, 2 * NB), f32), shape((3 * NB, 2 * NB), bf16)),
        in_specs=[SMEM] + [HBM] * 5 + [VMEM, HBM] + [VMEM] * 2,
        out_specs=(VMEM,) * 3,
        scratch_shapes=[pltpu.VMEM((2 * NB, features), bf16), pltpu.VMEM((NB, features), bf16),
                        pltpu.SemaphoreType.DMA((11,))],
        cost_estimate=SMALL,
        compiler_params=pltpu.CompilerParams(vmem_limit_bytes=GRANT),
    )(where, cols, *cols_far, weight_row, scaled0, norms0, inverse)

    fixed = (scaled0, scaled, jnp.concatenate([norms0, norms_c], axis=1), nug, inverse3, q_panel, corner)

    def whole(value):
        return pl.BlockSpec(value.shape, lambda i, _: (0, 0), pipeline_mode=pl.Buffered(1))

    rows_data = gathered.reshape(row_tiles * NB, features)
    tiles = 2
    out = pl.pallas_call(
        functools.partial(main_kernel, tiles, 4),
        out_shape=shape((row_tiles * NB * 4, 128), f32),
        grid_spec=pltpu.PrefetchScalarGridSpec(
            num_scalar_prefetch=1,
            grid=(row_tiles // tiles,),
            in_specs=[
                pl.BlockSpec((tiles * NB, features), lambda i, _: (i, 0)),
                pl.BlockSpec((tiles * NB, 1), lambda i, _: (i, 0)),
            ] + [whole(v) for v in fixed],
            out_specs=pl.BlockSpec((tiles * NB * 4, 128), lambda i, _: (i, 0)),
        ),
        compiler_params=pltpu.CompilerParams(vmem_limit_bytes=GRANT),
        cost_estimate=pl.CostEstimate(flops=30 * 10**9, bytes_accessed=48 * 2**20, transcendentals=0),
    )(where, rows_data, norms, *fixed)
    return out.reshape(row_tiles, 1, NB, 2, 1, NB)


def solution(mesh):
    placed = (P(None, "row", "col", None, None), P(), P(None, "row", "col", None))
    return jax.shard_map(
        local,
        mesh=mesh,
        in_specs=placed,
        out_specs=P(None, "row", None, None, "col", None),
        check_vma=False,
    )
```

time: 228 us -> 211 us (0.925)
  waiting for transfers between devices: 61.4 us -> 45.4 us
  Pallas kernels: 64.4 us -> 76.4 us
  other arithmetic: 8.32 us -> 2.82 us
  local copies, waits for them, and re-layouts: 19 us -> 14.6 us
  matrix products: 3.43 us -> 0 us
  blocking collectives: 43.4 us -> 41 us
    ppermute x4 -> x8, waiting for transfers between devices: 44.6 us -> 28.7 us  [the longest x1 11.4 us: local(): lax.ppermute(zero, 'row', down)]
    pallas_call x2 -> x3, Pallas kernels: 64.4 us -> 76.4 us  [the longest x1 40.2 us: local(): pl.pallas_call(functools.partial(main_kernel, tiles, 4), out_shape=shape(...]
    reduce_sum x1 -> x0, other arithmetic: 3.72 us -> none  [local(): w_norms = jnp.sum(w_wide * w_wide * ard_weight, axis=1)]
    dot_general x2 -> x0, matrix products: 3.43 us -> none  [the longest x1 1.86 us: local(): lax.dot_general(w_raw, w_scaled[:NB], NT, preferred_element_type=jnp.floa...]
    dynamic_update_slice x3 -> x0, local copies, waits for them, and re-layouts: 3.43 us -> none  [local(): w_raw = lax.dynamic_update_slice(w_raw, value, (0, at))]
    all_to_all x1, blocking collectives: 43.4 us -> 41 us  [local(): lax.all_to_all(jnp.concatenate([body[:, 0], body[:, 1], first, tail], axi...]
    ppermute x4 -> x8, starting transfers between devices: 6.53 us -> 8.51 us  [the longest x1 2.16 us: local(): lax.ppermute(above[NB // 2:], 'row', down)]
  transfers between devices with their start and end apart: 6 -> 10, of which waited for: 4 -> 6; matrix products, arithmetic and copies ran while one was open for 13% -> 8% of each run, Pallas kernels for 11% -> 17%
where the time goes in v3:
time: 211 us; the launch traced here: 208 us
  Pallas kernels  76.4 us (36%)
  waiting for transfers between devices  45.4 us (22%)
  blocking collectives  41 us (19%)
  local copies, waits for them, and re-layouts  14.6 us (7%)
  starting transfers between devices  13.9 us (7%)
  between operations  13.7 us (6%)
  other arithmetic  2.82 us (1%)
    all_to_all x1, blocking collectives, local(): lax.all_to_all(jnp.concatenate([body[:, 0], body[:, 1], first, tail], axi...  41 us
    pallas_call x1, Pallas kernels, local(): pl.pallas_call(functools.partial(main_kernel, tiles, 4), out_shape=shape(...  40.2 us
    pallas_call x1, Pallas kernels, local(): pl.pallas_call(corner_kernel, out_shape=(shape((NB, features), bf16), sha...  27.8 us
    all_to_all x1, waiting for transfers between devices, local(): sent = lax.all_to_all(jnp.concatenate([cut, extra], axis=3), 'row', 0, 0)  15.9 us
    ppermute x1, waiting for transfers between devices, local(): lax.ppermute(zero, 'row', down)  11.4 us
    pallas_call x1, Pallas kernels, local(): pl.pallas_call(column_kernel, out_shape=(shape((2 * NB, features), bf16),...  8.4 us
    ppermute x1, waiting for transfers between devices, local(): lax.ppermute(above[NB // 2:], 'row', down)  6.8 us
    all_to_all x1, starting transfers between devices, local(): sent = lax.all_to_all(jnp.concatenate([cut, extra], axis=3), 'row', 0, 0)  5.39 us
  transfers between devices with their start and end apart: 10, of which 6 were waited for; matrix products, arithmetic and copies ran while one was open for 8% of the time, Pallas kernels for 17%

profile of v3, /device:TPU:0, one launch (start us, length us, event | category | flops | bytes accessed | tf_op | source)
XLA Modules:
  0.0 207.8 jit_solution(8735012395268381882)
XLA Ops:
  6.5 0.0 all-gather.2.cloned.1.call-start
  6.5 0.7 all-gather.2.cloned.1.call-update
  7.3 1.9 reshape_reshape.3
  9.1 0.0 copy-done.11
  9.1 0.1 copy.52
  9.2 0.2 broadcast_in_dim.36
  9.4 0.6 pad_maximum_fusion
  10.0 0.0 copy-start
  10.0 0.0 copy-start.8
  10.0 1.1 copy.53
  11.2 5.4 %all-to-all-start = ((bf16[4,16,8,1152]{3,2,1,0:T(8,128)(2,1)}), bf16[4,16,8,1152]{3,2,1,0:T(8,128)(2,1)S(1)}, u32[]{:S(2)}, u32[]{:S(2)}) async-start(bf16[4,16,8,1152]{3,2,1,0:T(8,128)(2,1)} %copy.53), calls=%async_computation | async-start | bytes 2359296 | tf_op jit(solution)/shard_map/all_to_all | solution.py:221
  16.5 0.0 copy-done
  16.5 0.0 copy-done.8
  16.6 0.4 fusion
  16.9 0.1 copy.56
  17.0 0.1 broadcast_in_dim.42
  17.1 15.9 %all-to-all-done = bf16[4,16,8,1152]{3,2,1,0:T(8,128)(2,1)S(1)} async-done(((bf16[4,16,8,1152]{3,2,1,0:T(8,128)(2,1)}), bf16[4,16,8,1152]{3,2,1,0:T(8,128)(2,1)S(1)}, u32[]{:S(2)}, u32[]{:S(2)}) %all-to-all-start) | async-done | bytes 1179680 | tf_op jit(solution)/shard_map/all_to_all | solution.py:221
  33.0 0.1 copy.54
  33.2 0.2 copy.55
  33.4 0.2 copy.59
  33.5 0.2 copy.58
  33.7 0.1 slice_reduce_fusion
  33.8 1.1 slice_bitcast_fusion
  34.9 0.1 broadcast_in_dim.40
  35.1 2.4 %concatenate.10 = bf16[32,8,3200]{2,1,0:T(8,128)(2,1)S(1)} concatenate(bf16[32,8,1024]{2,1,0:T(8,128)(2,1)} %get-tuple-element.38, bf16[32,8,1024]{2,1,0:T(8,128)(2,1)} %get-tuple-element.37, bf16[32,8,1024]{2,1,0:T(8,128)(2,1)S(1)} %broadcast_in_dim.38, bf16[32,8,1]{2,1,0:T(8,128)(2,1)S(1)} %broadcast_in_dim.40, bf16[32,8,1]{2,1,0:T(8,128)(2,1)S(1)} %copy.58, ...), dimensions={2} | concatenate | bytes 3276800 | tf_op jit(solution)/shard_map/concatenate | solution.py:233
  37.5 41.0 %all_to_all.10 = bf16[32,8,3200]{2,1,0:T(8,128)(2,1)S(1)} all-to-all(bf16[32,8,3200]{2,1,0:T(8,128)(2,1)S(1)} %concatenate.10), channel_id=1, replica_groups=mesh['row'=4,'col'=32] {'col'}, dimensions={0} | all-to-all | bytes 3276800 | tf_op jit(solution)/shard_map/all_to_all | solution.py:233
  78.5 0.1 slice.96.own_ref
  78.6 0.0 copy-start.2
  78.6 0.1 collective-permute-start.1
  78.7 2.0 collective-permute-start
  80.7 11.4 %collective-permute-done.1.above_ref = bf16[256,1024]{1,0:T(8,128)(2,1)S(1)} collective-permute-done((bf16[256,1024]{1,0:T(8,128)(2,1)S(1)}, bf16[256,1024]{1,0:T(8,128)(2,1)S(1)}, u32[]{:S(2)}, u32[]{:S(2)}) %collective-permute-start.1) | collective-permute-done | bytes 524320 | tf_op jit(solution)/shard_map/ppermute | solution.py:247
  92.1 1.6 collective-permute-start.3
  93.7 0.0 collective-permute-done.below_ref
  93.7 0.6 collective-permute-start.2
  94.3 4.9 %collective-permute-done.3.far1_ref = bf16[128,1024]{1,0:T(8,128)(2,1)S(1)} collective-permute-done((bf16[128,1024]{1,0:T(8,128)(2,1)S(1)}, bf16[128,1024]{1,0:T(8,128)(2,1)S(1)}, u32[]{:S(2)}, u32[]{:S(2)}) %collective-permute-start.3) | collective-permute-done | bytes 262176 | tf_op jit(solution)/shard_map/ppermute | solution.py:249
  99.3 0.0 copy-done.3
  99.3 0.0 copy-done.4
  99.3 0.7 copy-done.7
  100.0 2.2 %collective-permute-done.2.far0_ref = bf16[128,1024]{1,0:T(8,128)(2,1)} collective-permute-done((bf16[128,1024]{1,0:T(8,128)(2,1)S(1)}, bf16[128,1024]{1,0:T(8,128)(2,1)}, u32[]{:S(2)}, u32[]{:S(2)}) %collective-permute-start.2) | collective-permute-done | bytes 262176 | tf_op jit(solution)/shard_map/ppermute | solution.py:248
  102.2 0.1 slice.81.own_ref
  102.3 0.0 copy-start.1
  102.3 0.9 collective-permute-start.5
  103.2 1.2 collective-permute-start.4
  104.4 0.6 pad_add_fusion.where_ref
  105.0 0.1 copy.61
  105.1 0.6 slice.100.nug_ref
  105.7 27.8 %shard_map.37 = (bf16[256,4096]{1,0:T(8,128)(2,1)}, f32[1,256]{1,0:T(1,128)}, f32[256,256]{1,0:T(8,128)}, f32[256,256]{1,0:T(8,128)}, bf16[768,256]{1,0:T(8,128)(2,1)}) custom-call(s32[2]{0:T(128)} %pad_add_fusion.where_ref, bf16[256,1024]{1,0:T(8,128)(2,1)} %copy-done.2, bf16[256,1024]{1,0:T(8,128)(2,1)} %copy-done.4, bf16[256,1024]{1,0:T(8,128)(2,1)} %copy-done.3, ...), custom_call_target="tpu_custom_call" | custom-call | flops 1 | bytes 1 | tf_op jit(solution)/shard_map/pallas_call | solution.py:253
  133.6 0.0 collective-permute-done.5.above_ref
  133.6 0.0 collective-permute-done.4.below_ref
  133.6 1.1 slice.82
  134.7 1.1 slice.83
  135.8 0.0 copy-done.1
  135.8 0.0 copy-done.9
  135.8 2.2 %collective-permute-start.7 = (bf16[128,2048]{1,0:T(8,128)(2,1)S(1)}, bf16[128,2048]{1,0:T(8,128)(2,1)S(1)}, u32[]{:S(2)}, u32[]{:S(2)}) collective-permute-start(bf16[128,2048]{1,0:T(8,128)(2,1)S(1)} %slice.83), channel_id=1, source_target_pairs={{0,96},{32,0},{64,32},{96,64},{1,97},{33,1},{65,33},{97,65},{2,98}... | collective-permute-start | bytes 1572872 | tf_op jit(solution)/shard_map/ppermute | solution.py:264
  137.9 0.0 collective-permute-start.6
  137.9 0.1 slice.92
  138.0 0.1 copy.60
  138.2 2.0 copy.65
  140.2 6.8 %collective-permute-done.7.far1_ref = bf16[128,2048]{1,0:T(8,128)(2,1)S(1)} collective-permute-done((bf16[128,2048]{1,0:T(8,128)(2,1)S(1)}, bf16[128,2048]{1,0:T(8,128)(2,1)S(1)}, u32[]{:S(2)}, u32[]{:S(2)}) %collective-permute-start.7) | collective-permute-done | bytes 524320 | tf_op jit(solution)/shard_map/ppermute | solution.py:264
  147.0 3.3 %collective-permute-done.6.far0_ref = bf16[128,2048]{1,0:T(8,128)(2,1)S(1)} collective-permute-done((bf16[128,2048]{1,0:T(8,128)(2,1)S(1)}, bf16[128,2048]{1,0:T(8,128)(2,1)S(1)}, u32[]{:S(2)}, u32[]{:S(2)}) %collective-permute-start.6) | collective-permute-done | bytes 524320 | tf_op jit(solution)/shard_map/ppermute | solution.py:264
  150.3 0.8 copy-done.6
  151.1 8.4 %shard_map.38 = (bf16[512,4096]{1,0:T(8,128)(2,1)}, f32[1,512]{1,0:T(1,128)}, bf16[768,512]{1,0:T(8,128)(2,1)}) custom-call(s32[2]{0:T(128)} %pad_add_fusion.where_ref, bf16[256,2048]{1,0:T(8,128)(2,1)} %copy-done.1, bf16[256,2048]{1,0:T(8,128)(2,1)} %collective-permute-done.4.below_ref, bf16[256,2048]{1,0:T(8,128)(2,1)} %collective-permute-done.5.above_ref, ...), custom_call_target="tpu_custom_call" | custom-call | flops 1 | bytes 1 | tf_op jit(solution)/shard_map/pallas_call | solution.py:265
  159.5 1.3 pad_maximum_fusion.1.wn_ref
  160.8 40.2 %shard_map.39 = f32[16384,128]{1,0:T(8,128)} custom-call(s32[2]{0:T(128)} %pad_add_fusion.where_ref, bf16[4096,4096]{1,0:T(8,128)(2,1)} %bitcast.71, f32[4096,1]{1,0:T(8,128)} %bitcast.60, bf16[256,4096]{1,0:T(8,128)(2,1)} %get-tuple-element.25.scaled0_ref.w0_ref, bf16[512,4096]{1,0:T(8,128)(2,1)} %get-tuple-element.32.wc_ref, ...), custom_call_target="tpu_custom_call" | custom-call | flops 30000001024 | bytes 50331648 | tf_op jit(solution)/shard_map/pallas_call | solution.py:283
  (29 shorter events, 0.2 us)
Async XLA Ops:
  6.5 2.6 %copy-start.11 = (bf16[16,1,1,8]{0,3,2,1:T(8,128)(2,1)S(1)}, bf16[16,1,1,8]{0,3,2,1:T(8,128)(2,1)}, u32[]{:S(2)}) copy-start(bf16[16,1,1,8]{0,3,2,1:T(8,128)(2,1)} %param.5) | copy-start | bytes 772
  6.5 154.2 %all-gather.2.cloned.1.call-start = ((), (), s32[]{:S(2)}) async-start(), calls=%async_computation.2 | async-start | bytes 34603008 | tf_op jit(solution)/shard_map/all_gather | solution.py:210
  10.0 6.6 %copy-start = (bf16[16,1,1,8,4096]{4,3,2,1,0:T(8,128)(2,1)S(1)}, bf16[16,1,1,8,4096]{4,3,2,1,0:T(8,128)(2,1)}, u32[]{:S(2)}) copy-start(bf16[16,1,1,8,4096]{4,3,2,1,0:T(8,128)(2,1)} %param.3) | copy-start | bytes 3145732
  10.0 6.5 %copy-start.8 = (f32[4096]{0:T(1024)S(1)}, f32[4096]{0:T(1024)}, u32[]{:S(2)}) copy-start(f32[4096]{0:T(1024)} %param.4) | copy-start | bytes 49156
  11.2 21.9 %all-to-all-start = ((bf16[4,16,8,1152]{3,2,1,0:T(8,128)(2,1)}), bf16[4,16,8,1152]{3,2,1,0:T(8,128)(2,1)S(1)}, u32[]{:S(2)}, u32[]{:S(2)}) async-start(bf16[4,16,8,1152]{3,2,1,0:T(8,128)(2,1)} %copy.53), calls=%async_computation | async-start | bytes 2359296 | tf_op jit(solution)/shard_map/all_to_all | solution.py:221
  78.6 27.2 %copy-start.2 = (bf16[256,1024]{1,0:T(8,128)(2,1)}, bf16[256,1024]{1,0:T(8,128)(2,1)S(1)}, u32[]{:S(2)}) copy-start(bf16[256,1024]{1,0:T(8,128)(2,1)S(1)} %slice.96.own_ref) | copy-start | bytes 1572868
  78.6 13.5 %collective-permute-start.1 = (bf16[256,1024]{1,0:T(8,128)(2,1)S(1)}, bf16[256,1024]{1,0:T(8,128)(2,1)S(1)}, u32[]{:S(2)}, u32[]{:S(2)}) collective-permute-start(bf16[256,1024]{1,0:T(8,128)(2,1)S(1)} %slice.96.own_ref), channel_id=1, source_target_pairs={{0,96},{32,0},{64,32},{96,64},{1,97},{33,1},{65,33},{97,65},{2,98}... | collective-permute-start | bytes 1572872 | tf_op jit(solution)/shard_map/ppermute | solution.py:247
  78.7 15.0 %collective-permute-start = (bf16[256,1024]{1,0:T(8,128)(2,1)S(1)}, bf16[256,1024]{1,0:T(8,128)(2,1)S(1)}, u32[]{:S(2)}, u32[]{:S(2)}) collective-permute-start(bf16[256,1024]{1,0:T(8,128)(2,1)S(1)} %slice.96.own_ref), channel_id=1, source_target_pairs={{0,32},{32,64},{64,96},{96,0},{1,33},{33,65},{65,97},{97,1},{2,34}... | collective-permute-start | bytes 1572872 | tf_op jit(solution)/shard_map/ppermute | solution.py:247
  92.1 7.1 %copy-start.3 = (bf16[256,1024]{1,0:T(8,128)(2,1)}, bf16[256,1024]{1,0:T(8,128)(2,1)S(1)}, u32[]{:S(2)}) copy-start(bf16[256,1024]{1,0:T(8,128)(2,1)S(1)} %collective-permute-done.1.above_ref) | copy-start | bytes 1572868
  92.1 7.1 %collective-permute-start.3 = (bf16[128,1024]{1,0:T(8,128)(2,1)S(1)}, bf16[128,1024]{1,0:T(8,128)(2,1)S(1)}, u32[]{:S(2)}, u32[]{:S(2)}) collective-permute-start(bf16[128,1024]{1,0:T(8,128)(2,1)S(1)} %slice.98), channel_id=1, source_target_pairs={{0,96},{32,0},{64,32},{96,64},{1,97},{33,1},{65,33},{97,65},{2,98}... | collective-permute-start | bytes 786440 | tf_op jit(solution)/shard_map/ppermute | solution.py:249
  93.7 5.6 %copy-start.4 = (bf16[256,1024]{1,0:T(8,128)(2,1)}, bf16[256,1024]{1,0:T(8,128)(2,1)S(1)}, u32[]{:S(2)}) copy-start(bf16[256,1024]{1,0:T(8,128)(2,1)S(1)} %collective-permute-done.below_ref) | copy-start | bytes 1572868
  93.7 8.5 %collective-permute-start.2 = (bf16[128,1024]{1,0:T(8,128)(2,1)S(1)}, bf16[128,1024]{1,0:T(8,128)(2,1)}, u32[]{:S(2)}, u32[]{:S(2)}) collective-permute-start(bf16[128,1024]{1,0:T(8,128)(2,1)S(1)} %slice.97), channel_id=1, source_target_pairs={{0,32},{32,64},{64,96},{96,0},{1,33},{33,65},{65,97},{97,1},{2,34}... | collective-permute-start | bytes 786440 | tf_op jit(solution)/shard_map/ppermute | solution.py:248
  99.3 0.7 copy-start.7
  102.3 33.4 %copy-start.1 = (bf16[256,2048]{1,0:T(8,128)(2,1)}, bf16[256,2048]{1,0:T(8,128)(2,1)S(1)}, u32[]{:S(2)}) copy-start(bf16[256,2048]{1,0:T(8,128)(2,1)S(1)} %slice.81.own_ref) | copy-start | bytes 3145732
  102.3 31.2 %collective-permute-start.5 = (bf16[256,2048]{1,0:T(8,128)(2,1)S(1)}, bf16[256,2048]{1,0:T(8,128)(2,1)}, u32[]{:S(2)}, u32[]{:S(2)}) collective-permute-start(bf16[256,2048]{1,0:T(8,128)(2,1)S(1)} %slice.81.own_ref), channel_id=1, source_target_pairs={{0,96},{32,0},{64,32},{96,64},{1,97},{33,1},{65,33},{97,65},{2,98}... | collective-permute-start | bytes 3145736 | tf_op jit(solution)/shard_map/ppermute | solution.py:252
  103.2 30.4 %collective-permute-start.4 = (bf16[256,2048]{1,0:T(8,128)(2,1)S(1)}, bf16[256,2048]{1,0:T(8,128)(2,1)}, u32[]{:S(2)}, u32[]{:S(2)}) collective-permute-start(bf16[256,2048]{1,0:T(8,128)(2,1)S(1)} %slice.81.own_ref), channel_id=1, source_target_pairs={{0,32},{32,64},{64,96},{96,0},{1,33},{33,65},{65,97},{97,1},{2,34}... | collective-permute-start | bytes 3145736 | tf_op jit(solution)/shard_map/ppermute | solution.py:252
  105.1 30.6 %copy-start.9 = (f32[1,1,3,256]{3,1,2,0:T(1,128)}, f32[1,1,3,256]{3,1,2,0:T(1,128)S(1)}, u32[]{:S(2)}) copy-start(f32[1,1,3,256]{3,1,2,0:T(1,128)S(1)} %copy.66) | copy-start | bytes 9220
  135.8 11.2 %collective-permute-start.7 = (bf16[128,2048]{1,0:T(8,128)(2,1)S(1)}, bf16[128,2048]{1,0:T(8,128)(2,1)S(1)}, u32[]{:S(2)}, u32[]{:S(2)}) collective-permute-start(bf16[128,2048]{1,0:T(8,128)(2,1)S(1)} %slice.83), channel_id=1, source_target_pairs={{0,96},{32,0},{64,32},{96,64},{1,97},{33,1},{65,33},{97,65},{2,98}... | collective-permute-start | bytes 1572872 | tf_op jit(solution)/shard_map/ppermute | solution.py:264
  137.9 12.4 %collective-permute-start.6 = (bf16[128,2048]{1,0:T(8,128)(2,1)S(1)}, bf16[128,2048]{1,0:T(8,128)(2,1)S(1)}, u32[]{:S(2)}, u32[]{:S(2)}) collective-permute-start(bf16[128,2048]{1,0:T(8,128)(2,1)S(1)} %slice.82), channel_id=1, source_target_pairs={{0,32},{32,64},{64,96},{96,0},{1,33},{33,65},{65,97},{97,1},{2,34}... | collective-permute-start | bytes 1572872 | tf_op jit(solution)/shard_map/ppermute | solution.py:264
  147.0 3.3 %copy-start.5 = (bf16[128,2048]{1,0:T(8,128)(2,1)}, bf16[128,2048]{1,0:T(8,128)(2,1)S(1)}, u32[]{:S(2)}) copy-start(bf16[128,2048]{1,0:T(8,128)(2,1)S(1)} %collective-permute-done.7.far1_ref) | copy-start | bytes 1572868
  150.3 0.8 copy-start.6
  151.1 8.4 %copy-start.10 = (f32[1,256]{1,0:T(1,128)S(1)}, f32[1,256]{1,0:T(1,128)}, u32[]{:S(2)}) copy-start(f32[1,256]{1,0:T(1,128)} %get-tuple-element.30.norm0_ref) | copy-start | bytes 3076
Sparse Core Ops, SparseCore 0:
  9.7 126.9 all-gather.1

commit v4 on v3

--- a/solution.py
+++ b/solution.py
@@ -11,6 +11,7 @@
 HIGH = lax.Precision.HIGHEST
 NT = (((1,), (1,)), ((), ()))
 NN = (((1,), (0,)), ((), ()))
+RING = (0, 3, 1, 2)
 GRANT = 62 * 2**20
 SMALL = pl.CostEstimate(flops=1, bytes_accessed=1, transcendentals=0)
 VMEM = pl.BlockSpec(memory_space=pltpu.VMEM)
@@ -103,17 +104,17 @@
         copy.wait()
 
 
-def corner_kernel(where_ref, own_ref, below_ref, above_ref, far0_ref, far1_ref, weight_ref, nug_ref,
+def corner_kernel(where_ref, mine_ref, theirs_ref, weight_ref, nug_ref,
                   scaled_ref, norm_ref, l_ref, x_ref, x3_ref, raw_ref, a_ref, sem):
-    quarter = own_ref.shape[1]
-    own, below, above, far = spots(where_ref, quarter)
-    bring(sem, (
-        (own_ref, raw_ref.at[:, pl.ds(own, quarter)]),
-        (below_ref, raw_ref.at[:, pl.ds(below, quarter)]),
-        (above_ref, raw_ref.at[:, pl.ds(above, quarter)]),
-        (far0_ref, raw_ref.at[: NB // 2, pl.ds(far, quarter)]),
-        (far1_ref, raw_ref.at[NB // 2 :, pl.ds(far, quarter)]),
-    ))
+    lines, half = mine_ref.shape[1:]
+    quarter = half // 2
+    core = lax.rem(where_ref[1], 2)
+    pairs = []
+    for n in range(mine_ref.shape[0]):
+        rows = pl.ds(pl.multiple_of(where_ref[2 + n] * lines, lines), lines)
+        pairs.append((mine_ref.at[n], raw_ref.at[rows, pl.ds(pl.multiple_of(core * half, half), half)]))
+        pairs.append((theirs_ref.at[n], raw_ref.at[rows, pl.ds(pl.multiple_of((1 - core) * half, half), half)]))
+    bring(sem, pairs)
     norms = jnp.zeros((NB, 1), jnp.float32)
     cross = jnp.zeros((NB, NB), jnp.float32)
     for j in range(4):
@@ -194,6 +195,18 @@
                 o_ref[pl.ds(n * NB * 4 + 2 * u + half, NB, stride=4), :] = result[:, 128 * half : 128 * (half + 1)]
 
 
+def x_move(step):
+    return [(y * 8 + x * 2 + k, y * 8 + (x + step) % 4 * 2 + k) for y in range(4) for x in range(4) for k in range(2)]
+
+
+def y_move(step):
+    return [(y * 8 + x * 2 + k, (y + step) % 4 * 8 + x * 2 + k) for y in range(4) for x in range(4) for k in range(2)]
+
+
+def ring_join(value, moves):
+    return jnp.concatenate([value] + [lax.ppermute(value, "col", moves(step)) for step in (1, -1, 2)], axis=0)
+
+
 def local(samples, ard_weight, nugget):
     row_count = lax.axis_size("row")
     col_count = lax.axis_size("col")
@@ -218,9 +231,23 @@
 
     cut = own.reshape(row_tiles, sub, row_count, quarter).transpose(2, 0, 1, 3)
     extra = jnp.broadcast_to(nugget.reshape(1, row_tiles, sub, 1), (row_count, row_tiles, sub, 128))
-    sent = lax.all_to_all(jnp.concatenate([cut, extra], axis=3), "row", 0, 0)
-    sent = sent.reshape(row_count, 2, fold, sub, quarter + 128).transpose(2, 0, 1, 3, 4)
+    share = features // row_tiles
+    zero = own[0].reshape(sub, row_tiles, share).transpose(1, 0, 2)
+    zero = jnp.broadcast_to(zero[None], (row_count, row_tiles, sub, share))
+    sent = lax.all_to_all(jnp.concatenate([cut, extra, zero], axis=3), "row", 0, 0)
+    zero = sent[0, :, :, quarter + 128 :].transpose(1, 0, 2).reshape(sub, features)
+    sent = sent[..., : quarter + 128].reshape(row_count, 2, fold, sub, quarter + 128).transpose(2, 0, 1, 3, 4)
     sent = sent.reshape(col_count, 2, sub, quarter + 128)
+
+    core = col_index % 2
+    chip_x, chip_y = col_index // 2 % 4, col_index // 8
+    sibling = [(i, i ^ 1) for i in range(col_count)]
+    left, right = zero[:, : features // 2], zero[:, features // 2 :]
+    kept = jnp.where(core == 0, left, right)
+    came = lax.ppermute(jnp.where(core == 0, right, left), "col", sibling)
+    block = jnp.where(core == 0, jnp.concatenate([kept, came]), jnp.concatenate([came, kept]))
+    mine = ring_join(ring_join(block[None], x_move), y_move)
+    theirs = lax.ppermute(mine, "col", sibling)
     body = sent[..., :quarter]
     tags = sent[..., quarter]
     tail = jnp.concatenate(
@@ -229,10 +256,9 @@
          jnp.zeros((col_count, sub, 61), bf16),
          jnp.broadcast_to(bits[None], (col_count, sub, 3 * row_tiles)),
          jnp.zeros((col_count, sub, 64 - 3 * row_tiles), bf16)], axis=2)
-    first = jnp.broadcast_to(body[0, 0][None], (col_count, sub, quarter))
-    got = lax.all_to_all(jnp.concatenate([body[:, 0], body[:, 1], first, tail], axis=2), "col", 0, 0)
+    got = lax.all_to_all(jnp.concatenate([body[:, 0], body[:, 1], tail], axis=2), "col", 0, 0)
     got = got.reshape(NB, -1)
-    tags = got[:, 3 * quarter :].astype(f32)
+    tags = got[:, 2 * quarter :].astype(f32)
     nug = tags[:, :3].T.reshape(1, 3 * NB)
     norm_bits = tags[:, 64 : 64 + 3 * row_tiles].reshape(NB, 3, row_tiles)
     norms = ((norm_bits[:, 0] + norm_bits[:, 1]) + norm_bits[:, 2]).T
@@ -240,26 +266,23 @@
     up = [(i, (i + 1) % row_count) for i in range(row_count)]
     down = [(i, (i - 1) % row_count) for i in range(row_count)]
 
-    where = jnp.stack([row_index, col_index]).astype(jnp.int32)
+    ring_of = jnp.array(RING, jnp.int32)
+    chips = lax.rem(chip_y + ring_of, 4)[:, None] * 4 + lax.rem(chip_x + ring_of, 4)[None, :]
+    where = jnp.concatenate([jnp.stack([row_index, col_index]), chips.reshape(-1)]).astype(jnp.int32)
     norms = norms.reshape(-1, 1)
 
-    zero = got[:, 2 * quarter : 3 * quarter]
-    below0, above0 = lax.ppermute(zero, "row", up), lax.ppermute(zero, "row", down)
-    zero_far = (below0, above0, lax.ppermute(below0[: NB // 2], "row", up),
-                lax.ppermute(above0[NB // 2 :], "row", down))
-    zero_far, got = lax.optimization_barrier((zero_far, got))
     cols = got[:, : 2 * quarter]
     below, above = lax.ppermute(cols, "row", up), lax.ppermute(cols, "row", down)
     scaled0, norms0, corner, inverse, inverse3 = pl.pallas_call(
         corner_kernel,
         out_shape=(shape((NB, features), bf16), shape((1, NB), f32), shape((NB, NB), f32), shape((NB, NB), f32),
                    shape((3 * NB, NB), bf16)),
-        in_specs=[SMEM] + [HBM] * 5 + [VMEM] * 2,
+        in_specs=[SMEM] + [HBM] * 2 + [VMEM] * 2,
         out_specs=(VMEM,) * 5,
-        scratch_shapes=[pltpu.VMEM((NB, features), bf16), pltpu.VMEM((NB, NB), f32), pltpu.SemaphoreType.DMA((5,))],
+        scratch_shapes=[pltpu.VMEM((NB, features), bf16), pltpu.VMEM((NB, NB), f32), pltpu.SemaphoreType.DMA((32,))],
         cost_estimate=SMALL,
         compiler_params=pltpu.CompilerParams(vmem_limit_bytes=GRANT),
-    )(where, zero, *zero_far, weight_row, nug[:, :NB])
+    )(where, mine, theirs, weight_row, nug[:, :NB])
     corner, below, above = lax.optimization_barrier((corner, below, above))
     cols_far = (below, above, lax.ppermute(below[: NB // 2], "row", up), lax.ppermute(above[NB // 2 :], "row", down))
     scaled, norms_c, q_panel = pl.pallas_call(

time: 211 us -> 203 us (0.962); the launches traced: 208 us -> 203 us
  blocking collectives: 41 us -> 0 us
  waiting for transfers between devices: 45.4 us -> 64.4 us
  starting transfers between devices: 13.9 us -> 26.9 us
    all_to_all x1 -> x0, blocking collectives: 41 us -> none  [local(): lax.all_to_all(jnp.concatenate([body[:, 0], body[:, 1], first, tail], axi...]
    ppermute x4 -> x8, waiting for transfers between devices: 18.6 us -> 32.7 us  [the longest x6 32.2 us: ring_join(): lax.ppermute(value, 'col', moves(step))]
    all_to_all x1 -> x2, starting transfers between devices: 5.39 us -> 12.2 us  [the longest x1 6.65 us: local(): lax.all_to_all(jnp.concatenate([body[:, 0], body[:, 1], tail], axis=2), '...]
    ppermute x4 -> x8, starting transfers between devices: 4.25 us -> 10.5 us  [the longest x6 10.5 us: ring_join(): lax.ppermute(value, 'col', moves(step))]
    all_to_all x1 -> x2, waiting for transfers between devices: 15.9 us -> 18.8 us  [the longest x1 18.8 us: local(): lax.all_to_all(jnp.concatenate([cut, extra, zero], axis=3), 'row', 0, 0)]
    ppermute x1, waiting for transfers between devices: 6.8 us -> 9.5 us  [local(): lax.ppermute(above[NB // 2:], 'row', down)]
    unnamed x27 -> x24, local copies, waits for them, and re-layouts: 3.57 us -> 6.18 us
  transfers between devices with their start and end apart: 10 -> 15, of which waited for: 6 -> 6; matrix products, arithmetic and copies ran while one was open for 8% -> 10% of each run, Pallas kernels for 17% -> 18%
where the time goes in v4:
time: 203 us
  Pallas kernels  77.1 us (38%)
  waiting for transfers between devices  64.4 us (32%)
  starting transfers between devices  26.9 us (13%)
  local copies, waits for them, and re-layouts  16.5 us (8%)
  between operations  13.7 us (7%)
  other arithmetic  4.22 us (2%)
    pallas_call x1, Pallas kernels, local(): pl.pallas_call(functools.partial(main_kernel, tiles, 4), out_shape=shape(...  40.2 us
    ppermute x6, waiting for transfers between devices, ring_join(): lax.ppermute(value, 'col', moves(step))  32.2 us
    pallas_call x1, Pallas kernels, local(): pl.pallas_call(corner_kernel, out_shape=(shape((NB, features), bf16), sha...  28.1 us
    all_to_all x1, waiting for transfers between devices, local(): lax.all_to_all(jnp.concatenate([cut, extra, zero], axis=3), 'row', 0, 0)  18.8 us
    ppermute x6, starting transfers between devices, ring_join(): lax.ppermute(value, 'col', moves(step))  10.5 us
    ppermute x1, waiting for transfers between devices, local(): lax.ppermute(above[NB // 2:], 'row', down)  9.5 us
    pallas_call x1, Pallas kernels, local(): pl.pallas_call(column_kernel, out_shape=(shape((2 * NB, features), bf16),...  8.73 us
    all_to_all x1, starting transfers between devices, local(): lax.all_to_all(jnp.concatenate([body[:, 0], body[:, 1], tail], axis=2), '...  6.65 us
  transfers between devices with their start and end apart: 15, of which 6 were waited for; matrix products, arithmetic and copies ran while one was open for 10% of the time, Pallas kernels for 18%

profile of v4, /device:TPU:0, one launch (start us, length us, event | category | flops | bytes accessed | tf_op | source)
XLA Modules:
  0.0 202.7 jit_solution(12913955763489853179)
XLA Ops:
  6.5 0.7 all-gather.2.cloned.1.call-update
  7.3 0.8 slice.67
  8.1 0.8 copy.50
  8.9 1.3 copy.65
  10.2 0.1 broadcast_in_dim.38
  10.3 1.2 pad_maximum_fusion
  11.5 5.5 %all-to-all-start = ((bf16[4,16,8,1408]{3,2,1,0:T(8,128)(2,1)}), bf16[4,16,8,1408]{3,2,1,0:T(8,128)(2,1)S(1)}, u32[]{:S(2)}, u32[]{:S(2)}) async-start(bf16[4,16,8,1408]{3,2,1,0:T(8,128)(2,1)} %pad_maximum_fusion), calls=%async_computation | async-start | bytes 2883584 | tf_op jit(solution)/shard_map/all_to_all | solution.py:237
  17.0 0.4 fusion
  17.4 0.1 copy.53
  17.5 0.1 broadcast_in_dim.43
  17.6 18.8 %all-to-all-done = bf16[4,16,8,1408]{3,2,1,0:T(8,128)(2,1)S(1)} async-done(((bf16[4,16,8,1408]{3,2,1,0:T(8,128)(2,1)}), bf16[4,16,8,1408]{3,2,1,0:T(8,128)(2,1)S(1)}, u32[]{:S(2)}, u32[]{:S(2)}) %all-to-all-start) | async-done | bytes 1441824 | tf_op jit(solution)/shard_map/all_to_all | solution.py:237
  36.3 0.1 slice.88
  36.4 0.1 copy.51
  36.6 0.1 collective-permute-start
  36.7 0.2 copy.52
  36.9 0.1 slice_bitcast_fusion
  37.0 0.2 copy.56
  37.2 0.2 copy.55
  37.4 0.5 collective-permute-done
  37.9 0.6 constant_dynamic-update-slice_fusion.6
  38.5 3.0 %collective-permute-start.3 = (bf16[1,16,2048]{2,1,0:T(8,128)(2,1)S(1)}, bf16[1,16,2048]{2,1,0:T(8,128)(2,1)S(1)}, u32[]{:S(2)}, u32[]{:S(2)}) collective-permute-start(bf16[1,16,2048]{2,1,0:T(8,128)(2,1)S(1)} %get-tuple-element.28), channel_id=1, source_target_pairs={{0,4},{1,5},{2,6},{3,7},{4,0},{5,1},{6,2},{7,3},{8,12},{9,13},{10,... | collective-permute-start | bytes 196616 | tf_op jit(solution)/shard_map/ppermute | solution.py:207
  41.5 1.1 collective-permute-start.2
  42.7 0.9 collective-permute-start.1
  43.6 0.1 slice_reduce_fusion
  43.7 0.1 broadcast_in_dim.41
  43.8 2.1 %concatenate.45 = bf16[32,8,2176]{2,1,0:T(8,128)(2,1)} concatenate(bf16[32,8,1024]{2,1,0:T(8,128)(2,1)S(1)} %get-tuple-element.30, bf16[32,8,1024]{2,1,0:T(8,128)(2,1)S(1)} %get-tuple-element.29, bf16[32,8,1]{2,1,0:T(8,128)(2,1)S(1)} %broadcast_in_dim.41, bf16[32,8,1]{2,1,0:T(8,128)(2,1)S(1)} %copy.55, bf16[32,8,1]{2,1,0:T(8,128)(2,1)S(1)} %copy.56, ...), dimensions={2} | concatenate | bytes 2228224 | tf_op jit(solution)/shard_map/concatenate | solution.py:259
  45.9 6.6 %all-to-all-start.1 = ((bf16[32,8,2176]{2,1,0:T(8,128)(2,1)}), bf16[32,8,2176]{2,1,0:T(8,128)(2,1)S(1)}, u32[]{:S(2)}, u32[]{:S(2)}) async-start(bf16[32,8,2176]{2,1,0:T(8,128)(2,1)} %concatenate.45), calls=%async_computation.1 | async-start | bytes 2228224 | tf_op jit(solution)/shard_map/all_to_all | solution.py:259
  52.6 0.0 collective-permute-done.2
  52.6 0.0 collective-permute-done.1
  52.7 0.0 copy-start.7
  52.7 3.4 %collective-permute-start.6 = (bf16[4,16,2048]{2,1,0:T(8,128)(2,1)S(1)}, bf16[4,16,2048]{2,1,0:T(8,128)(2,1)S(1)}, u32[]{:S(2)}, u32[]{:S(2)}) collective-permute-start(bf16[4,16,2048]{2,1,0:T(8,128)(2,1)S(1)} %pad_maximum_fusion.1), channel_id=1, source_target_pairs={{0,16},{1,17},{2,18},{3,19},{4,20},{5,21},{6,22},{7,23},{8,24},{9,... | collective-permute-start | bytes 786440 | tf_op jit(solution)/shard_map/ppermute | solution.py:207
  56.1 1.2 collective-permute-start.5
  57.2 0.9 collective-permute-start.4
  58.1 0.6 constant_dynamic-update-slice_fusion.5
  58.7 0.6 constant_dynamic-update-slice_fusion.4
  59.3 0.6 constant_dynamic-update-slice_fusion.3
  59.9 30.7 %collective-permute-done.4 = bf16[4,16,2048]{2,1,0:T(8,128)(2,1)S(1)} collective-permute-done((bf16[4,16,2048]{2,1,0:T(8,128)(2,1)S(1)}, bf16[4,16,2048]{2,1,0:T(8,128)(2,1)S(1)}, u32[]{:S(2)}, u32[]{:S(2)}) %collective-permute-start.4) | collective-permute-done | bytes 262176 | tf_op jit(solution)/shard_map/ppermute | solution.py:207
  90.7 0.7 constant_dynamic-update-slice_fusion.2
  91.4 1.5 collective-permute-done.5
  92.8 0.7 constant_dynamic-update-slice_fusion.1
  93.6 0.7 constant_dynamic-update-slice_fusion.mine_ref
  94.3 0.1 slice.105.own_ref
  94.4 0.0 copy-start.1
  94.4 0.1 collective-permute-start.9
  94.5 2.0 collective-permute-start.8
  96.5 0.1 broadcast_add_fusion
  96.6 0.1 add.56
  96.7 0.6 pad_add_fusion.where_ref
  97.3 0.1 copy.58
  97.4 0.5 slice.104.nug_ref
  98.0 28.1 %shard_map.46 = (bf16[256,4096]{1,0:T(8,128)(2,1)}, f32[1,256]{1,0:T(1,128)}, f32[256,256]{1,0:T(8,128)}, f32[256,256]{1,0:T(8,128)}, bf16[768,256]{1,0:T(8,128)(2,1)}) custom-call(s32[18]{0:T(128)} %pad_add_fusion.where_ref, bf16[16,16,2048]{2,1,0:T(8,128)(2,1)} %constant_dynamic-update-slice_fusion.mine_ref, ...), custom_call_target="tpu_custom_call" | custom-call | flops 1 | bytes 1 | tf_op jit(solution)/shard_map/pallas_call | solution.py:276
  126.1 1.1 slice.86
  127.2 1.1 slice.87
  128.4 1.5 collective-permute-start.11
  129.9 0.6 collective-permute-start.10
  130.5 0.1 slice.96
  130.6 0.1 copy.57
  130.7 2.0 %copy.62 = f32[1,4096]{0,1:T(8,128)} copy(f32[1,4096]{1,0:T(1,128)S(1)} %bitcast.75) | data formatting | bytes 32768
  132.7 9.5 %collective-permute-done.11.far1_ref = bf16[128,2048]{1,0:T(8,128)(2,1)S(1)} collective-permute-done((bf16[128,2048]{1,0:T(8,128)(2,1)S(1)}, bf16[128,2048]{1,0:T(8,128)(2,1)S(1)}, u32[]{:S(2)}, u32[]{:S(2)}) %collective-permute-start.11) | collective-permute-done | bytes 524320 | tf_op jit(solution)/shard_map/ppermute | solution.py:287
  142.2 2.7 %collective-permute-done.10.far0_ref = bf16[128,2048]{1,0:T(8,128)(2,1)S(1)} collective-permute-done((bf16[128,2048]{1,0:T(8,128)(2,1)S(1)}, bf16[128,2048]{1,0:T(8,128)(2,1)S(1)}, u32[]{:S(2)}, u32[]{:S(2)}) %collective-permute-start.10) | collective-permute-done | bytes 524320 | tf_op jit(solution)/shard_map/ppermute | solution.py:287
  144.9 0.8 copy-done.3
  145.7 8.7 %shard_map.47 = (bf16[512,4096]{1,0:T(8,128)(2,1)}, f32[1,512]{1,0:T(1,128)}, bf16[768,512]{1,0:T(8,128)(2,1)}) custom-call(s32[18]{0:T(128)} %pad_add_fusion.where_ref, bf16[256,2048]{1,0:T(8,128)(2,1)} %copy-done.1, bf16[256,2048]{1,0:T(8,128)(2,1)} %collective-permute-done.8.below_ref, bf16[256,2048]{1,0:T(8,128)(2,1)} %collective-permute-done.9.above_ref, ...), custom_call_target="tpu_custom_call" | custom-call | flops 1 | bytes 1 | tf_op jit(solution)/shard_map/pallas_call | solution.py:288
  154.4 1.3 pad_maximum_fusion.2.wn_ref
  155.7 40.2 %shard_map.48 = f32[16384,128]{1,0:T(8,128)} custom-call(s32[18]{0:T(128)} %pad_add_fusion.where_ref, bf16[4096,4096]{1,0:T(8,128)(2,1)} %bitcast.83, f32[4096,1]{1,0:T(8,128)} %bitcast.69, bf16[256,4096]{1,0:T(8,128)(2,1)} %get-tuple-element.16.scaled0_ref.w0_ref, bf16[512,4096]{1,0:T(8,128)(2,1)} %get-tuple-element.22.wc_ref, ...), custom_call_target="tpu_custom_call" | custom-call | flops 30000001024 | bytes 50331648 | tf_op jit(solution)/shard_map/pallas_call | solution.py:306
  (40 shorter events, 0.3 us)
Async XLA Ops:
  6.5 149.2 %all-gather.2.cloned.1.call-start = ((), (), s32[]{:S(2)}) async-start(), calls=%async_computation.2 | async-start | bytes 34603008 | tf_op jit(solution)/shard_map/all_gather | solution.py:223
  11.5 5.5 %copy-start = (bf16[16,1,1,8,4096]{4,3,2,1,0:T(8,128)(2,1)S(1)}, bf16[16,1,1,8,4096]{4,3,2,1,0:T(8,128)(2,1)}, u32[]{:S(2)}) copy-start(bf16[16,1,1,8,4096]{4,3,2,1,0:T(8,128)(2,1)} %param.4) | copy-start | bytes 3145732
  11.5 5.5 %copy-start.4 = (f32[4096]{0:T(1024)S(1)}, f32[4096]{0:T(1024)}, u32[]{:S(2)}) copy-start(f32[4096]{0:T(1024)} %param.5) | copy-start | bytes 49156
  11.5 24.8 %all-to-all-start = ((bf16[4,16,8,1408]{3,2,1,0:T(8,128)(2,1)}), bf16[4,16,8,1408]{3,2,1,0:T(8,128)(2,1)S(1)}, u32[]{:S(2)}, u32[]{:S(2)}) async-start(bf16[4,16,8,1408]{3,2,1,0:T(8,128)(2,1)} %pad_maximum_fusion), calls=%async_computation | async-start | bytes 2883584 | tf_op jit(solution)/shard_map/all_to_all | solution.py:237
  36.6 1.3 collective-permute-start
  38.5 14.1 %collective-permute-start.3 = (bf16[1,16,2048]{2,1,0:T(8,128)(2,1)S(1)}, bf16[1,16,2048]{2,1,0:T(8,128)(2,1)S(1)}, u32[]{:S(2)}, u32[]{:S(2)}) collective-permute-start(bf16[1,16,2048]{2,1,0:T(8,128)(2,1)S(1)} %get-tuple-element.28), channel_id=1, source_target_pairs={{0,4},{1,5},{2,6},{3,7},{4,0},{5,1},{6,2},{7,3},{8,12},{9,13},{10,... | collective-permute-start | bytes 196616 | tf_op jit(solution)/shard_map/ppermute | solution.py:207
  41.5 11.1 %collective-permute-start.2 = (bf16[1,16,2048]{2,1,0:T(8,128)(2,1)S(1)}, bf16[1,16,2048]{2,1,0:T(8,128)(2,1)S(1)}, u32[]{:S(2)}, u32[]{:S(2)}) collective-permute-start(bf16[1,16,2048]{2,1,0:T(8,128)(2,1)S(1)} %get-tuple-element.28), channel_id=1, source_target_pairs={{0,6},{1,7},{2,0},{3,1},{4,2},{5,3},{6,4},{7,5},{8,14},{9,15},{10,... | collective-permute-start | bytes 196616 | tf_op jit(solution)/shard_map/ppermute | solution.py:207
  42.7 9.9 %collective-permute-start.1 = (bf16[1,16,2048]{2,1,0:T(8,128)(2,1)S(1)}, bf16[1,16,2048]{2,1,0:T(8,128)(2,1)S(1)}, u32[]{:S(2)}, u32[]{:S(2)}) collective-permute-start(bf16[1,16,2048]{2,1,0:T(8,128)(2,1)S(1)} %get-tuple-element.28), channel_id=1, source_target_pairs={{0,2},{1,3},{2,4},{3,5},{4,6},{5,7},{6,0},{7,1},{8,10},{9,11},{10,... | collective-permute-start | bytes 196616 | tf_op jit(solution)/shard_map/ppermute | solution.py:207
  45.9 48.4 %all-to-all-start.1 = ((bf16[32,8,2176]{2,1,0:T(8,128)(2,1)}), bf16[32,8,2176]{2,1,0:T(8,128)(2,1)S(1)}, u32[]{:S(2)}, u32[]{:S(2)}) async-start(bf16[32,8,2176]{2,1,0:T(8,128)(2,1)} %concatenate.45), calls=%async_computation.1 | async-start | bytes 2228224 | tf_op jit(solution)/shard_map/all_to_all | solution.py:259
  52.7 43.9 %copy-start.7 = (s32[4]{0:T(128)S(1)}, s32[4]{0:T(128)}, u32[]{:S(2)}) copy-start(s32[4]{0:T(128)} %constant.67.clone) | copy-start | bytes 52
  52.7 40.9 %collective-permute-start.6 = (bf16[4,16,2048]{2,1,0:T(8,128)(2,1)S(1)}, bf16[4,16,2048]{2,1,0:T(8,128)(2,1)S(1)}, u32[]{:S(2)}, u32[]{:S(2)}) collective-permute-start(bf16[4,16,2048]{2,1,0:T(8,128)(2,1)S(1)} %pad_maximum_fusion.1), channel_id=1, source_target_pairs={{0,16},{1,17},{2,18},{3,19},{4,20},{5,21},{6,22},{7,23},{8,24},{9,... | collective-permute-start | bytes 786440 | tf_op jit(solution)/shard_map/ppermute | solution.py:207
  56.1 36.8 %collective-permute-start.5 = (bf16[4,16,2048]{2,1,0:T(8,128)(2,1)S(1)}, bf16[4,16,2048]{2,1,0:T(8,128)(2,1)S(1)}, u32[]{:S(2)}, u32[]{:S(2)}) collective-permute-start(bf16[4,16,2048]{2,1,0:T(8,128)(2,1)S(1)} %pad_maximum_fusion.1), channel_id=1, source_target_pairs={{0,24},{1,25},{2,26},{3,27},{4,28},{5,29},{6,30},{7,31},{8,0},{9,1... | collective-permute-start | bytes 786440 | tf_op jit(solution)/shard_map/ppermute | solution.py:207
  57.2 33.5 %collective-permute-start.4 = (bf16[4,16,2048]{2,1,0:T(8,128)(2,1)S(1)}, bf16[4,16,2048]{2,1,0:T(8,128)(2,1)S(1)}, u32[]{:S(2)}, u32[]{:S(2)}) collective-permute-start(bf16[4,16,2048]{2,1,0:T(8,128)(2,1)S(1)} %pad_maximum_fusion.1), channel_id=1, source_target_pairs={{0,8},{1,9},{2,10},{3,11},{4,12},{5,13},{6,14},{7,15},{8,16},{9,17... | collective-permute-start | bytes 786440 | tf_op jit(solution)/shard_map/ppermute | solution.py:207
  94.3 3.7 %collective-permute-start.7 = (bf16[16,16,2048]{2,1,0:T(8,128)(2,1)}, bf16[16,16,2048]{2,1,0:T(8,128)(2,1)}, u32[]{:S(2)}, u32[]{:S(2)}) collective-permute-start(bf16[16,16,2048]{2,1,0:T(8,128)(2,1)} %constant_dynamic-update-slice_fusion.mine_ref), channel_id=1, source_target_pairs={{0,1},{1,0},{2,3},{3,2},{4,5},{5,4},{6,7},{7,6},{8,9},{9,8},{10,11... | collective-permute-start | bytes 3145736 | tf_op jit(solution)/shard_map/ppermute | solution.py:250
  94.4 33.9 %copy-start.1 = (bf16[256,2048]{1,0:T(8,128)(2,1)}, bf16[256,2048]{1,0:T(8,128)(2,1)S(1)}, u32[]{:S(2)}) copy-start(bf16[256,2048]{1,0:T(8,128)(2,1)S(1)} %slice.105.own_ref) | copy-start | bytes 3145732
  94.4 31.7 %collective-permute-start.9 = (bf16[256,2048]{1,0:T(8,128)(2,1)S(1)}, bf16[256,2048]{1,0:T(8,128)(2,1)}, u32[]{:S(2)}, u32[]{:S(2)}) collective-permute-start(bf16[256,2048]{1,0:T(8,128)(2,1)S(1)} %slice.105.own_ref), channel_id=1, source_target_pairs={{0,96},{32,0},{64,32},{96,64},{1,97},{33,1},{65,33},{97,65},{2,98}... | collective-permute-start | bytes 3145736 | tf_op jit(solution)/shard_map/ppermute | solution.py:275
  94.5 31.6 %collective-permute-start.8 = (bf16[256,2048]{1,0:T(8,128)(2,1)S(1)}, bf16[256,2048]{1,0:T(8,128)(2,1)}, u32[]{:S(2)}, u32[]{:S(2)}) collective-permute-start(bf16[256,2048]{1,0:T(8,128)(2,1)S(1)} %slice.105.own_ref), channel_id=1, source_target_pairs={{0,32},{32,64},{64,96},{96,0},{1,33},{33,65},{65,97},{97,1},{2,34}... | collective-permute-start | bytes 3145736 | tf_op jit(solution)/shard_map/ppermute | solution.py:275
  97.4 30.9 %copy-start.5 = (f32[1,1,3,256]{3,1,2,0:T(1,128)}, f32[1,1,3,256]{3,1,2,0:T(1,128)S(1)}, u32[]{:S(2)}) copy-start(f32[1,1,3,256]{3,1,2,0:T(1,128)S(1)} %copy.63) | copy-start | bytes 9220
  128.4 13.8 %collective-permute-start.11 = (bf16[128,2048]{1,0:T(8,128)(2,1)S(1)}, bf16[128,2048]{1,0:T(8,128)(2,1)S(1)}, u32[]{:S(2)}, u32[]{:S(2)}) collective-permute-start(bf16[128,2048]{1,0:T(8,128)(2,1)S(1)} %slice.87), channel_id=1, source_target_pairs={{0,96},{32,0},{64,32},{96,64},{1,97},{33,1},{65,33},{97,65},{2,98}... | collective-permute-start | bytes 1572872 | tf_op jit(solution)/shard_map/ppermute | solution.py:287
  129.9 15.0 %collective-permute-start.10 = (bf16[128,2048]{1,0:T(8,128)(2,1)S(1)}, bf16[128,2048]{1,0:T(8,128)(2,1)S(1)}, u32[]{:S(2)}, u32[]{:S(2)}) collective-permute-start(bf16[128,2048]{1,0:T(8,128)(2,1)S(1)} %slice.86), channel_id=1, source_target_pairs={{0,32},{32,64},{64,96},{96,0},{1,33},{33,65},{65,97},{97,1},{2,34}... | collective-permute-start | bytes 1572872 | tf_op jit(solution)/shard_map/ppermute | solution.py:287
  142.2 2.7 %copy-start.2 = (bf16[128,2048]{1,0:T(8,128)(2,1)}, bf16[128,2048]{1,0:T(8,128)(2,1)S(1)}, u32[]{:S(2)}) copy-start(bf16[128,2048]{1,0:T(8,128)(2,1)S(1)} %collective-permute-done.11.far1_ref) | copy-start | bytes 1572868
  144.9 0.8 copy-start.3
  145.7 8.7 %copy-start.6 = (f32[1,256]{1,0:T(1,128)S(1)}, f32[1,256]{1,0:T(1,128)}, u32[]{:S(2)}) copy-start(f32[1,256]{1,0:T(1,128)} %get-tuple-element.20.norm0_ref) | copy-start | bytes 3076
Sparse Core Ops, SparseCore 0:
  9.7 140.5 all-gather.1

commit v5 on v4

--- a/solution.py
+++ b/solution.py
@@ -42,24 +42,38 @@
     height = 32
     rows = lax.broadcasted_iota(jnp.int32, (size, size), 0)
     cols = lax.broadcasted_iota(jnp.int32, (size, size), 1)
+    parts = [block[g * height : (g + 1) * height] for g in range(size // height)]
+    inner = lax.broadcasted_iota(jnp.int32, (height, 1), 0)
+    lane = lax.broadcasted_iota(jnp.int32, (1, size), 1)
+
+    def spread(value):
+        return jnp.broadcast_to(value, (value.shape[0], size))
+
+    for j in range(0, size, 2):
+        first, at = divmod(j, height)
+        row0 = parts[first][at : at + 1, :]
+        row1 = parts[first][at + 1 : at + 2, :]
+        a, b = spread(row0[:, j : j + 1]), spread(row0[:, j + 1 : j + 2])
+        c, d = spread(row1[:, j : j + 1]), spread(row1[:, j + 1 : j + 2])
+        inverse = 1.0 / a
+        scale, ratio = c * inverse, b * inverse
+        row0 = row0 + (lane == j).astype(jnp.float32)
+        row1 = row1 - scale * row0 + (lane == j + 1).astype(jnp.float32)
+        row1 = row1 * (1.0 / (d - scale * b))
+        row0 = row0 * inverse
+        for g in range(first, size // height):
+            left = spread(parts[g][:, j : j + 1])
+            right = spread(parts[g][:, j + 1 : j + 2]) - left * ratio
+            if g == first:
+                left = jnp.where(inner > at, left, 0.0)
+                right = jnp.where(inner > at + 1, right, 0.0)
+            parts[g] = parts[g] - left * row0 - right * row1
+    whole = jnp.concatenate(parts, axis=0)
     eye = (rows == cols).astype(jnp.float32)
-    whole = jnp.concatenate([block, eye], axis=1)
-    parts = [whole[g * height : (g + 1) * height] for g in range(size // height)]
-    inner = lax.broadcasted_iota(jnp.int32, (height, 1), 0)
-    for j in range(size):
-        first, at = divmod(j, height)
-        pivot_row = parts[first][at : at + 1, :]
-        pivot_row = pivot_row * (1.0 / pivot_row[:, j : j + 1])
-        for g in range(first, size // height):
-            factor = parts[g][:, j : j + 1]
-            if g == first:
-                factor = jnp.where(inner > at, factor, 0.0)
-            parts[g] = parts[g] - factor * pivot_row
-    whole = jnp.concatenate(parts, axis=0)
-    pivots = jnp.sum(whole[:, :size] * eye, axis=1, keepdims=True)
+    pivots = jnp.sum(whole * eye, axis=1, keepdims=True)
     root = lax.rsqrt(pivots)
     root = root * (1.5 - 0.5 * pivots * root * root)
-    return whole[:, size:] * root
+    return jnp.where(rows > cols, whole, eye) * root
 
 
 def store_factor(a_ref, l_ref, x_ref):
@@ -135,34 +149,50 @@
     store_triple(x3_ref, x_ref[...].T)
 
 
-def column_kernel(where_ref, own_ref, below_ref, above_ref, far0_ref, far1_ref, weight_ref, scaled0_ref, norm0_ref,
-                  x_ref, scaled_ref, norm_ref, q_ref, raw_ref, zero_ref, sem):
+def column_kernel(where_ref, own_ref, below_ref, above_ref, weight_ref, scaled0_ref,
+                  scaled_ref, norm_ref, cross_ref, raw_ref, zero_ref, sem):
     quarter = own_ref.shape[1] // 2
-    own, below, above, far = spots(where_ref, quarter)
     pairs = [(scaled0_ref, zero_ref)]
-    for u in range(2):
-        rows = slice(u * NB, (u + 1) * NB)
-        part = slice(u * quarter, (u + 1) * quarter)
-        pairs += [
-            (own_ref.at[:, part], raw_ref.at[rows, pl.ds(own, quarter)]),
-            (below_ref.at[:, part], raw_ref.at[rows, pl.ds(below, quarter)]),
-            (above_ref.at[:, part], raw_ref.at[rows, pl.ds(above, quarter)]),
-            (far0_ref.at[:, part], raw_ref.at[u * NB : u * NB + NB // 2, pl.ds(far, quarter)]),
-            (far1_ref.at[:, part], raw_ref.at[u * NB + NB // 2 : (u + 1) * NB, pl.ds(far, quarter)]),
-        ]
+    for n, ref in enumerate((own_ref, below_ref, above_ref)):
+        for u in range(2):
+            pairs.append((ref.at[:, u * quarter : (u + 1) * quarter], raw_ref.at[n, u * NB : (u + 1) * NB]))
     bring(sem, pairs)
     norms = jnp.zeros((2 * NB, 1), jnp.float32)
     cross = jnp.zeros((2 * NB, NB), jnp.float32)
-    for j in range(4):
-        part = slice(j * quarter, (j + 1) * quarter)
-        raw = raw_ref[:, part]
+    for n, spot in enumerate(spots(where_ref, quarter)[:3]):
+        weight = weight_ref[:, pl.ds(spot, quarter)]
+        raw = raw_ref[n]
         wide = raw.astype(jnp.float32)
-        scaled_ref[:, part] = (wide * weight_ref[:, part]).astype(jnp.bfloat16)
-        norms += jnp.sum(wide * wide * weight_ref[:, part], axis=1, keepdims=True)
-        cross += dot_fast(raw, zero_ref[:, part], NT)
-    norm_ref[...] = as_row(norms)
+        scaled_ref[:, pl.ds(spot, quarter)] = (wide * weight).astype(jnp.bfloat16)
+        norms += jnp.sum(wide * wide * weight, axis=1, keepdims=True)
+        cross += dot_fast(raw, zero_ref[:, pl.ds(spot, quarter)], NT)
+    norm_ref[...] = norms
+    cross_ref[...] = cross
+
+
+def far_kernel(where_ref, far0_ref, far1_ref, weight_ref, scaled0_ref, norm0_ref, x_ref, part_norm_ref, part_cross_ref,
+               before_ref, scaled_ref, norm_ref, q_ref, raw_ref, zero_ref, out_ref, sem):
+    quarter = far0_ref.shape[1] // 2
+    spot = spots(where_ref, quarter)[3]
+    pairs = [(scaled0_ref.at[:, pl.ds(spot, quarter)], zero_ref)]
+    for u in range(2):
+        part = slice(u * quarter, (u + 1) * quarter)
+        pairs.append((far0_ref.at[:, part], raw_ref.at[u * NB : u * NB + NB // 2]))
+        pairs.append((far1_ref.at[:, part], raw_ref.at[u * NB + NB // 2 : (u + 1) * NB]))
+    bring(sem, pairs)
+    weight = weight_ref[:, pl.ds(spot, quarter)]
+    raw = raw_ref[...]
+    wide = raw.astype(jnp.float32)
+    out_ref[...] = (wide * weight).astype(jnp.bfloat16)
+    back = pltpu.make_async_copy(out_ref, scaled_ref.at[:, pl.ds(spot, quarter)], sem.at[0])
+    back.start()
+    norms = part_norm_ref[...] + jnp.sum(wide * wide * weight, axis=1, keepdims=True)
+    cross = part_cross_ref[...] + dot_fast(raw, zero_ref[...], NT)
+    norm_ref[:, :NB] = norm0_ref[...]
+    norm_ref[:, NB:] = as_row(norms)
     kern = jnp.exp(-0.5 * (norms + norm0_ref[...] - 2.0 * cross))
     store_triple(q_ref, dot_high(x_ref[...], kern, NT))
+    back.wait()
 
 
 def main_kernel(tiles, rows_dev, where_ref, rows_ref, norm_ref, w0_ref, wc_ref, wn_ref, nug_ref, inv_ref, q_ref, l_ref, o_ref):
@@ -246,7 +276,10 @@
     kept = jnp.where(core == 0, left, right)
     came = lax.ppermute(jnp.where(core == 0, right, left), "col", sibling)
     block = jnp.where(core == 0, jnp.concatenate([kept, came]), jnp.concatenate([came, kept]))
-    mine = ring_join(ring_join(block[None], x_move), y_move)
+    line = ring_join(block[None], x_move)
+    below, above = lax.ppermute(line, "col", y_move(1)), lax.ppermute(line, "col", y_move(-1))
+    mine = jnp.concatenate(
+        [line, below, above, lax.ppermute(below[:2], "col", y_move(1)), lax.ppermute(above[2:], "col", y_move(-1))])
     theirs = lax.ppermute(mine, "col", sibling)
     body = sent[..., :quarter]
     tags = sent[..., quarter]
@@ -284,19 +317,32 @@
         compiler_params=pltpu.CompilerParams(vmem_limit_bytes=GRANT),
     )(where, mine, theirs, weight_row, nug[:, :NB])
     corner, below, above = lax.optimization_barrier((corner, below, above))
-    cols_far = (below, above, lax.ppermute(below[: NB // 2], "row", up), lax.ppermute(above[NB // 2 :], "row", down))
-    scaled, norms_c, q_panel = pl.pallas_call(
+    cols_far = (lax.ppermute(below[: NB // 2], "row", up), lax.ppermute(above[NB // 2 :], "row", down))
+    limit = pltpu.CompilerParams(vmem_limit_bytes=GRANT)
+    near = shape((2 * NB, features), bf16)
+    scaled, norms_c, cross_c = pl.pallas_call(
         column_kernel,
-        out_shape=(shape((2 * NB, features), bf16), shape((1, 2 * NB), f32), shape((3 * NB, 2 * NB), bf16)),
-        in_specs=[SMEM] + [HBM] * 5 + [VMEM, HBM] + [VMEM] * 2,
+        out_shape=(near, shape((2 * NB, 1), f32), shape((2 * NB, NB), f32)),
+        in_specs=[SMEM] + [HBM] * 3 + [VMEM, HBM],
         out_specs=(VMEM,) * 3,
-        scratch_shapes=[pltpu.VMEM((2 * NB, features), bf16), pltpu.VMEM((NB, features), bf16),
-                        pltpu.SemaphoreType.DMA((11,))],
+        scratch_shapes=[pltpu.VMEM((3, 2 * NB, quarter), bf16), pltpu.VMEM((NB, features), bf16),
+                        pltpu.SemaphoreType.DMA((7,))],
         cost_estimate=SMALL,
-        compiler_params=pltpu.CompilerParams(vmem_limit_bytes=GRANT),
-    )(where, cols, *cols_far, weight_row, scaled0, norms0, inverse)
-
-    fixed = (scaled0, scaled, jnp.concatenate([norms0, norms_c], axis=1), nug, inverse3, q_panel, corner)
+        compiler_params=limit,
+    )(where, cols, below, above, weight_row, scaled0)
+    scaled, wn, q_panel = pl.pallas_call(
+        far_kernel,
+        out_shape=(near, shape((1, 3 * NB), f32), shape((3 * NB, 2 * NB), bf16)),
+        in_specs=[SMEM] + [HBM] * 2 + [VMEM, HBM] + [VMEM] * 4 + [HBM],
+        out_specs=(HBM, VMEM, VMEM),
+        scratch_shapes=[pltpu.VMEM((2 * NB, quarter), bf16), pltpu.VMEM((NB, quarter), bf16),
+                        pltpu.VMEM((2 * NB, quarter), bf16), pltpu.SemaphoreType.DMA((5,))],
+        input_output_aliases={9: 0},
+        cost_estimate=SMALL,
+        compiler_params=limit,
+    )(where, *cols_far, weight_row, scaled0, norms0, inverse, norms_c, cross_c, scaled)
+
+    fixed = (scaled0, scaled, wn, nug, inverse3, q_panel, corner)
 
     def whole(value):
         return pl.BlockSpec(value.shape, lambda i, _: (0, 0), pipeline_mode=pl.Buffered(1))

time: 203 us -> 196 us (0.966)
  Pallas kernels: 77.1 us -> 71.5 us
  waiting for transfers between devices: 64.4 us -> 60.9 us
  local copies, waits for them, and re-layouts: 16.5 us -> 18.7 us
    ppermute x6 -> x3, waiting for transfers between devices: 32.2 us -> 0.01 us  [ring_join(): lax.ppermute(value, 'col', moves(step))]
    ppermute x0 -> x4, waiting for transfers between devices: none -> 30.5 us  [the longest x1 24 us: local(): lax.ppermute(line, 'col', y_move(-1))]
    pallas_call x1, Pallas kernels: 28.1 us -> 19.2 us  [local(): pl.pallas_call(corner_kernel, out_shape=(shape((NB, features), bf16), sha...]
    ppermute x1, waiting for transfers between devices: 9.5 us -> 2.37 us  [local(): lax.ppermute(above[NB // 2:], 'row', down)]
    ppermute x6 -> x3, starting transfers between devices: 10.5 us -> 5.05 us  [ring_join(): lax.ppermute(value, 'col', moves(step))]
    ppermute x0 -> x4, starting transfers between devices: none -> 5.28 us  [the longest x1 3.11 us: local(): lax.ppermute(line, 'col', y_move(-1))]
    pallas_call x1 -> x2, Pallas kernels: 8.73 us -> 12.1 us  [the longest x1 6.98 us: local(): pl.pallas_call(column_kernel, out_shape=(near, shape((2 * NB, 1), f32), s...]
    ppermute x1, waiting for transfers between devices: 0.01 us -> 2.99 us  [local(): lax.ppermute(cols, 'row', down)]
  transfers between devices with their start and end apart: 15 -> 16, of which waited for: 6 -> 9; matrix products, arithmetic and copies ran while one was open for 10% -> 11% of each run, Pallas kernels for 18% -> 16%
where the time goes in v5:
time: 196 us; the launch traced here: 195 us
  Pallas kernels  71.5 us (36%)
  waiting for transfers between devices  60.9 us (31%)
  starting transfers between devices  26.7 us (14%)
  local copies, waits for them, and re-layouts  18.7 us (10%)
  between operations  13.7 us (7%)
  other arithmetic  2.97 us (2%)
    pallas_call x1, Pallas kernels, local(): pl.pallas_call(functools.partial(main_kernel, tiles, 4), out_shape=shape(...  40.2 us
    ppermute x1, waiting for transfers between devices, local(): lax.ppermute(line, 'col', y_move(-1))  24 us
    pallas_call x1, Pallas kernels, local(): pl.pallas_call(corner_kernel, out_shape=(shape((NB, features), bf16), sha...  19.2 us
    all_to_all x1, waiting for transfers between devices, local(): lax.all_to_all(jnp.concatenate([cut, extra, zero], axis=3), 'row', 0, 0)  18.8 us
    pallas_call x1, Pallas kernels, local(): pl.pallas_call(column_kernel, out_shape=(near, shape((2 * NB, 1), f32), s...  6.98 us
    unnamed x23, local copies, waits for them, and re-layouts  6.84 us
    all_to_all x1, starting transfers between devices, local(): lax.all_to_all(jnp.concatenate([body[:, 0], body[:, 1], tail], axis=2), '...  6.65 us
    ppermute x1, waiting for transfers between devices, local(): lax.ppermute(below[:2], 'col', y_move(1))  6.53 us
  transfers between devices with their start and end apart: 16, of which 9 were waited for; matrix products, arithmetic and copies ran while one was open for 11% of the time, Pallas kernels for 16%

profile of v5, /device:TPU:0, one launch (start us, length us, event | category | flops | bytes accessed | tf_op | source)
XLA Modules:
  0.0 194.5 jit_solution(2910442659485193458)
XLA Ops:
  6.5 0.7 all-gather.2.cloned.1.call-update
  7.3 0.8 slice.73
  8.1 0.8 copy.51
  8.9 1.3 copy.66
  10.2 0.1 broadcast_in_dim.38
  10.3 1.2 pad_maximum_fusion
  11.5 5.5 %all-to-all-start = ((bf16[4,16,8,1408]{3,2,1,0:T(8,128)(2,1)}), bf16[4,16,8,1408]{3,2,1,0:T(8,128)(2,1)S(1)}, u32[]{:S(2)}, u32[]{:S(2)}) async-start(bf16[4,16,8,1408]{3,2,1,0:T(8,128)(2,1)} %pad_maximum_fusion), calls=%async_computation | async-start | bytes 2883584 | tf_op jit(solution)/shard_map/all_to_all | solution.py:267
  17.0 0.4 fusion
  17.4 0.1 copy.54
  17.5 0.1 broadcast_in_dim.43
  17.6 18.8 %all-to-all-done = bf16[4,16,8,1408]{3,2,1,0:T(8,128)(2,1)S(1)} async-done(((bf16[4,16,8,1408]{3,2,1,0:T(8,128)(2,1)}), bf16[4,16,8,1408]{3,2,1,0:T(8,128)(2,1)S(1)}, u32[]{:S(2)}, u32[]{:S(2)}) %all-to-all-start) | async-done | bytes 1441824 | tf_op jit(solution)/shard_map/all_to_all | solution.py:267
  36.3 0.1 slice.96
  36.4 0.1 copy.52
  36.6 0.1 collective-permute-start
  36.7 0.2 copy.53
  36.9 0.1 slice_bitcast_fusion
  37.0 0.2 copy.57
  37.2 0.2 copy.56
  37.4 0.5 collective-permute-done
  37.9 0.6 constant_dynamic-update-slice_fusion.7
  38.5 3.0 %collective-permute-start.3 = (bf16[1,16,2048]{2,1,0:T(8,128)(2,1)S(1)}, bf16[1,16,2048]{2,1,0:T(8,128)(2,1)S(1)}, u32[]{:S(2)}, u32[]{:S(2)}) collective-permute-start(bf16[1,16,2048]{2,1,0:T(8,128)(2,1)S(1)} %get-tuple-element.34), channel_id=1, source_target_pairs={{0,4},{1,5},{2,6},{3,7},{4,0},{5,1},{6,2},{7,3},{8,12},{9,13},{10,... | collective-permute-start | bytes 196616 | tf_op jit(solution)/shard_map/ppermute | solution.py:237
  41.5 1.1 collective-permute-start.2
  42.7 0.9 collective-permute-start.1
  43.6 0.1 slice_reduce_fusion
  43.7 0.1 broadcast_in_dim.41
  43.8 2.1 %concatenate.42 = bf16[32,8,2176]{2,1,0:T(8,128)(2,1)} concatenate(bf16[32,8,1024]{2,1,0:T(8,128)(2,1)S(1)} %get-tuple-element.36, bf16[32,8,1024]{2,1,0:T(8,128)(2,1)S(1)} %get-tuple-element.35, bf16[32,8,1]{2,1,0:T(8,128)(2,1)S(1)} %broadcast_in_dim.41, bf16[32,8,1]{2,1,0:T(8,128)(2,1)S(1)} %copy.56, bf16[32,8,1]{2,1,0:T(8,128)(2,1)S(1)} %copy.57, ...), dimensions={2} | concatenate | bytes 2228224 | tf_op jit(solution)/shard_map/concatenate | solution.py:292
  45.9 6.6 %all-to-all-start.1 = ((bf16[32,8,2176]{2,1,0:T(8,128)(2,1)}), bf16[32,8,2176]{2,1,0:T(8,128)(2,1)S(1)}, u32[]{:S(2)}, u32[]{:S(2)}) async-start(bf16[32,8,2176]{2,1,0:T(8,128)(2,1)} %concatenate.42), calls=%async_computation.1 | async-start | bytes 2228224 | tf_op jit(solution)/shard_map/all_to_all | solution.py:292
  52.7 3.1 %collective-permute-start.5 = (bf16[4,16,2048]{2,1,0:T(8,128)(2,1)S(1)}, bf16[4,16,2048]{2,1,0:T(8,128)(2,1)S(1)}, u32[]{:S(2)}, u32[]{:S(2)}) collective-permute-start(bf16[4,16,2048]{2,1,0:T(8,128)(2,1)S(1)} %pad_maximum_fusion.1), channel_id=1, source_target_pairs={{0,24},{1,25},{2,26},{3,27},{4,28},{5,29},{6,30},{7,31},{8,0},{9,1... | collective-permute-start | bytes 786440 | tf_op jit(solution)/shard_map/ppermute | solution.py:280
  55.8 0.6 constant_dynamic-update-slice_fusion.6
  56.4 0.6 constant_dynamic-update-slice_fusion.5
  57.1 0.6 constant_dynamic-update-slice_fusion.4
  57.7 24.0 %collective-permute-done.5 = bf16[4,16,2048]{2,1,0:T(8,128)(2,1)S(1)} collective-permute-done((bf16[4,16,2048]{2,1,0:T(8,128)(2,1)S(1)}, bf16[4,16,2048]{2,1,0:T(8,128)(2,1)S(1)}, u32[]{:S(2)}, u32[]{:S(2)}) %collective-permute-start.5) | collective-permute-done | bytes 262176 | tf_op jit(solution)/shard_map/ppermute | solution.py:280
  81.6 0.5 collective-permute-start.7
  82.2 1.6 collective-permute-start.6
  83.8 0.7 constant_dynamic-update-slice_fusion.3
  84.5 0.7 constant_dynamic-update-slice_fusion.2
  85.3 6.5 %collective-permute-done.6 = bf16[2,16,2048]{2,1,0:T(8,128)(2,1)S(1)} collective-permute-done((bf16[2,16,2048]{2,1,0:T(8,128)(2,1)S(1)}, bf16[2,16,2048]{2,1,0:T(8,128)(2,1)S(1)}, u32[]{:S(2)}, u32[]{:S(2)}) %collective-permute-start.6) | collective-permute-done | bytes 131104 | tf_op jit(solution)/shard_map/ppermute | solution.py:282
  91.8 0.7 constant_dynamic-update-slice_fusion.1
  92.5 0.7 constant_dynamic-update-slice_fusion.mine_ref
  93.1 0.1 slice.115.own_ref
  93.3 0.4 collective-permute-start.10
  93.7 1.7 collective-permute-start.9
  95.4 0.1 broadcast_add_fusion
  95.4 0.1 add.56
  95.5 0.6 pad_add_fusion.where_ref
  96.1 0.1 copy.59
  96.2 0.6 slice.114.nug_ref
  96.8 19.2 %shard_map.46 = (bf16[256,4096]{1,0:T(8,128)(2,1)}, f32[1,256]{1,0:T(1,128)}, f32[256,256]{1,0:T(8,128)}, f32[256,256]{1,0:T(8,128)}, bf16[768,256]{1,0:T(8,128)(2,1)}) custom-call(s32[18]{0:T(128)} %pad_add_fusion.where_ref, bf16[16,16,2048]{2,1,0:T(8,128)(2,1)} %constant_dynamic-update-slice_fusion.mine_ref, ...), custom_call_target="tpu_custom_call" | custom-call | flops 1 | bytes 1 | tf_op jit(solution)/shard_map/pallas_call | solution.py:309
  116.0 3.0 %collective-permute-done.10.above_ref = bf16[256,2048]{1,0:T(8,128)(2,1)} collective-permute-done((bf16[256,2048]{1,0:T(8,128)(2,1)S(1)}, bf16[256,2048]{1,0:T(8,128)(2,1)}, u32[]{:S(2)}, u32[]{:S(2)}) %collective-permute-start.10) | collective-permute-done | bytes 1048608 | tf_op jit(solution)/shard_map/ppermute | solution.py:308
  119.0 1.5 collective-permute-done.9.below_ref
  120.5 1.9 slice.94
  122.4 1.9 slice.95
  124.3 0.0 collective-permute-start.12
  124.3 2.0 %collective-permute-start.11 = (bf16[128,2048]{1,0:T(8,128)(2,1)}, bf16[128,2048]{1,0:T(8,128)(2,1)S(1)}, u32[]{:S(2)}, u32[]{:S(2)}) collective-permute-start(bf16[128,2048]{1,0:T(8,128)(2,1)} %slice.94), channel_id=1, source_target_pairs={{0,32},{32,64},{64,96},{96,0},{1,33},{33,65},{65,97},{97,1},{2,34}... | collective-permute-start | bytes 1572872 | tf_op jit(solution)/shard_map/ppermute | solution.py:320
  126.3 0.1 slice.104
  126.4 0.1 copy.58
  126.5 2.0 %copy.63 = f32[1,4096]{0,1:T(8,128)} copy(f32[1,4096]{1,0:T(1,128)S(1)} %bitcast.76) | data formatting | bytes 32768
  128.6 7.0 %shard_map.47 = (bf16[512,4096]{1,0:T(8,128)(2,1)}, f32[512,1]{1,0:T(8,128)}, f32[512,256]{1,0:T(8,128)}) custom-call(s32[18]{0:T(128)} %pad_add_fusion.where_ref, bf16[256,2048]{1,0:T(8,128)(2,1)} %copy-done.1, bf16[256,2048]{1,0:T(8,128)(2,1)} %collective-permute-done.9.below_ref, bf16[256,2048]{1,0:T(8,128)(2,1)} %collective-permute-done.10.above_ref, ...), custom_call_target="tpu_custom_call" | custom-call | flops 1 | bytes 1 | tf_op jit(solution)/shard_map/pallas_call | solution.py:323
  135.6 2.4 %collective-permute-done.12.far1_ref = bf16[128,2048]{1,0:T(8,128)(2,1)S(1)} collective-permute-done((bf16[128,2048]{1,0:T(8,128)(2,1)}, bf16[128,2048]{1,0:T(8,128)(2,1)S(1)}, u32[]{:S(2)}, u32[]{:S(2)}) %collective-permute-start.12) | collective-permute-done | bytes 524320 | tf_op jit(solution)/shard_map/ppermute | solution.py:320
  137.9 1.5 collective-permute-done.11.far0_ref
  139.4 0.8 copy-done.3
  140.2 5.1 %shard_map.48 = (bf16[512,4096]{1,0:T(8,128)(2,1)}, f32[1,768]{1,0:T(1,128)}, bf16[768,512]{1,0:T(8,128)(2,1)}) custom-call(s32[18]{0:T(128)} %pad_add_fusion.where_ref, bf16[128,2048]{1,0:T(8,128)(2,1)} %copy-done.3, bf16[128,2048]{1,0:T(8,128)(2,1)} %copy-done.2, f32[1,4096]{1,0:T(1,128)} %bitcast.72, ...), custom_call_target="tpu_custom_call", output_to_operand_aliasing={{0}: (9, {})} | custom-call | flops 1 | bytes 1 | tf_op jit(solution)/shard_map/pallas_call | solution.py:333
  145.4 2.1 %all-gather.2.cloned.1.call-done = bf16[16,1,32,8,4096]{4,3,2,1,0:T(8,128)(2,1)} async-done(((bf16[16,1,1,8,4096]{4,3,2,1,0:T(8,128)(2,1)}), bf16[16,1,32,8,4096]{4,3,2,1,0:T(8,128)(2,1)}) %all-gather.2.cloned.1.call-update) | async-done | bytes 33554448 | tf_op jit(solution)/shard_map/all_gather | solution.py:253
  147.5 40.2 %shard_map.49 = f32[16384,128]{1,0:T(8,128)} custom-call(s32[18]{0:T(128)} %pad_add_fusion.where_ref, bf16[4096,4096]{1,0:T(8,128)(2,1)} %bitcast.84, f32[4096,1]{1,0:T(8,128)} %bitcast.69, bf16[256,4096]{1,0:T(8,128)(2,1)} %get-tuple-element.19.scaled0_ref.w0_ref, bf16[512,4096]{1,0:T(8,128)(2,1)} %get-tuple-element.28.wc_ref, ...), custom_call_target="tpu_custom_call" | custom-call | flops 30000001024 | bytes 50331648 | tf_op jit(solution)/shard_map/pallas_call | solution.py:352
  (43 shorter events, 0.3 us)
Async XLA Ops:
  6.5 140.9 %all-gather.2.cloned.1.call-start = ((), (), s32[]{:S(2)}) async-start(), calls=%async_computation.2 | async-start | bytes 34603008 | tf_op jit(solution)/shard_map/all_gather | solution.py:253
  11.5 5.5 %copy-start = (bf16[16,1,1,8,4096]{4,3,2,1,0:T(8,128)(2,1)S(1)}, bf16[16,1,1,8,4096]{4,3,2,1,0:T(8,128)(2,1)}, u32[]{:S(2)}) copy-start(bf16[16,1,1,8,4096]{4,3,2,1,0:T(8,128)(2,1)} %param.4) | copy-start | bytes 3145732
  11.5 5.5 %copy-start.4 = (f32[4096]{0:T(1024)S(1)}, f32[4096]{0:T(1024)}, u32[]{:S(2)}) copy-start(f32[4096]{0:T(1024)} %param.5) | copy-start | bytes 49156
  11.5 24.8 %all-to-all-start = ((bf16[4,16,8,1408]{3,2,1,0:T(8,128)(2,1)}), bf16[4,16,8,1408]{3,2,1,0:T(8,128)(2,1)S(1)}, u32[]{:S(2)}, u32[]{:S(2)}) async-start(bf16[4,16,8,1408]{3,2,1,0:T(8,128)(2,1)} %pad_maximum_fusion), calls=%async_computation | async-start | bytes 2883584 | tf_op jit(solution)/shard_map/all_to_all | solution.py:267
  36.6 1.3 collective-permute-start
  38.5 14.1 %collective-permute-start.3 = (bf16[1,16,2048]{2,1,0:T(8,128)(2,1)S(1)}, bf16[1,16,2048]{2,1,0:T(8,128)(2,1)S(1)}, u32[]{:S(2)}, u32[]{:S(2)}) collective-permute-start(bf16[1,16,2048]{2,1,0:T(8,128)(2,1)S(1)} %get-tuple-element.34), channel_id=1, source_target_pairs={{0,4},{1,5},{2,6},{3,7},{4,0},{5,1},{6,2},{7,3},{8,12},{9,13},{10,... | collective-permute-start | bytes 196616 | tf_op jit(solution)/shard_map/ppermute | solution.py:237
  41.5 11.1 %collective-permute-start.2 = (bf16[1,16,2048]{2,1,0:T(8,128)(2,1)S(1)}, bf16[1,16,2048]{2,1,0:T(8,128)(2,1)S(1)}, u32[]{:S(2)}, u32[]{:S(2)}) collective-permute-start(bf16[1,16,2048]{2,1,0:T(8,128)(2,1)S(1)} %get-tuple-element.34), channel_id=1, source_target_pairs={{0,6},{1,7},{2,0},{3,1},{4,2},{5,3},{6,4},{7,5},{8,14},{9,15},{10,... | collective-permute-start | bytes 196616 | tf_op jit(solution)/shard_map/ppermute | solution.py:237
  42.7 9.9 %collective-permute-start.1 = (bf16[1,16,2048]{2,1,0:T(8,128)(2,1)S(1)}, bf16[1,16,2048]{2,1,0:T(8,128)(2,1)S(1)}, u32[]{:S(2)}, u32[]{:S(2)}) collective-permute-start(bf16[1,16,2048]{2,1,0:T(8,128)(2,1)S(1)} %get-tuple-element.34), channel_id=1, source_target_pairs={{0,2},{1,3},{2,4},{3,5},{4,6},{5,7},{6,0},{7,1},{8,10},{9,11},{10,... | collective-permute-start | bytes 196616 | tf_op jit(solution)/shard_map/ppermute | solution.py:237
  45.9 47.2 %all-to-all-start.1 = ((bf16[32,8,2176]{2,1,0:T(8,128)(2,1)}), bf16[32,8,2176]{2,1,0:T(8,128)(2,1)S(1)}, u32[]{:S(2)}, u32[]{:S(2)}) async-start(bf16[32,8,2176]{2,1,0:T(8,128)(2,1)} %concatenate.42), calls=%async_computation.1 | async-start | bytes 2228224 | tf_op jit(solution)/shard_map/all_to_all | solution.py:292
  52.7 29.0 %collective-permute-start.5 = (bf16[4,16,2048]{2,1,0:T(8,128)(2,1)S(1)}, bf16[4,16,2048]{2,1,0:T(8,128)(2,1)S(1)}, u32[]{:S(2)}, u32[]{:S(2)}) collective-permute-start(bf16[4,16,2048]{2,1,0:T(8,128)(2,1)S(1)} %pad_maximum_fusion.1), channel_id=1, source_target_pairs={{0,24},{1,25},{2,26},{3,27},{4,28},{5,29},{6,30},{7,31},{8,0},{9,1... | collective-permute-start | bytes 786440 | tf_op jit(solution)/shard_map/ppermute | solution.py:280
  55.8 26.4 %collective-permute-start.4 = (bf16[4,16,2048]{2,1,0:T(8,128)(2,1)S(1)}, bf16[4,16,2048]{2,1,0:T(8,128)(2,1)S(1)}, u32[]{:S(2)}, u32[]{:S(2)}) collective-permute-start(bf16[4,16,2048]{2,1,0:T(8,128)(2,1)S(1)} %pad_maximum_fusion.1), channel_id=1, source_target_pairs={{0,8},{1,9},{2,10},{3,11},{4,12},{5,13},{6,14},{7,15},{8,16},{9,17... | collective-permute-start | bytes 786440 | tf_op jit(solution)/shard_map/ppermute | solution.py:280
  57.7 37.7 %copy-start.6 = (s32[4]{0:T(128)S(1)}, s32[4]{0:T(128)}, u32[]{:S(2)}) copy-start(s32[4]{0:T(128)} %constant.67.clone) | copy-start | bytes 52
  81.6 10.8 %collective-permute-start.7 = (bf16[2,16,2048]{2,1,0:T(8,128)(2,1)S(1)}, bf16[2,16,2048]{2,1,0:T(8,128)(2,1)S(1)}, u32[]{:S(2)}, u32[]{:S(2)}) collective-permute-start(bf16[2,16,2048]{2,1,0:T(8,128)(2,1)S(1)} %slice.112), channel_id=1, source_target_pairs={{0,24},{1,25},{2,26},{3,27},{4,28},{5,29},{6,30},{7,31},{8,0},{9,1... | collective-permute-start | bytes 393224 | tf_op jit(solution)/shard_map/ppermute | solution.py:282
  82.2 9.6 %collective-permute-start.6 = (bf16[2,16,2048]{2,1,0:T(8,128)(2,1)S(1)}, bf16[2,16,2048]{2,1,0:T(8,128)(2,1)S(1)}, u32[]{:S(2)}, u32[]{:S(2)}) collective-permute-start(bf16[2,16,2048]{2,1,0:T(8,128)(2,1)S(1)} %slice.111), channel_id=1, source_target_pairs={{0,8},{1,9},{2,10},{3,11},{4,12},{5,13},{6,14},{7,15},{8,16},{9,17... | collective-permute-start | bytes 393224 | tf_op jit(solution)/shard_map/ppermute | solution.py:282
  93.1 3.7 %collective-permute-start.8 = (bf16[16,16,2048]{2,1,0:T(8,128)(2,1)}, bf16[16,16,2048]{2,1,0:T(8,128)(2,1)}, u32[]{:S(2)}, u32[]{:S(2)}) collective-permute-start(bf16[16,16,2048]{2,1,0:T(8,128)(2,1)} %constant_dynamic-update-slice_fusion.mine_ref), channel_id=1, source_target_pairs={{0,1},{1,0},{2,3},{3,2},{4,5},{5,4},{6,7},{7,6},{8,9},{9,8},{10,11... | collective-permute-start | bytes 3145736 | tf_op jit(solution)/shard_map/ppermute | solution.py:283
  93.2 31.0 %copy-start.1 = (bf16[256,2048]{1,0:T(8,128)(2,1)}, bf16[256,2048]{1,0:T(8,128)(2,1)S(1)}, u32[]{:S(2)}) copy-start(bf16[256,2048]{1,0:T(8,128)(2,1)S(1)} %slice.115.own_ref) | copy-start | bytes 3145732
  93.3 25.7 %collective-permute-start.10 = (bf16[256,2048]{1,0:T(8,128)(2,1)S(1)}, bf16[256,2048]{1,0:T(8,128)(2,1)}, u32[]{:S(2)}, u32[]{:S(2)}) collective-permute-start(bf16[256,2048]{1,0:T(8,128)(2,1)S(1)} %slice.115.own_ref), channel_id=1, source_target_pairs={{0,96},{32,0},{64,32},{96,64},{1,97},{33,1},{65,33},{97,65},{2,98}... | collective-permute-start | bytes 3145736 | tf_op jit(solution)/shard_map/ppermute | solution.py:308
  93.7 26.8 %collective-permute-start.9 = (bf16[256,2048]{1,0:T(8,128)(2,1)S(1)}, bf16[256,2048]{1,0:T(8,128)(2,1)}, u32[]{:S(2)}, u32[]{:S(2)}) collective-permute-start(bf16[256,2048]{1,0:T(8,128)(2,1)S(1)} %slice.115.own_ref), channel_id=1, source_target_pairs={{0,32},{32,64},{64,96},{96,0},{1,33},{33,65},{65,97},{97,1},{2,34}... | collective-permute-start | bytes 3145736 | tf_op jit(solution)/shard_map/ppermute | solution.py:308
  96.2 28.1 %copy-start.5 = (f32[1,1,3,256]{3,1,2,0:T(1,128)}, f32[1,1,3,256]{3,1,2,0:T(1,128)S(1)}, u32[]{:S(2)}) copy-start(f32[1,1,3,256]{3,1,2,0:T(1,128)S(1)} %copy.64) | copy-start | bytes 9220
  124.3 13.6 %collective-permute-start.12 = (bf16[128,2048]{1,0:T(8,128)(2,1)}, bf16[128,2048]{1,0:T(8,128)(2,1)S(1)}, u32[]{:S(2)}, u32[]{:S(2)}) collective-permute-start(bf16[128,2048]{1,0:T(8,128)(2,1)} %slice.95), channel_id=1, source_target_pairs={{0,96},{32,0},{64,32},{96,64},{1,97},{33,1},{65,33},{97,65},{2,98}... | collective-permute-start | bytes 1572872 | tf_op jit(solution)/shard_map/ppermute | solution.py:320
  124.3 15.1 %collective-permute-start.11 = (bf16[128,2048]{1,0:T(8,128)(2,1)}, bf16[128,2048]{1,0:T(8,128)(2,1)S(1)}, u32[]{:S(2)}, u32[]{:S(2)}) collective-permute-start(bf16[128,2048]{1,0:T(8,128)(2,1)} %slice.94), channel_id=1, source_target_pairs={{0,32},{32,64},{64,96},{96,0},{1,33},{33,65},{65,97},{97,1},{2,34}... | collective-permute-start | bytes 1572872 | tf_op jit(solution)/shard_map/ppermute | solution.py:320
  137.9 1.5 copy-start.2
  139.4 0.8 copy-start.3
Sparse Core Ops, SparseCore 0:
  9.7 137.7 all-gather.1

commit v6 on v5

--- a/solution.py
+++ b/solution.py
@@ -11,7 +11,6 @@
 HIGH = lax.Precision.HIGHEST
 NT = (((1,), (1,)), ((), ()))
 NN = (((1,), (0,)), ((), ()))
-RING = (0, 3, 1, 2)
 GRANT = 62 * 2**20
 SMALL = pl.CostEstimate(flops=1, bytes_accessed=1, transcendentals=0)
 VMEM = pl.BlockSpec(memory_space=pltpu.VMEM)
@@ -120,14 +119,14 @@
 
 def corner_kernel(where_ref, mine_ref, theirs_ref, weight_ref, nug_ref,
                   scaled_ref, norm_ref, l_ref, x_ref, x3_ref, raw_ref, a_ref, sem):
-    lines, half = mine_ref.shape[1:]
-    quarter = half // 2
+    eighth = mine_ref.shape[1]
+    quarter = 2 * eighth
     core = lax.rem(where_ref[1], 2)
     pairs = []
-    for n in range(mine_ref.shape[0]):
-        rows = pl.ds(pl.multiple_of(where_ref[2 + n] * lines, lines), lines)
-        pairs.append((mine_ref.at[n], raw_ref.at[rows, pl.ds(pl.multiple_of(core * half, half), half)]))
-        pairs.append((theirs_ref.at[n], raw_ref.at[rows, pl.ds(pl.multiple_of((1 - core) * half, half), half)]))
+    for n, spot in enumerate(spots(where_ref, quarter)):
+        for ref, side in ((mine_ref, core), (theirs_ref, 1 - core)):
+            at = pl.multiple_of(spot + side * eighth, eighth)
+            pairs.append((ref.at[n * NB : (n + 1) * NB], raw_ref.at[:, pl.ds(at, eighth)]))
     bring(sem, pairs)
     norms = jnp.zeros((NB, 1), jnp.float32)
     cross = jnp.zeros((NB, NB), jnp.float32)
@@ -149,13 +148,15 @@
     store_triple(x3_ref, x_ref[...].T)
 
 
-def column_kernel(where_ref, own_ref, below_ref, above_ref, weight_ref, scaled0_ref,
-                  scaled_ref, norm_ref, cross_ref, raw_ref, zero_ref, sem):
-    quarter = own_ref.shape[1] // 2
+def column_kernel(where_ref, own0_ref, own1_ref, below0_ref, below1_ref, above0_ref, above1_ref, weight_ref,
+                  scaled0_ref, scaled_ref, norm_ref, cross_ref, raw_ref, zero_ref, sem):
+    quarter = own0_ref.shape[1] // 2
     pairs = [(scaled0_ref, zero_ref)]
-    for n, ref in enumerate((own_ref, below_ref, above_ref)):
+    for n, group in enumerate(((own0_ref, own1_ref), (below0_ref, below1_ref), (above0_ref, above1_ref))):
         for u in range(2):
-            pairs.append((ref.at[:, u * quarter : (u + 1) * quarter], raw_ref.at[n, u * NB : (u + 1) * NB]))
+            for side, ref in enumerate(group):
+                rows = slice(u * NB + side * NB // 2, u * NB + (side + 1) * NB // 2)
+                pairs.append((ref.at[:, u * quarter : (u + 1) * quarter], raw_ref.at[n, rows]))
     bring(sem, pairs)
     norms = jnp.zeros((2 * NB, 1), jnp.float32)
     cross = jnp.zeros((2 * NB, NB), jnp.float32)
@@ -225,18 +226,6 @@
                 o_ref[pl.ds(n * NB * 4 + 2 * u + half, NB, stride=4), :] = result[:, 128 * half : 128 * (half + 1)]
 
 
-def x_move(step):
-    return [(y * 8 + x * 2 + k, y * 8 + (x + step) % 4 * 2 + k) for y in range(4) for x in range(4) for k in range(2)]
-
-
-def y_move(step):
-    return [(y * 8 + x * 2 + k, (y + step) % 4 * 8 + x * 2 + k) for y in range(4) for x in range(4) for k in range(2)]
-
-
-def ring_join(value, moves):
-    return jnp.concatenate([value] + [lax.ppermute(value, "col", moves(step)) for step in (1, -1, 2)], axis=0)
-
-
 def local(samples, ard_weight, nugget):
     row_count = lax.axis_size("row")
     col_count = lax.axis_size("col")
@@ -261,26 +250,10 @@
 
     cut = own.reshape(row_tiles, sub, row_count, quarter).transpose(2, 0, 1, 3)
     extra = jnp.broadcast_to(nugget.reshape(1, row_tiles, sub, 1), (row_count, row_tiles, sub, 128))
-    share = features // row_tiles
-    zero = own[0].reshape(sub, row_tiles, share).transpose(1, 0, 2)
-    zero = jnp.broadcast_to(zero[None], (row_count, row_tiles, sub, share))
-    sent = lax.all_to_all(jnp.concatenate([cut, extra, zero], axis=3), "row", 0, 0)
-    zero = sent[0, :, :, quarter + 128 :].transpose(1, 0, 2).reshape(sub, features)
-    sent = sent[..., : quarter + 128].reshape(row_count, 2, fold, sub, quarter + 128).transpose(2, 0, 1, 3, 4)
+    sent = lax.all_to_all(jnp.concatenate([cut, extra], axis=3), "row", 0, 0)
+    sent = sent.reshape(row_count, 2, fold, sub, quarter + 128).transpose(2, 0, 1, 3, 4)
     sent = sent.reshape(col_count, 2, sub, quarter + 128)
 
-    core = col_index % 2
-    chip_x, chip_y = col_index // 2 % 4, col_index // 8
-    sibling = [(i, i ^ 1) for i in range(col_count)]
-    left, right = zero[:, : features // 2], zero[:, features // 2 :]
-    kept = jnp.where(core == 0, left, right)
-    came = lax.ppermute(jnp.where(core == 0, right, left), "col", sibling)
-    block = jnp.where(core == 0, jnp.concatenate([kept, came]), jnp.concatenate([came, kept]))
-    line = ring_join(block[None], x_move)
-    below, above = lax.ppermute(line, "col", y_move(1)), lax.ppermute(line, "col", y_move(-1))
-    mine = jnp.concatenate(
-        [line, below, above, lax.ppermute(below[:2], "col", y_move(1)), lax.ppermute(above[2:], "col", y_move(-1))])
-    theirs = lax.ppermute(mine, "col", sibling)
     body = sent[..., :quarter]
     tags = sent[..., quarter]
     tail = jnp.concatenate(
@@ -289,9 +262,13 @@
          jnp.zeros((col_count, sub, 61), bf16),
          jnp.broadcast_to(bits[None], (col_count, sub, 3 * row_tiles)),
          jnp.zeros((col_count, sub, 64 - 3 * row_tiles), bf16)], axis=2)
-    got = lax.all_to_all(jnp.concatenate([body[:, 0], body[:, 1], tail], axis=2), "col", 0, 0)
+    eighth = quarter // 2
+    zero = jnp.stack([body[0, 0, :, :eighth], body[0, 0, :, eighth:]])
+    zero = jnp.broadcast_to(zero[None], (col_count // 2, 2, sub, eighth)).reshape(col_count, sub, eighth)
+    payload = jnp.concatenate([body[:, 0], body[:, 1], zero, tail], axis=2)
+    got = lax.all_to_all(payload, "col", 0, 0)
     got = got.reshape(NB, -1)
-    tags = got[:, 2 * quarter :].astype(f32)
+    tags = got[:, 2 * quarter + eighth :].astype(f32)
     nug = tags[:, :3].T.reshape(1, 3 * NB)
     norm_bits = tags[:, 64 : 64 + 3 * row_tiles].reshape(NB, 3, row_tiles)
     norms = ((norm_bits[:, 0] + norm_bits[:, 1]) + norm_bits[:, 2]).T
@@ -299,37 +276,44 @@
     up = [(i, (i + 1) % row_count) for i in range(row_count)]
     down = [(i, (i - 1) % row_count) for i in range(row_count)]
 
-    ring_of = jnp.array(RING, jnp.int32)
-    chips = lax.rem(chip_y + ring_of, 4)[:, None] * 4 + lax.rem(chip_x + ring_of, 4)[None, :]
-    where = jnp.concatenate([jnp.stack([row_index, col_index]), chips.reshape(-1)]).astype(jnp.int32)
+    where = jnp.stack([row_index, col_index]).astype(jnp.int32)
     norms = norms.reshape(-1, 1)
 
-    cols = got[:, : 2 * quarter]
-    below, above = lax.ppermute(cols, "row", up), lax.ppermute(cols, "row", down)
+    zero = [got[: NB // 2, 2 * quarter : 2 * quarter + eighth], got[NB // 2 :, 2 * quarter : 2 * quarter + eighth]]
+    below = [lax.ppermute(value, "row", up) for value in zero]
+    above = [lax.ppermute(value, "row", down) for value in zero]
+    far = [lax.ppermute(below[0], "row", up), lax.ppermute(above[1], "row", down)]
+    far, got = lax.optimization_barrier((far, got))
+    mine = jnp.concatenate([*zero, *below, *above, *far])
+    theirs = lax.ppermute(mine, "col", [(i, i ^ 1) for i in range(col_count)])
+
+    cols = [got[: NB // 2, : 2 * quarter], got[NB // 2 :, : 2 * quarter]]
+    below = [lax.ppermute(value, "row", up) for value in cols]
+    above = [lax.ppermute(value, "row", down) for value in cols]
     scaled0, norms0, corner, inverse, inverse3 = pl.pallas_call(
         corner_kernel,
         out_shape=(shape((NB, features), bf16), shape((1, NB), f32), shape((NB, NB), f32), shape((NB, NB), f32),
                    shape((3 * NB, NB), bf16)),
         in_specs=[SMEM] + [HBM] * 2 + [VMEM] * 2,
         out_specs=(VMEM,) * 5,
-        scratch_shapes=[pltpu.VMEM((NB, features), bf16), pltpu.VMEM((NB, NB), f32), pltpu.SemaphoreType.DMA((32,))],
+        scratch_shapes=[pltpu.VMEM((NB, features), bf16), pltpu.VMEM((NB, NB), f32), pltpu.SemaphoreType.DMA((8,))],
         cost_estimate=SMALL,
         compiler_params=pltpu.CompilerParams(vmem_limit_bytes=GRANT),
     )(where, mine, theirs, weight_row, nug[:, :NB])
     corner, below, above = lax.optimization_barrier((corner, below, above))
-    cols_far = (lax.ppermute(below[: NB // 2], "row", up), lax.ppermute(above[NB // 2 :], "row", down))
+    cols_far = (lax.ppermute(below[0], "row", up), lax.ppermute(above[1], "row", down))
     limit = pltpu.CompilerParams(vmem_limit_bytes=GRANT)
     near = shape((2 * NB, features), bf16)
     scaled, norms_c, cross_c = pl.pallas_call(
         column_kernel,
         out_shape=(near, shape((2 * NB, 1), f32), shape((2 * NB, NB), f32)),
-        in_specs=[SMEM] + [HBM] * 3 + [VMEM, HBM],
+        in_specs=[SMEM] + [HBM] * 6 + [VMEM, HBM],
         out_specs=(VMEM,) * 3,
         scratch_shapes=[pltpu.VMEM((3, 2 * NB, quarter), bf16), pltpu.VMEM((NB, features), bf16),
-                        pltpu.SemaphoreType.DMA((7,))],
+                        pltpu.SemaphoreType.DMA((13,))],
         cost_estimate=SMALL,
         compiler_params=limit,
-    )(where, cols, below, above, weight_row, scaled0)
+    )(where, *cols, *below, *above, weight_row, scaled0)
     scaled, wn, q_panel = pl.pallas_call(
         far_kernel,
         out_shape=(near, shape((1, 3 * NB), f32), shape((3 * NB, 2 * NB), bf16)),

time: 196 us -> 182 us (0.929)
  local copies, waits for them, and re-layouts: 18.7 us -> 10.8 us
  waiting for transfers between devices: 60.9 us -> 58.4 us
    ppermute x13, waiting for transfers between devices: 39.4 us -> 15.1 us  [the longest x2 7.23 us: local(): lax.ppermute(below[0], 'row', up)]
    all_to_all x2, waiting for transfers between devices: 18.8 us -> 42.6 us  [the longest x1 26.7 us: local(): got = lax.all_to_all(payload, 'col', 0, 0)]
    slice x8 -> x2, local copies, waits for them, and re-layouts: 4.89 us -> 1.05 us  [the longest x1 1.03 us: local(): cols = [got[:NB // 2, :2 * quarter], got[NB // 2:, :2 * quarter]]]
    unnamed x23 -> x25, local copies, waits for them, and re-layouts: 6.84 us -> 3.63 us
    all_gather x1, waiting for transfers between devices: 2.1 us -> 0.02 us  [local(): gathered = lax.all_gather(samples, 'col', axis=2, tiled=True)]
    ppermute x13, starting transfers between devices: 14.5 us -> 12.5 us  [the longest x2 3.68 us: local(): lax.ppermute(above[1], 'row', down)]
  transfers between devices with their start and end apart: 16 -> 16, of which waited for: 9 -> 9; matrix products, arithmetic and copies ran while one was open for 11% -> 6% of each run, Pallas kernels for 16% -> 17%
where the time goes in v6:
time: 182 us; the launch traced here: 181 us
  Pallas kernels  71.4 us (39%)
  waiting for transfers between devices  58.4 us (32%)
  starting transfers between devices  25.3 us (14%)
  between operations  13.7 us (8%)
  local copies, waits for them, and re-layouts  10.8 us (6%)
    pallas_call x1, Pallas kernels, local(): pl.pallas_call(functools.partial(main_kernel, tiles, 4), out_shape=shape(...  40.2 us
    all_to_all x1, waiting for transfers between devices, local(): got = lax.all_to_all(payload, 'col', 0, 0)  26.7 us
    pallas_call x1, Pallas kernels, local(): pl.pallas_call(corner_kernel, out_shape=(shape((NB, features), bf16), sha...  19 us
    all_to_all x1, waiting for transfers between devices, local(): sent = lax.all_to_all(jnp.concatenate([cut, extra], axis=3), 'row', 0, 0)  15.9 us
    all_to_all x1, starting transfers between devices, local(): got = lax.all_to_all(payload, 'col', 0, 0)  7.32 us
    ppermute x2, waiting for transfers between devices, local(): lax.ppermute(below[0], 'row', up)  7.23 us
    pallas_call x1, Pallas kernels, local(): pl.pallas_call(column_kernel, out_shape=(near, shape((2 * NB, 1), f32), s...  7.08 us
    all_to_all x1, starting transfers between devices, local(): sent = lax.all_to_all(jnp.concatenate([cut, extra], axis=3), 'row', 0, 0)  5.52 us
  transfers between devices with their start and end apart: 16, of which 9 were waited for; matrix products, arithmetic and copies ran while one was open for 6% of the time, Pallas kernels for 17%

profile of v6, /device:TPU:0, one launch (start us, length us, event | category | flops | bytes accessed | tf_op | source)
XLA Modules:
  0.0 181.3 jit_solution(3159997535081844481)
XLA Ops:
  6.5 0.7 all-gather.2.cloned.1.call-update
  7.3 0.5 copy-done
  7.8 0.8 reshape_reshape.3
  8.6 0.1 copy.55
  8.6 0.2 broadcast_in_dim.35
  8.9 0.6 pad_maximum_fusion
  9.4 1.1 copy.56
  10.6 5.5 %all-to-all-start = ((bf16[4,16,8,1152]{3,2,1,0:T(8,128)(2,1)}), bf16[4,16,8,1152]{3,2,1,0:T(8,128)(2,1)S(1)}, u32[]{:S(2)}, u32[]{:S(2)}) async-start(bf16[4,16,8,1152]{3,2,1,0:T(8,128)(2,1)} %copy.56), calls=%async_computation | async-start | bytes 2359296 | tf_op jit(solution)/shard_map/all_to_all | solution.py:253
  16.1 0.0 copy-done.5
  16.1 0.4 fusion
  16.5 0.1 copy.59
  16.6 0.1 broadcast_in_dim.40
  16.6 15.9 %all-to-all-done = bf16[4,16,8,1152]{3,2,1,0:T(8,128)(2,1)S(1)} async-done(((bf16[4,16,8,1152]{3,2,1,0:T(8,128)(2,1)}), bf16[4,16,8,1152]{3,2,1,0:T(8,128)(2,1)S(1)}, u32[]{:S(2)}, u32[]{:S(2)}) %all-to-all-start) | async-done | bytes 1179680 | tf_op jit(solution)/shard_map/all_to_all | solution.py:253
  32.6 0.1 copy.57
  32.7 0.2 copy.58
  32.9 0.2 copy.62
  33.1 0.2 copy.61
  33.2 0.1 slice_reduce_fusion
  33.4 0.1 slice_bitcast_fusion
  33.5 0.1 broadcast_in_dim.38
  33.7 1.9 %concatenate.10 = bf16[32,8,2688]{2,1,0:T(8,128)(2,1)} concatenate(bf16[32,8,1024]{2,1,0:T(8,128)(2,1)S(1)} %get-tuple-element.50, bf16[32,8,1024]{2,1,0:T(8,128)(2,1)S(1)} %get-tuple-element.49, bf16[32,8,512]{2,1,0:T(8,128)(2,1)S(1)} %bitcast.65, bf16[32,8,1]{2,1,0:T(8,128)(2,1)S(1)} %broadcast_in_dim.38, bf16[32,8,1]{2,1,0:T(8,128)(2,1)S(1)} %copy.61, ...), dimensions={2} | concatenate | bytes 2752512 | tf_op jit(solution)/shard_map/concatenate | solution.py:268
  35.6 7.3 %all-to-all-start.1 = ((bf16[32,8,2688]{2,1,0:T(8,128)(2,1)}), bf16[32,8,2688]{2,1,0:T(8,128)(2,1)S(1)}, u32[]{:S(2)}, u32[]{:S(2)}) async-start(bf16[32,8,2688]{2,1,0:T(8,128)(2,1)} %concatenate.10), calls=%async_computation.1 | async-start | bytes 2752512 | tf_op jit(solution)/shard_map/all_to_all | solution.py:269
  42.9 26.7 %all-to-all-done.1 = bf16[32,8,2688]{2,1,0:T(8,128)(2,1)S(1)} async-done(((bf16[32,8,2688]{2,1,0:T(8,128)(2,1)}), bf16[32,8,2688]{2,1,0:T(8,128)(2,1)S(1)}, u32[]{:S(2)}, u32[]{:S(2)}) %all-to-all-start.1) | async-done | bytes 1376288 | tf_op jit(solution)/shard_map/all_to_all | solution.py:269
  69.6 0.1 collective-permute-start.3
  69.6 2.0 %collective-permute-start.1 = (bf16[128,512]{1,0:T(8,128)(2,1)S(1)}, bf16[128,512]{1,0:T(8,128)(2,1)S(1)}, u32[]{:S(2)}, u32[]{:S(2)}) collective-permute-start(bf16[128,512]{1,0:T(8,128)(2,1)S(1)} %get-tuple-element.45), channel_id=1, source_target_pairs={{0,32},{32,64},{64,96},{96,0},{1,33},{33,65},{65,97},{97,1},{2,34}... | collective-permute-start | bytes 393224 | tf_op jit(solution)/shard_map/ppermute | solution.py:283
  71.7 1.3 collective-permute-start.2
  73.0 0.7 collective-permute-start
  73.7 1.6 collective-permute-done.3
  75.4 1.0 collective-permute-start.5
  76.3 2.8 %collective-permute-done = bf16[128,512]{1,0:T(8,128)(2,1)S(1)} collective-permute-done((bf16[128,512]{1,0:T(8,128)(2,1)S(1)}, bf16[128,512]{1,0:T(8,128)(2,1)S(1)}, u32[]{:S(2)}, u32[]{:S(2)}) %collective-permute-start) | collective-permute-done | bytes 131104 | tf_op jit(solution)/shard_map/ppermute | solution.py:283
  79.1 0.0 collective-permute-start.4
  79.1 0.0 collective-permute-done.1
  79.2 0.0 collective-permute-done.2
  79.2 1.1 collective-permute-done.5
  80.3 5.0 %collective-permute-done.4 = bf16[128,512]{1,0:T(8,128)(2,1)S(1)} collective-permute-done((bf16[128,512]{1,0:T(8,128)(2,1)S(1)}, bf16[128,512]{1,0:T(8,128)(2,1)S(1)}, u32[]{:S(2)}, u32[]{:S(2)}) %collective-permute-start.4) | collective-permute-done | bytes 131104 | tf_op jit(solution)/shard_map/ppermute | solution.py:285
  85.3 0.0 copy-start.2
  85.4 0.1 collective-permute-start.6
  85.5 1.0 fusion.3
  86.5 0.0 collective-permute-start.10
  86.5 2.0 %collective-permute-start.8 = (bf16[128,2048]{1,0:T(8,128)(2,1)S(1)}, bf16[128,2048]{1,0:T(8,128)(2,1)}, u32[]{:S(2)}, u32[]{:S(2)}) collective-permute-start(bf16[128,2048]{1,0:T(8,128)(2,1)S(1)} %get-tuple-element.43.own1_ref), channel_id=1, source_target_pairs={{0,32},{32,64},{64,96},{96,0},{1,33},{33,65},{65,97},{97,1},{2,34}... | collective-permute-start | bytes 1572872 | tf_op jit(solution)/shard_map/ppermute | solution.py:291
  88.5 1.2 collective-permute-start.9
  89.7 0.8 collective-permute-start.7
  90.6 0.7 pad_add_fusion.where_ref
  91.3 0.1 copy.64
  91.3 0.6 slice.102.nug_ref
  91.9 0.0 collective-permute-done.6.theirs_ref
  91.9 19.0 %shard_map.37 = (bf16[256,4096]{1,0:T(8,128)(2,1)}, f32[1,256]{1,0:T(1,128)}, f32[256,256]{1,0:T(8,128)}, f32[256,256]{1,0:T(8,128)}, bf16[768,256]{1,0:T(8,128)(2,1)}) custom-call(s32[2]{0:T(128)} %pad_add_fusion.where_ref, bf16[1024,512]{1,0:T(8,128)(2,1)} %copy-done.2, bf16[1024,512]{1,0:T(8,128)(2,1)} %collective-permute-done.6.theirs_ref, ...), custom_call_target="tpu_custom_call" | custom-call | flops 1 | bytes 1 | tf_op jit(solution)/shard_map/pallas_call | solution.py:293
  110.9 0.0 collective-permute-done.10.above1_ref
  110.9 0.0 collective-permute-done.8.below1_ref
  111.0 1.1 collective-permute-done.9.above0_ref
  112.0 1.2 collective-permute-done.7.below0_ref
  113.3 0.5 collective-permute-start.11
  113.8 2.7 %collective-permute-start.12 = (bf16[128,2048]{1,0:T(8,128)(2,1)}, bf16[128,2048]{1,0:T(8,128)(2,1)S(1)}, u32[]{:S(2)}, u32[]{:S(2)}) collective-permute-start(bf16[128,2048]{1,0:T(8,128)(2,1)} %collective-permute-done.10.above1_ref), channel_id=1, source_target_pairs={{0,96},{32,0},{64,32},{96,64},{1,97},{33,1},{65,33},{97,65},{2,98}... | collective-permute-start | bytes 1572872 | tf_op jit(solution)/shard_map/ppermute | solution.py:304
  116.5 0.1 slice.94
  116.6 0.1 copy.63
  116.7 2.0 %copy.68 = f32[1,4096]{0,1:T(8,128)} copy(f32[1,4096]{1,0:T(1,128)S(1)} %bitcast.70) | data formatting | bytes 32768
  118.7 7.1 %shard_map.38 = (bf16[512,4096]{1,0:T(8,128)(2,1)}, f32[512,1]{1,0:T(8,128)}, f32[512,256]{1,0:T(8,128)}) custom-call(s32[2]{0:T(128)} %pad_add_fusion.where_ref, bf16[128,2048]{1,0:T(8,128)(2,1)} %get-tuple-element.44.own0_ref, bf16[128,2048]{1,0:T(8,128)(2,1)} %copy-done.1, bf16[128,2048]{1,0:T(8,128)(2,1)} %collective-permute-done.7.below0_ref, ...), custom_call_target="tpu_custom_call" | custom-call | flops 1 | bytes 1 | tf_op jit(solution)/shard_map/pallas_call | solution.py:307
  125.8 2.2 %collective-permute-done.11.far0_ref = bf16[128,2048]{1,0:T(8,128)(2,1)S(1)} collective-permute-done((bf16[128,2048]{1,0:T(8,128)(2,1)}, bf16[128,2048]{1,0:T(8,128)(2,1)S(1)}, u32[]{:S(2)}, u32[]{:S(2)}) %collective-permute-start.11) | collective-permute-done | bytes 524320 | tf_op jit(solution)/shard_map/ppermute | solution.py:304
  128.1 0.0 collective-permute-done.12.far1_ref
  128.1 0.8 copy-done.3
  128.9 0.2 copy-done.4
  129.1 5.1 %shard_map.39 = (bf16[512,4096]{1,0:T(8,128)(2,1)}, f32[1,768]{1,0:T(1,128)}, bf16[768,512]{1,0:T(8,128)(2,1)}) custom-call(s32[2]{0:T(128)} %pad_add_fusion.where_ref, bf16[128,2048]{1,0:T(8,128)(2,1)} %copy-done.3, bf16[128,2048]{1,0:T(8,128)(2,1)} %copy-done.4, f32[1,4096]{1,0:T(1,128)} %bitcast.68, ...), custom_call_target="tpu_custom_call", output_to_operand_aliasing={{0}: (9, {})} | custom-call | flops 1 | bytes 1 | tf_op jit(solution)/shard_map/pallas_call | solution.py:317
  134.2 0.0 all-gather.2.cloned.1.call-done
  134.2 40.2 %shard_map.40 = f32[16384,128]{1,0:T(8,128)} custom-call(s32[2]{0:T(128)} %pad_add_fusion.where_ref, bf16[4096,4096]{1,0:T(8,128)(2,1)} %bitcast.77, f32[4096,1]{1,0:T(8,128)} %bitcast.64, bf16[256,4096]{1,0:T(8,128)(2,1)} %get-tuple-element.26.scaled0_ref.w0_ref, bf16[512,4096]{1,0:T(8,128)(2,1)} %get-tuple-element.38.wc_ref, ...), custom_call_target="tpu_custom_call" | custom-call | flops 30000001024 | bytes 50331648 | tf_op jit(solution)/shard_map/pallas_call | solution.py:336
  (36 shorter events, 0.3 us)
Async XLA Ops:
  6.5 1.2 copy-start
  6.5 2.0 %copy-start.7 = (bf16[16,1,1,8]{0,3,2,1:T(8,128)(2,1)S(1)}, bf16[16,1,1,8]{0,3,2,1:T(8,128)(2,1)}, u32[]{:S(2)}) copy-start(bf16[16,1,1,8]{0,3,2,1:T(8,128)(2,1)} %param.5) | copy-start | bytes 772
  6.5 127.7 %all-gather.2.cloned.1.call-start = ((), (), s32[]{:S(2)}) async-start(), calls=%async_computation.2 | async-start | bytes 34603008 | tf_op jit(solution)/shard_map/all_gather | solution.py:242
  10.6 5.5 %copy-start.5 = (f32[4096]{0:T(1024)S(1)}, f32[4096]{0:T(1024)}, u32[]{:S(2)}) copy-start(f32[4096]{0:T(1024)} %param.4) | copy-start | bytes 49156
  10.6 22.0 %all-to-all-start = ((bf16[4,16,8,1152]{3,2,1,0:T(8,128)(2,1)}), bf16[4,16,8,1152]{3,2,1,0:T(8,128)(2,1)S(1)}, u32[]{:S(2)}, u32[]{:S(2)}) async-start(bf16[4,16,8,1152]{3,2,1,0:T(8,128)(2,1)} %copy.56), calls=%async_computation | async-start | bytes 2359296 | tf_op jit(solution)/shard_map/all_to_all | solution.py:253
  35.6 34.0 %all-to-all-start.1 = ((bf16[32,8,2688]{2,1,0:T(8,128)(2,1)}), bf16[32,8,2688]{2,1,0:T(8,128)(2,1)S(1)}, u32[]{:S(2)}, u32[]{:S(2)}) async-start(bf16[32,8,2688]{2,1,0:T(8,128)(2,1)} %concatenate.10), calls=%async_computation.1 | async-start | bytes 2752512 | tf_op jit(solution)/shard_map/all_to_all | solution.py:269
  69.6 5.8 %collective-permute-start.3 = (bf16[128,512]{1,0:T(8,128)(2,1)S(1)}, bf16[128,512]{1,0:T(8,128)(2,1)S(1)}, u32[]{:S(2)}, u32[]{:S(2)}) collective-permute-start(bf16[128,512]{1,0:T(8,128)(2,1)S(1)} %get-tuple-element.45), channel_id=1, source_target_pairs={{0,96},{32,0},{64,32},{96,64},{1,97},{33,1},{65,33},{97,65},{2,98}... | collective-permute-start | bytes 393224 | tf_op jit(solution)/shard_map/ppermute | solution.py:284
  69.6 9.5 %collective-permute-start.1 = (bf16[128,512]{1,0:T(8,128)(2,1)S(1)}, bf16[128,512]{1,0:T(8,128)(2,1)S(1)}, u32[]{:S(2)}, u32[]{:S(2)}) collective-permute-start(bf16[128,512]{1,0:T(8,128)(2,1)S(1)} %get-tuple-element.45), channel_id=1, source_target_pairs={{0,32},{32,64},{64,96},{96,0},{1,33},{33,65},{65,97},{97,1},{2,34}... | collective-permute-start | bytes 393224 | tf_op jit(solution)/shard_map/ppermute | solution.py:283
  71.7 7.5 %collective-permute-start.2 = (bf16[128,512]{1,0:T(8,128)(2,1)S(1)}, bf16[128,512]{1,0:T(8,128)(2,1)S(1)}, u32[]{:S(2)}, u32[]{:S(2)}) collective-permute-start(bf16[128,512]{1,0:T(8,128)(2,1)S(1)} %get-tuple-element.46), channel_id=1, source_target_pairs={{0,96},{32,0},{64,32},{96,64},{1,97},{33,1},{65,33},{97,65},{2,98}... | collective-permute-start | bytes 393224 | tf_op jit(solution)/shard_map/ppermute | solution.py:284
  73.0 6.2 %collective-permute-start = (bf16[128,512]{1,0:T(8,128)(2,1)S(1)}, bf16[128,512]{1,0:T(8,128)(2,1)S(1)}, u32[]{:S(2)}, u32[]{:S(2)}) collective-permute-start(bf16[128,512]{1,0:T(8,128)(2,1)S(1)} %get-tuple-element.46), channel_id=1, source_target_pairs={{0,32},{32,64},{64,96},{96,0},{1,33},{33,65},{65,97},{97,1},{2,34}... | collective-permute-start | bytes 393224 | tf_op jit(solution)/shard_map/ppermute | solution.py:283
  75.4 5.0 %collective-permute-start.5 = (bf16[128,512]{1,0:T(8,128)(2,1)S(1)}, bf16[128,512]{1,0:T(8,128)(2,1)S(1)}, u32[]{:S(2)}, u32[]{:S(2)}) collective-permute-start(bf16[128,512]{1,0:T(8,128)(2,1)S(1)} %collective-permute-done.3), channel_id=1, source_target_pairs={{0,96},{32,0},{64,32},{96,64},{1,97},{33,1},{65,33},{97,65},{2,98}... | collective-permute-start | bytes 393224 | tf_op jit(solution)/shard_map/ppermute | solution.py:285
  79.1 6.2 %collective-permute-start.4 = (bf16[128,512]{1,0:T(8,128)(2,1)S(1)}, bf16[128,512]{1,0:T(8,128)(2,1)S(1)}, u32[]{:S(2)}, u32[]{:S(2)}) collective-permute-start(bf16[128,512]{1,0:T(8,128)(2,1)S(1)} %collective-permute-done), channel_id=1, source_target_pairs={{0,32},{32,64},{64,96},{96,0},{1,33},{33,65},{65,97},{97,1},{2,34}... | collective-permute-start | bytes 393224 | tf_op jit(solution)/shard_map/ppermute | solution.py:285
  85.3 5.9 %copy-start.2 = (bf16[1024,512]{1,0:T(8,128)(2,1)}, bf16[1024,512]{1,0:T(8,128)(2,1)S(1)}, u32[]{:S(2)}) copy-start(bf16[1024,512]{1,0:T(8,128)(2,1)S(1)} %constant_dynamic-update-slice_fusion.mine_ref) | copy-start | bytes 3145732
  85.4 6.6 %collective-permute-start.6 = (bf16[1024,512]{1,0:T(8,128)(2,1)S(1)}, bf16[1024,512]{1,0:T(8,128)(2,1)}, u32[]{:S(2)}, u32[]{:S(2)}) collective-permute-start(bf16[1024,512]{1,0:T(8,128)(2,1)S(1)} %constant_dynamic-update-slice_fusion.mine_ref), channel_id=1, source_target_pairs={{0,1},{1,0},{2,3},{3,2},{4,5},{5,4},{6,7},{7,6},{8,9},{9,8},{10,11... | collective-permute-start | bytes 3145736 | tf_op jit(solution)/shard_map/ppermute | solution.py:288
  86.5 30.1 %copy-start.1 = (bf16[128,2048]{1,0:T(8,128)(2,1)}, bf16[128,2048]{1,0:T(8,128)(2,1)S(1)}, u32[]{:S(2)}) copy-start(bf16[128,2048]{1,0:T(8,128)(2,1)S(1)} %get-tuple-element.43.own1_ref) | copy-start | bytes 1572868
  86.5 24.5 %collective-permute-start.10 = (bf16[128,2048]{1,0:T(8,128)(2,1)S(1)}, bf16[128,2048]{1,0:T(8,128)(2,1)}, u32[]{:S(2)}, u32[]{:S(2)}) collective-permute-start(bf16[128,2048]{1,0:T(8,128)(2,1)S(1)} %get-tuple-element.43.own1_ref), channel_id=1, source_target_pairs={{0,96},{32,0},{64,32},{96,64},{1,97},{33,1},{65,33},{97,65},{2,98}... | collective-permute-start | bytes 1572872 | tf_op jit(solution)/shard_map/ppermute | solution.py:292
  86.5 24.5 %collective-permute-start.8 = (bf16[128,2048]{1,0:T(8,128)(2,1)S(1)}, bf16[128,2048]{1,0:T(8,128)(2,1)}, u32[]{:S(2)}, u32[]{:S(2)}) collective-permute-start(bf16[128,2048]{1,0:T(8,128)(2,1)S(1)} %get-tuple-element.43.own1_ref), channel_id=1, source_target_pairs={{0,32},{32,64},{64,96},{96,0},{1,33},{33,65},{65,97},{97,1},{2,34}... | collective-permute-start | bytes 1572872 | tf_op jit(solution)/shard_map/ppermute | solution.py:291
  88.5 23.5 %collective-permute-start.9 = (bf16[128,2048]{1,0:T(8,128)(2,1)}, bf16[128,2048]{1,0:T(8,128)(2,1)}, u32[]{:S(2)}, u32[]{:S(2)}) collective-permute-start(bf16[128,2048]{1,0:T(8,128)(2,1)} %get-tuple-element.44.own0_ref), channel_id=1, source_target_pairs={{0,96},{32,0},{64,32},{96,64},{1,97},{33,1},{65,33},{97,65},{2,98}... | collective-permute-start | bytes 1572872 | tf_op jit(solution)/shard_map/ppermute | solution.py:292
  89.7 23.5 %collective-permute-start.7 = (bf16[128,2048]{1,0:T(8,128)(2,1)}, bf16[128,2048]{1,0:T(8,128)(2,1)}, u32[]{:S(2)}, u32[]{:S(2)}) collective-permute-start(bf16[128,2048]{1,0:T(8,128)(2,1)} %get-tuple-element.44.own0_ref), channel_id=1, source_target_pairs={{0,32},{32,64},{64,96},{96,0},{1,33},{33,65},{65,97},{97,1},{2,34}... | collective-permute-start | bytes 1572872 | tf_op jit(solution)/shard_map/ppermute | solution.py:291
  91.3 27.4 %copy-start.6 = (f32[1,1,3,256]{3,1,2,0:T(1,128)}, f32[1,1,3,256]{3,1,2,0:T(1,128)S(1)}, u32[]{:S(2)}) copy-start(f32[1,1,3,256]{3,1,2,0:T(1,128)S(1)} %copy.69) | copy-start | bytes 9220
  113.3 14.8 %collective-permute-start.11 = (bf16[128,2048]{1,0:T(8,128)(2,1)}, bf16[128,2048]{1,0:T(8,128)(2,1)S(1)}, u32[]{:S(2)}, u32[]{:S(2)}) collective-permute-start(bf16[128,2048]{1,0:T(8,128)(2,1)} %collective-permute-done.7.below0_ref), channel_id=1, source_target_pairs={{0,32},{32,64},{64,96},{96,0},{1,33},{33,65},{65,97},{97,1},{2,34}... | collective-permute-start | bytes 1572872 | tf_op jit(solution)/shard_map/ppermute | solution.py:304
  113.8 14.3 %collective-permute-start.12 = (bf16[128,2048]{1,0:T(8,128)(2,1)}, bf16[128,2048]{1,0:T(8,128)(2,1)S(1)}, u32[]{:S(2)}, u32[]{:S(2)}) collective-permute-start(bf16[128,2048]{1,0:T(8,128)(2,1)} %collective-permute-done.10.above1_ref), channel_id=1, source_target_pairs={{0,96},{32,0},{64,32},{96,64},{1,97},{33,1},{65,33},{97,65},{2,98}... | collective-permute-start | bytes 1572872 | tf_op jit(solution)/shard_map/ppermute | solution.py:304
  128.1 0.8 copy-start.3
  128.1 1.0 copy-start.4
Sparse Core Ops, SparseCore 0:
  9.7 122.5 all-gather.1

commit v7 on v6

--- a/solution.py
+++ b/solution.py
@@ -118,7 +118,7 @@
 
 
 def corner_kernel(where_ref, mine_ref, theirs_ref, weight_ref, nug_ref,
-                  scaled_ref, norm_ref, l_ref, x_ref, x3_ref, raw_ref, a_ref, sem):
+                  scaled_ref, norm_ref, l_ref, x_ref, raw_ref, a_ref, sem):
     eighth = mine_ref.shape[1]
     quarter = 2 * eighth
     core = lax.rem(where_ref[1], 2)
@@ -145,7 +145,6 @@
     tile = jnp.exp(-0.5 * (norms + row_norms - 2.0 * cross)) + jnp.where(eye, nug_ref[...], 0.0)
     a_ref[...] = 0.5 * (tile + tile.T)
     store_factor(a_ref, l_ref, x_ref)
-    store_triple(x3_ref, x_ref[...].T)
 
 
 def column_kernel(where_ref, own0_ref, own1_ref, below0_ref, below1_ref, above0_ref, above1_ref, weight_ref,
@@ -192,11 +191,14 @@
     norm_ref[:, :NB] = norm0_ref[...]
     norm_ref[:, NB:] = as_row(norms)
     kern = jnp.exp(-0.5 * (norms + norm0_ref[...] - 2.0 * cross))
-    store_triple(q_ref, dot_high(x_ref[...], kern, NT))
+    turned = x_ref[...].T
+    solved = dot_high(turned, dot_high(x_ref[...], kern, NT))
+    store_triple(q_ref, jnp.concatenate(
+        [jnp.where(where_ref[1] == 0, turned, solved[:, :NB]), solved[:, NB:]], axis=1))
     back.wait()
 
 
-def main_kernel(tiles, rows_dev, where_ref, rows_ref, norm_ref, w0_ref, wc_ref, wn_ref, nug_ref, inv_ref, q_ref, l_ref, o_ref):
+def main_kernel(tiles, rows_dev, where_ref, rows_ref, norm_ref, w0_ref, wc_ref, wn_ref, nug_ref, q_ref, l_ref, o_ref):
     step = pl.program_id(0)
     row, col = where_ref[0], where_ref[1]
     eye = lax.broadcasted_iota(jnp.int32, (NB, NB), 0) == lax.broadcasted_iota(jnp.int32, (NB, NB), 1)
@@ -208,20 +210,14 @@
         kern = jnp.exp(-0.5 * (norms + wn_ref[...] - 2.0 * cross))
         left = kern[:, :NB] + jnp.where(eye & (tile == 0), nug_ref[:, :NB], 0.0)
         high, low = halves(left)
-        panel = lax.dot_general(
-            jnp.concatenate([high, high, low], axis=1), inv_ref[...], NN, preferred_element_type=jnp.float32
-        )
-        high, low = halves(panel)
-        update = lax.dot_general(
-            jnp.concatenate([high, high, low], axis=1), q_ref[...], NN, preferred_element_type=jnp.float32
-        )
+        update = dot_fast(jnp.concatenate([high, high, low], axis=1), q_ref[...], NN)
         first_tile = tile == 0
         for u in range(2):
             part = slice(NB * (u + 1), NB * (u + 2))
             own = kern[:, part] + jnp.where(eye & (tile == col + 32 * u), nug_ref[:, part], 0.0)
             result = jnp.where(first_tile, own, own - update[:, NB * u : NB * (u + 1)])
             if u == 0:
-                result = jnp.where(col == 0, jnp.where(first_tile, l_ref[...], panel), result)
+                result = jnp.where(col == 0, jnp.where(first_tile, l_ref[...], update[:, :NB]), result)
             for half in range(2):
                 o_ref[pl.ds(n * NB * 4 + 2 * u + half, NB, stride=4), :] = result[:, 128 * half : 128 * (half + 1)]
 
@@ -290,12 +286,11 @@
     cols = [got[: NB // 2, : 2 * quarter], got[NB // 2 :, : 2 * quarter]]
     below = [lax.ppermute(value, "row", up) for value in cols]
     above = [lax.ppermute(value, "row", down) for value in cols]
-    scaled0, norms0, corner, inverse, inverse3 = pl.pallas_call(
+    scaled0, norms0, corner, inverse = pl.pallas_call(
         corner_kernel,
-        out_shape=(shape((NB, features), bf16), shape((1, NB), f32), shape((NB, NB), f32), shape((NB, NB), f32),
-                   shape((3 * NB, NB), bf16)),
+        out_shape=(shape((NB, features), bf16), shape((1, NB), f32), shape((NB, NB), f32), shape((NB, NB), f32)),
         in_specs=[SMEM] + [HBM] * 2 + [VMEM] * 2,
-        out_specs=(VMEM,) * 5,
+        out_specs=(VMEM,) * 4,
         scratch_shapes=[pltpu.VMEM((NB, features), bf16), pltpu.VMEM((NB, NB), f32), pltpu.SemaphoreType.DMA((8,))],
         cost_estimate=SMALL,
         compiler_params=pltpu.CompilerParams(vmem_limit_bytes=GRANT),
@@ -326,7 +321,7 @@
         compiler_params=limit,
     )(where, *cols_far, weight_row, scaled0, norms0, inverse, norms_c, cross_c, scaled)
 
-    fixed = (scaled0, scaled, wn, nug, inverse3, q_panel, corner)
+    fixed = (scaled0, scaled, wn, nug, q_panel, corner)
 
     def whole(value):
         return pl.BlockSpec(value.shape, lambda i, _: (0, 0), pipeline_mode=pl.Buffered(1))

time: 182 us -> 181 us (level)
  local copies, waits for them, and re-layouts: 10.8 us -> 14.3 us
  waiting for transfers between devices: 58.4 us -> 55.2 us
    unnamed x25 -> x23, local copies, waits for them, and re-layouts: 3.63 us -> 7.41 us
    pallas_call x1, Pallas kernels: 40.2 us -> 37.9 us  [local(): pl.pallas_call(functools.partial(main_kernel, tiles, 4), out_shape=shape(...]
  transfers between devices with their start and end apart: 16 -> 16, of which waited for: 9 -> 8; matrix products, arithmetic and copies ran while one was open for 6% -> 8% of each run, Pallas kernels for 17% -> 18%
where the time goes in v7:
time: 181 us; the launch traced here: 180 us
  Pallas kernels  69.7 us (39%)
  waiting for transfers between devices  55.2 us (30%)
  starting transfers between devices  25.9 us (14%)
  local copies, waits for them, and re-layouts  14.3 us (8%)
  between operations  13.7 us (8%)
    pallas_call x1, Pallas kernels, local(): pl.pallas_call(functools.partial(main_kernel, tiles, 4), out_shape=shape(...  37.9 us
    all_to_all x1, waiting for transfers between devices, local(): got = lax.all_to_all(payload, 'col', 0, 0)  26.7 us
    pallas_call x1, Pallas kernels, local(): pl.pallas_call(corner_kernel, out_shape=(shape((NB, features), bf16), sha...  18.8 us
    all_to_all x1, waiting for transfers between devices, local(): sent = lax.all_to_all(jnp.concatenate([cut, extra], axis=3), 'row', 0, 0)  15.9 us
    unnamed x23, local copies, waits for them, and re-layouts  7.41 us
    all_to_all x1, starting transfers between devices, local(): got = lax.all_to_all(payload, 'col', 0, 0)  7.32 us
    pallas_call x1, Pallas kernels, local(): pl.pallas_call(column_kernel, out_shape=(near, shape((2 * NB, 1), f32), s...  7.03 us
    ppermute x2, waiting for transfers between devices, local(): lax.ppermute(below[0], 'row', up)  5.94 us
  transfers between devices with their start and end apart: 16, of which 8 were waited for; matrix products, arithmetic and copies ran while one was open for 8% of the time, Pallas kernels for 18%

profile of v7, /device:TPU:0, one launch (start us, length us, event | category | flops | bytes accessed | tf_op | source)
XLA Modules:
  0.0 180.4 jit_solution(4088115331976458708)
XLA Ops:
  6.5 0.7 all-gather.2.cloned.1.call-update
  7.3 0.5 copy-done
  7.8 0.8 reshape_reshape.3
  8.6 0.1 copy.55
  8.6 0.2 broadcast_in_dim.35
  8.9 0.6 pad_maximum_fusion
  9.4 1.1 copy.56
  10.6 5.5 %all-to-all-start = ((bf16[4,16,8,1152]{3,2,1,0:T(8,128)(2,1)}), bf16[4,16,8,1152]{3,2,1,0:T(8,128)(2,1)S(1)}, u32[]{:S(2)}, u32[]{:S(2)}) async-start(bf16[4,16,8,1152]{3,2,1,0:T(8,128)(2,1)} %copy.56), calls=%async_computation | async-start | bytes 2359296 | tf_op jit(solution)/shard_map/all_to_all | solution.py:249
  16.1 0.4 fusion
  16.5 0.1 copy.59
  16.6 0.1 broadcast_in_dim.40
  16.6 15.9 %all-to-all-done = bf16[4,16,8,1152]{3,2,1,0:T(8,128)(2,1)S(1)} async-done(((bf16[4,16,8,1152]{3,2,1,0:T(8,128)(2,1)}), bf16[4,16,8,1152]{3,2,1,0:T(8,128)(2,1)S(1)}, u32[]{:S(2)}, u32[]{:S(2)}) %all-to-all-start) | async-done | bytes 1179680 | tf_op jit(solution)/shard_map/all_to_all | solution.py:249
  32.6 0.1 copy.57
  32.7 0.2 copy.58
  32.9 0.2 copy.62
  33.1 0.2 copy.61
  33.2 0.1 slice_reduce_fusion
  33.4 0.1 slice_bitcast_fusion
  33.5 0.1 broadcast_in_dim.38
  33.7 1.9 %concatenate.10 = bf16[32,8,2688]{2,1,0:T(8,128)(2,1)} concatenate(bf16[32,8,1024]{2,1,0:T(8,128)(2,1)S(1)} %get-tuple-element.48, bf16[32,8,1024]{2,1,0:T(8,128)(2,1)S(1)} %get-tuple-element.47, bf16[32,8,512]{2,1,0:T(8,128)(2,1)S(1)} %bitcast.65, bf16[32,8,1]{2,1,0:T(8,128)(2,1)S(1)} %broadcast_in_dim.38, bf16[32,8,1]{2,1,0:T(8,128)(2,1)S(1)} %copy.61, ...), dimensions={2} | concatenate | bytes 2752512 | tf_op jit(solution)/shard_map/concatenate | solution.py:264
  35.6 7.3 %all-to-all-start.1 = ((bf16[32,8,2688]{2,1,0:T(8,128)(2,1)}), bf16[32,8,2688]{2,1,0:T(8,128)(2,1)S(1)}, u32[]{:S(2)}, u32[]{:S(2)}) async-start(bf16[32,8,2688]{2,1,0:T(8,128)(2,1)} %concatenate.10), calls=%async_computation.1 | async-start | bytes 2752512 | tf_op jit(solution)/shard_map/all_to_all | solution.py:265
  42.9 26.7 %all-to-all-done.1 = bf16[32,8,2688]{2,1,0:T(8,128)(2,1)S(1)} async-done(((bf16[32,8,2688]{2,1,0:T(8,128)(2,1)}), bf16[32,8,2688]{2,1,0:T(8,128)(2,1)S(1)}, u32[]{:S(2)}, u32[]{:S(2)}) %all-to-all-start.1) | async-done | bytes 1376288 | tf_op jit(solution)/shard_map/all_to_all | solution.py:265
  69.6 0.1 collective-permute-start.3
  69.6 2.0 %collective-permute-start.1 = (bf16[128,512]{1,0:T(8,128)(2,1)S(1)}, bf16[128,512]{1,0:T(8,128)(2,1)S(1)}, u32[]{:S(2)}, u32[]{:S(2)}) collective-permute-start(bf16[128,512]{1,0:T(8,128)(2,1)S(1)} %get-tuple-element.43), channel_id=1, source_target_pairs={{0,32},{32,64},{64,96},{96,0},{1,33},{33,65},{65,97},{97,1},{2,34}... | collective-permute-start | bytes 393224 | tf_op jit(solution)/shard_map/ppermute | solution.py:279
  71.7 1.3 collective-permute-start.2
  73.0 0.7 collective-permute-start
  73.7 0.7 slice_dynamic-update-slice_fusion
  74.4 0.9 collective-permute-done.3
  75.4 1.6 collective-permute-start.5
  76.9 2.2 %collective-permute-done = bf16[128,512]{1,0:T(8,128)(2,1)S(1)} collective-permute-done((bf16[128,512]{1,0:T(8,128)(2,1)S(1)}, bf16[128,512]{1,0:T(8,128)(2,1)S(1)}, u32[]{:S(2)}, u32[]{:S(2)}) %collective-permute-start) | collective-permute-done | bytes 131104 | tf_op jit(solution)/shard_map/ppermute | solution.py:279
  79.1 0.0 collective-permute-start.4
  79.1 0.7 constant_dynamic-update-slice_fusion.5
  79.8 0.7 constant_dynamic-update-slice_fusion.4
  80.5 0.7 constant_dynamic-update-slice_fusion.3
  81.1 0.7 constant_dynamic-update-slice_fusion.2
  81.8 0.0 collective-permute-done.5
  81.8 3.5 %collective-permute-done.4 = bf16[128,512]{1,0:T(8,128)(2,1)S(1)} collective-permute-done((bf16[128,512]{1,0:T(8,128)(2,1)S(1)}, bf16[128,512]{1,0:T(8,128)(2,1)S(1)}, u32[]{:S(2)}, u32[]{:S(2)}) %collective-permute-start.4) | collective-permute-done | bytes 131104 | tf_op jit(solution)/shard_map/ppermute | solution.py:281
  85.3 0.7 constant_dynamic-update-slice_fusion.1
  86.0 0.7 constant_dynamic-update-slice_fusion.mine_ref
  86.6 0.0 collective-permute-start.6
  86.6 0.1 fusion.3
  86.8 0.1 collective-permute-start.10
  86.9 2.0 %collective-permute-start.8 = (bf16[128,2048]{1,0:T(8,128)(2,1)S(1)}, bf16[128,2048]{1,0:T(8,128)(2,1)}, u32[]{:S(2)}, u32[]{:S(2)}) collective-permute-start(bf16[128,2048]{1,0:T(8,128)(2,1)S(1)} %get-tuple-element.41.own1_ref), channel_id=1, source_target_pairs={{0,32},{32,64},{64,96},{96,0},{1,33},{33,65},{65,97},{97,1},{2,34}... | collective-permute-start | bytes 1572872 | tf_op jit(solution)/shard_map/ppermute | solution.py:287
  88.9 1.3 collective-permute-start.9
  90.2 0.7 collective-permute-start.7
  90.9 0.6 pad_add_fusion.where_ref
  91.5 0.1 copy.64
  91.6 0.6 slice.102.nug_ref
  92.2 18.8 %shard_map.37 = (bf16[256,4096]{1,0:T(8,128)(2,1)}, f32[1,256]{1,0:T(1,128)}, f32[256,256]{1,0:T(8,128)}, f32[256,256]{1,0:T(8,128)}) custom-call(s32[2]{0:T(128)} %pad_add_fusion.where_ref, bf16[1024,512]{1,0:T(8,128)(2,1)} %constant_dynamic-update-slice_fusion.mine_ref, bf16[1024,512]{1,0:T(8,128)(2,1)} %collective-permute-done.6.theirs_ref, ...), custom_call_target="tpu_custom_call" | custom-call | flops 1 | bytes 1 | tf_op jit(solution)/shard_map/pallas_call | solution.py:289
  111.0 0.0 collective-permute-done.8.below1_ref
  111.1 1.5 collective-permute-done.9.above0_ref
  112.5 1.3 collective-permute-done.7.below0_ref
  113.8 0.5 collective-permute-start.11
  114.3 2.8 %collective-permute-start.12 = (bf16[128,2048]{1,0:T(8,128)(2,1)}, bf16[128,2048]{1,0:T(8,128)(2,1)}, u32[]{:S(2)}, u32[]{:S(2)}) collective-permute-start(bf16[128,2048]{1,0:T(8,128)(2,1)} %collective-permute-done.10.above1_ref), channel_id=1, source_target_pairs={{0,96},{32,0},{64,32},{96,64},{1,97},{33,1},{65,33},{97,65},{2,98}... | collective-permute-start | bytes 1572872 | tf_op jit(solution)/shard_map/ppermute | solution.py:299
  117.1 0.1 slice.94
  117.2 0.1 copy.63
  117.3 2.0 %copy.68 = f32[1,4096]{0,1:T(8,128)} copy(f32[1,4096]{1,0:T(1,128)S(1)} %bitcast.70) | data formatting | bytes 32768
  119.3 7.0 %shard_map.38 = (bf16[512,4096]{1,0:T(8,128)(2,1)}, f32[512,1]{1,0:T(8,128)}, f32[512,256]{1,0:T(8,128)}) custom-call(s32[2]{0:T(128)} %pad_add_fusion.where_ref, bf16[128,2048]{1,0:T(8,128)(2,1)} %copy-done.2, bf16[128,2048]{1,0:T(8,128)(2,1)} %copy-done.1, bf16[128,2048]{1,0:T(8,128)(2,1)} %collective-permute-done.7.below0_ref, ...), custom_call_target="tpu_custom_call" | custom-call | flops 1 | bytes 1 | tf_op jit(solution)/shard_map/pallas_call | solution.py:302
  126.4 2.4 %collective-permute-done.11.far0_ref = bf16[128,2048]{1,0:T(8,128)(2,1)S(1)} collective-permute-done((bf16[128,2048]{1,0:T(8,128)(2,1)}, bf16[128,2048]{1,0:T(8,128)(2,1)S(1)}, u32[]{:S(2)}, u32[]{:S(2)}) %collective-permute-start.11) | collective-permute-done | bytes 524320 | tf_op jit(solution)/shard_map/ppermute | solution.py:299
  128.8 0.0 collective-permute-done.12.far1_ref
  128.8 0.8 copy-done.3
  129.6 5.9 %shard_map.39 = (bf16[512,4096]{1,0:T(8,128)(2,1)}, f32[1,768]{1,0:T(1,128)}, bf16[768,512]{1,0:T(8,128)(2,1)}) custom-call(s32[2]{0:T(128)} %pad_add_fusion.where_ref, bf16[128,2048]{1,0:T(8,128)(2,1)} %copy-done.3, bf16[128,2048]{1,0:T(8,128)(2,1)} %collective-permute-done.12.far1_ref, f32[1,4096]{1,0:T(1,128)} %bitcast.68, ...), custom_call_target="tpu_custom_call", output_to_operand_aliasing={{0}: (9, {})} | custom-call | flops 1 | bytes 1 | tf_op jit(solution)/shard_map/pallas_call | solution.py:312
  135.6 0.0 all-gather.2.cloned.1.call-done
  135.6 37.9 %shard_map.40 = f32[16384,128]{1,0:T(8,128)} custom-call(s32[2]{0:T(128)} %pad_add_fusion.where_ref, bf16[4096,4096]{1,0:T(8,128)(2,1)} %bitcast.77, f32[4096,1]{1,0:T(8,128)} %bitcast.64, bf16[256,4096]{1,0:T(8,128)(2,1)} %get-tuple-element.25.scaled0_ref.w0_ref, bf16[512,4096]{1,0:T(8,128)(2,1)} %get-tuple-element.37.wc_ref, ...), custom_call_target="tpu_custom_call" | custom-call | flops 30000001024 | bytes 50331648 | tf_op jit(solution)/shard_map/pallas_call | solution.py:331
  (34 shorter events, 0.2 us)
Async XLA Ops:
  6.5 1.2 copy-start
  6.5 2.0 %copy-start.6 = (bf16[16,1,1,8]{0,3,2,1:T(8,128)(2,1)S(1)}, bf16[16,1,1,8]{0,3,2,1:T(8,128)(2,1)}, u32[]{:S(2)}) copy-start(bf16[16,1,1,8]{0,3,2,1:T(8,128)(2,1)} %param.5) | copy-start | bytes 772
  6.5 129.0 %all-gather.2.cloned.1.call-start = ((), (), s32[]{:S(2)}) async-start(), calls=%async_computation.2 | async-start | bytes 34603008 | tf_op jit(solution)/shard_map/all_gather | solution.py:238
  10.6 5.5 %copy-start.4 = (f32[4096]{0:T(1024)S(1)}, f32[4096]{0:T(1024)}, u32[]{:S(2)}) copy-start(f32[4096]{0:T(1024)} %param.4) | copy-start | bytes 49156
  10.6 22.0 %all-to-all-start = ((bf16[4,16,8,1152]{3,2,1,0:T(8,128)(2,1)}), bf16[4,16,8,1152]{3,2,1,0:T(8,128)(2,1)S(1)}, u32[]{:S(2)}, u32[]{:S(2)}) async-start(bf16[4,16,8,1152]{3,2,1,0:T(8,128)(2,1)} %copy.56), calls=%async_computation | async-start | bytes 2359296 | tf_op jit(solution)/shard_map/all_to_all | solution.py:249
  35.6 34.0 %all-to-all-start.1 = ((bf16[32,8,2688]{2,1,0:T(8,128)(2,1)}), bf16[32,8,2688]{2,1,0:T(8,128)(2,1)S(1)}, u32[]{:S(2)}, u32[]{:S(2)}) async-start(bf16[32,8,2688]{2,1,0:T(8,128)(2,1)} %concatenate.10), calls=%async_computation.1 | async-start | bytes 2752512 | tf_op jit(solution)/shard_map/all_to_all | solution.py:265
  69.6 5.8 %collective-permute-start.3 = (bf16[128,512]{1,0:T(8,128)(2,1)S(1)}, bf16[128,512]{1,0:T(8,128)(2,1)S(1)}, u32[]{:S(2)}, u32[]{:S(2)}) collective-permute-start(bf16[128,512]{1,0:T(8,128)(2,1)S(1)} %get-tuple-element.43), channel_id=1, source_target_pairs={{0,96},{32,0},{64,32},{96,64},{1,97},{33,1},{65,33},{97,65},{2,98}... | collective-permute-start | bytes 393224 | tf_op jit(solution)/shard_map/ppermute | solution.py:280
  69.6 10.2 %collective-permute-start.1 = (bf16[128,512]{1,0:T(8,128)(2,1)S(1)}, bf16[128,512]{1,0:T(8,128)(2,1)S(1)}, u32[]{:S(2)}, u32[]{:S(2)}) collective-permute-start(bf16[128,512]{1,0:T(8,128)(2,1)S(1)} %get-tuple-element.43), channel_id=1, source_target_pairs={{0,32},{32,64},{64,96},{96,0},{1,33},{33,65},{65,97},{97,1},{2,34}... | collective-permute-start | bytes 393224 | tf_op jit(solution)/shard_map/ppermute | solution.py:279
  71.7 8.8 %collective-permute-start.2 = (bf16[128,512]{1,0:T(8,128)(2,1)S(1)}, bf16[128,512]{1,0:T(8,128)(2,1)S(1)}, u32[]{:S(2)}, u32[]{:S(2)}) collective-permute-start(bf16[128,512]{1,0:T(8,128)(2,1)S(1)} %get-tuple-element.44), channel_id=1, source_target_pairs={{0,96},{32,0},{64,32},{96,64},{1,97},{33,1},{65,33},{97,65},{2,98}... | collective-permute-start | bytes 393224 | tf_op jit(solution)/shard_map/ppermute | solution.py:280
  73.0 6.2 %collective-permute-start = (bf16[128,512]{1,0:T(8,128)(2,1)S(1)}, bf16[128,512]{1,0:T(8,128)(2,1)S(1)}, u32[]{:S(2)}, u32[]{:S(2)}) collective-permute-start(bf16[128,512]{1,0:T(8,128)(2,1)S(1)} %get-tuple-element.44), channel_id=1, source_target_pairs={{0,32},{32,64},{64,96},{96,0},{1,33},{33,65},{65,97},{97,1},{2,34}... | collective-permute-start | bytes 393224 | tf_op jit(solution)/shard_map/ppermute | solution.py:279
  75.4 6.5 %collective-permute-start.5 = (bf16[128,512]{1,0:T(8,128)(2,1)S(1)}, bf16[128,512]{1,0:T(8,128)(2,1)S(1)}, u32[]{:S(2)}, u32[]{:S(2)}) collective-permute-start(bf16[128,512]{1,0:T(8,128)(2,1)S(1)} %collective-permute-done.3), channel_id=1, source_target_pairs={{0,96},{32,0},{64,32},{96,64},{1,97},{33,1},{65,33},{97,65},{2,98}... | collective-permute-start | bytes 393224 | tf_op jit(solution)/shard_map/ppermute | solution.py:281
  79.1 6.2 %collective-permute-start.4 = (bf16[128,512]{1,0:T(8,128)(2,1)S(1)}, bf16[128,512]{1,0:T(8,128)(2,1)S(1)}, u32[]{:S(2)}, u32[]{:S(2)}) collective-permute-start(bf16[128,512]{1,0:T(8,128)(2,1)S(1)} %collective-permute-done), channel_id=1, source_target_pairs={{0,32},{32,64},{64,96},{96,0},{1,33},{33,65},{65,97},{97,1},{2,34}... | collective-permute-start | bytes 393224 | tf_op jit(solution)/shard_map/ppermute | solution.py:281
  86.6 5.6 %collective-permute-start.6 = (bf16[1024,512]{1,0:T(8,128)(2,1)}, bf16[1024,512]{1,0:T(8,128)(2,1)}, u32[]{:S(2)}, u32[]{:S(2)}) collective-permute-start(bf16[1024,512]{1,0:T(8,128)(2,1)} %constant_dynamic-update-slice_fusion.mine_ref), channel_id=1, source_target_pairs={{0,1},{1,0},{2,3},{3,2},{4,5},{5,4},{6,7},{7,6},{8,9},{9,8},{10,11... | collective-permute-start | bytes 3145736 | tf_op jit(solution)/shard_map/ppermute | solution.py:284
  86.8 30.4 %copy-start.1 = (bf16[128,2048]{1,0:T(8,128)(2,1)}, bf16[128,2048]{1,0:T(8,128)(2,1)S(1)}, u32[]{:S(2)}) copy-start(bf16[128,2048]{1,0:T(8,128)(2,1)S(1)} %get-tuple-element.41.own1_ref) | copy-start | bytes 1572868
  86.8 30.4 %copy-start.2 = (bf16[128,2048]{1,0:T(8,128)(2,1)}, bf16[128,2048]{1,0:T(8,128)(2,1)S(1)}, u32[]{:S(2)}) copy-start(bf16[128,2048]{1,0:T(8,128)(2,1)S(1)} %get-tuple-element.42.own0_ref) | copy-start | bytes 1572868
  86.8 24.2 %collective-permute-start.10 = (bf16[128,2048]{1,0:T(8,128)(2,1)S(1)}, bf16[128,2048]{1,0:T(8,128)(2,1)}, u32[]{:S(2)}, u32[]{:S(2)}) collective-permute-start(bf16[128,2048]{1,0:T(8,128)(2,1)S(1)} %get-tuple-element.41.own1_ref), channel_id=1, source_target_pairs={{0,96},{32,0},{64,32},{96,64},{1,97},{33,1},{65,33},{97,65},{2,98}... | collective-permute-start | bytes 1572872 | tf_op jit(solution)/shard_map/ppermute | solution.py:288
  86.9 24.2 %collective-permute-start.8 = (bf16[128,2048]{1,0:T(8,128)(2,1)S(1)}, bf16[128,2048]{1,0:T(8,128)(2,1)}, u32[]{:S(2)}, u32[]{:S(2)}) collective-permute-start(bf16[128,2048]{1,0:T(8,128)(2,1)S(1)} %get-tuple-element.41.own1_ref), channel_id=1, source_target_pairs={{0,32},{32,64},{64,96},{96,0},{1,33},{33,65},{65,97},{97,1},{2,34}... | collective-permute-start | bytes 1572872 | tf_op jit(solution)/shard_map/ppermute | solution.py:287
  88.9 23.6 %collective-permute-start.9 = (bf16[128,2048]{1,0:T(8,128)(2,1)S(1)}, bf16[128,2048]{1,0:T(8,128)(2,1)}, u32[]{:S(2)}, u32[]{:S(2)}) collective-permute-start(bf16[128,2048]{1,0:T(8,128)(2,1)S(1)} %get-tuple-element.42.own0_ref), channel_id=1, source_target_pairs={{0,96},{32,0},{64,32},{96,64},{1,97},{33,1},{65,33},{97,65},{2,98}... | collective-permute-start | bytes 1572872 | tf_op jit(solution)/shard_map/ppermute | solution.py:288
  90.2 23.6 %collective-permute-start.7 = (bf16[128,2048]{1,0:T(8,128)(2,1)S(1)}, bf16[128,2048]{1,0:T(8,128)(2,1)}, u32[]{:S(2)}, u32[]{:S(2)}) collective-permute-start(bf16[128,2048]{1,0:T(8,128)(2,1)S(1)} %get-tuple-element.42.own0_ref), channel_id=1, source_target_pairs={{0,32},{32,64},{64,96},{96,0},{1,33},{33,65},{65,97},{97,1},{2,34}... | collective-permute-start | bytes 1572872 | tf_op jit(solution)/shard_map/ppermute | solution.py:287
  91.6 27.7 %copy-start.5 = (f32[1,1,3,256]{3,1,2,0:T(1,128)}, f32[1,1,3,256]{3,1,2,0:T(1,128)S(1)}, u32[]{:S(2)}) copy-start(f32[1,1,3,256]{3,1,2,0:T(1,128)S(1)} %copy.69) | copy-start | bytes 9220
  113.8 15.0 %collective-permute-start.11 = (bf16[128,2048]{1,0:T(8,128)(2,1)}, bf16[128,2048]{1,0:T(8,128)(2,1)S(1)}, u32[]{:S(2)}, u32[]{:S(2)}) collective-permute-start(bf16[128,2048]{1,0:T(8,128)(2,1)} %collective-permute-done.7.below0_ref), channel_id=1, source_target_pairs={{0,32},{32,64},{64,96},{96,0},{1,33},{33,65},{65,97},{97,1},{2,34}... | collective-permute-start | bytes 1572872 | tf_op jit(solution)/shard_map/ppermute | solution.py:299
  114.3 14.5 %collective-permute-start.12 = (bf16[128,2048]{1,0:T(8,128)(2,1)}, bf16[128,2048]{1,0:T(8,128)(2,1)}, u32[]{:S(2)}, u32[]{:S(2)}) collective-permute-start(bf16[128,2048]{1,0:T(8,128)(2,1)} %collective-permute-done.10.above1_ref), channel_id=1, source_target_pairs={{0,96},{32,0},{64,32},{96,64},{1,97},{33,1},{65,33},{97,65},{2,98}... | collective-permute-start | bytes 1572872 | tf_op jit(solution)/shard_map/ppermute | solution.py:299
  128.8 0.8 copy-start.3
Sparse Core Ops, SparseCore 0:
  9.7 122.5 all-gather.1

commit v8 on v7

--- a/solution.py
+++ b/solution.py
@@ -118,7 +118,7 @@
 
 
 def corner_kernel(where_ref, mine_ref, theirs_ref, weight_ref, nug_ref,
-                  scaled_ref, norm_ref, l_ref, x_ref, raw_ref, a_ref, sem):
+                  scaled_ref, norm_ref, l_ref, x_ref, turned_ref, raw_ref, a_ref, sem):
     eighth = mine_ref.shape[1]
     quarter = 2 * eighth
     core = lax.rem(where_ref[1], 2)
@@ -145,6 +145,7 @@
     tile = jnp.exp(-0.5 * (norms + row_norms - 2.0 * cross)) + jnp.where(eye, nug_ref[...], 0.0)
     a_ref[...] = 0.5 * (tile + tile.T)
     store_factor(a_ref, l_ref, x_ref)
+    turned_ref[...] = x_ref[...].T
 
 
 def column_kernel(where_ref, own0_ref, own1_ref, below0_ref, below1_ref, above0_ref, above1_ref, weight_ref,
@@ -170,7 +171,7 @@
     cross_ref[...] = cross
 
 
-def far_kernel(where_ref, far0_ref, far1_ref, weight_ref, scaled0_ref, norm0_ref, x_ref, part_norm_ref, part_cross_ref,
+def far_kernel(where_ref, far0_ref, far1_ref, weight_ref, scaled0_ref, norm0_ref, x_ref, turned_ref, part_norm_ref, part_cross_ref,
                before_ref, scaled_ref, norm_ref, q_ref, raw_ref, zero_ref, out_ref, sem):
     quarter = far0_ref.shape[1] // 2
     spot = spots(where_ref, quarter)[3]
@@ -191,7 +192,7 @@
     norm_ref[:, :NB] = norm0_ref[...]
     norm_ref[:, NB:] = as_row(norms)
     kern = jnp.exp(-0.5 * (norms + norm0_ref[...] - 2.0 * cross))
-    turned = x_ref[...].T
+    turned = turned_ref[...]
     solved = dot_high(turned, dot_high(x_ref[...], kern, NT))
     store_triple(q_ref, jnp.concatenate(
         [jnp.where(where_ref[1] == 0, turned, solved[:, :NB]), solved[:, NB:]], axis=1))
@@ -286,11 +287,12 @@
     cols = [got[: NB // 2, : 2 * quarter], got[NB // 2 :, : 2 * quarter]]
     below = [lax.ppermute(value, "row", up) for value in cols]
     above = [lax.ppermute(value, "row", down) for value in cols]
-    scaled0, norms0, corner, inverse = pl.pallas_call(
+    scaled0, norms0, corner, inverse, turned = pl.pallas_call(
         corner_kernel,
-        out_shape=(shape((NB, features), bf16), shape((1, NB), f32), shape((NB, NB), f32), shape((NB, NB), f32)),
+        out_shape=(shape((NB, features), bf16), shape((1, NB), f32), shape((NB, NB), f32), shape((NB, NB), f32),
+                   shape((NB, NB), f32)),
         in_specs=[SMEM] + [HBM] * 2 + [VMEM] * 2,
-        out_specs=(VMEM,) * 4,
+        out_specs=(VMEM,) * 5,
         scratch_shapes=[pltpu.VMEM((NB, features), bf16), pltpu.VMEM((NB, NB), f32), pltpu.SemaphoreType.DMA((8,))],
         cost_estimate=SMALL,
         compiler_params=pltpu.CompilerParams(vmem_limit_bytes=GRANT),
@@ -312,14 +314,14 @@
     scaled, wn, q_panel = pl.pallas_call(
         far_kernel,
         out_shape=(near, shape((1, 3 * NB), f32), shape((3 * NB, 2 * NB), bf16)),
-        in_specs=[SMEM] + [HBM] * 2 + [VMEM, HBM] + [VMEM] * 4 + [HBM],
+        in_specs=[SMEM] + [HBM] * 2 + [VMEM, HBM] + [VMEM] * 5 + [HBM],
         out_specs=(HBM, VMEM, VMEM),
         scratch_shapes=[pltpu.VMEM((2 * NB, quarter), bf16), pltpu.VMEM((NB, quarter), bf16),
                         pltpu.VMEM((2 * NB, quarter), bf16), pltpu.SemaphoreType.DMA((5,))],
-        input_output_aliases={9: 0},
+        input_output_aliases={10: 0},
         cost_estimate=SMALL,
         compiler_params=limit,
-    )(where, *cols_far, weight_row, scaled0, norms0, inverse, norms_c, cross_c, scaled)
+    )(where, *cols_far, weight_row, scaled0, norms0, inverse, turned, norms_c, cross_c, scaled)
 
     fixed = (scaled0, scaled, wn, nug, q_panel, corner)
 

time: 181 us -> 180 us (level)
  local copies, waits for them, and re-layouts: 14.3 us -> 10.8 us
  waiting for transfers between devices: 55.2 us -> 58.5 us
    unnamed x23 -> x25, local copies, waits for them, and re-layouts: 7.41 us -> 3.63 us
  transfers between devices with their start and end apart: 16 -> 16, of which waited for: 8 -> 9; matrix products, arithmetic and copies ran while one was open for 8% -> 6% of each run, Pallas kernels for 18% -> 18%
where the time goes in v8:
time: 180 us
  Pallas kernels  69.7 us (39%)
  waiting for transfers between devices  58.5 us (32%)
  starting transfers between devices  25.3 us (14%)
  between operations  13.7 us (8%)
  local copies, waits for them, and re-layouts  10.8 us (6%)
    pallas_call x1, Pallas kernels, local(): pl.pallas_call(functools.partial(main_kernel, tiles, 4), out_shape=shape(...  37.9 us
    all_to_all x1, waiting for transfers between devices, local(): got = lax.all_to_all(payload, 'col', 0, 0)  26.7 us
    pallas_call x1, Pallas kernels, local(): pl.pallas_call(corner_kernel, out_shape=(shape((NB, features), bf16), sha...  18.9 us
    all_to_all x1, waiting for transfers between devices, local(): sent = lax.all_to_all(jnp.concatenate([cut, extra], axis=3), 'row', 0, 0)  15.9 us
    all_to_all x1, starting transfers between devices, local(): got = lax.all_to_all(payload, 'col', 0, 0)  7.32 us
    ppermute x2, waiting for transfers between devices, local(): lax.ppermute(below[0], 'row', up)  7.25 us
    pallas_call x1, Pallas kernels, local(): pl.pallas_call(column_kernel, out_shape=(near, shape((2 * NB, 1), f32), s...  7.06 us
    pallas_call x1, Pallas kernels, local(): pl.pallas_call(far_kernel, out_shape=(near, shape((1, 3 * NB), f32), shap...  5.75 us
  transfers between devices with their start and end apart: 16, of which 9 were waited for; matrix products, arithmetic and copies ran while one was open for 6% of the time, Pallas kernels for 18%

profile of v8, /device:TPU:0, one launch (start us, length us, event | category | flops | bytes accessed | tf_op | source)
XLA Modules:
  0.0 179.6 jit_solution(14454590733052815464)
XLA Ops:
  6.5 0.7 all-gather.2.cloned.1.call-update
  7.3 0.5 copy-done
  7.8 0.8 reshape_reshape.3
  8.6 0.0 copy-done.7
  8.6 0.1 copy.55
  8.6 0.2 broadcast_in_dim.35
  8.9 0.6 pad_maximum_fusion
  9.4 1.1 copy.56
  10.6 5.5 %all-to-all-start = ((bf16[4,16,8,1152]{3,2,1,0:T(8,128)(2,1)}), bf16[4,16,8,1152]{3,2,1,0:T(8,128)(2,1)S(1)}, u32[]{:S(2)}, u32[]{:S(2)}) async-start(bf16[4,16,8,1152]{3,2,1,0:T(8,128)(2,1)} %copy.56), calls=%async_computation | async-start | bytes 2359296 | tf_op jit(solution)/shard_map/all_to_all | solution.py:250
  16.1 0.4 fusion
  16.5 0.1 copy.59
  16.6 0.1 broadcast_in_dim.40
  16.6 15.9 %all-to-all-done = bf16[4,16,8,1152]{3,2,1,0:T(8,128)(2,1)S(1)} async-done(((bf16[4,16,8,1152]{3,2,1,0:T(8,128)(2,1)}), bf16[4,16,8,1152]{3,2,1,0:T(8,128)(2,1)S(1)}, u32[]{:S(2)}, u32[]{:S(2)}) %all-to-all-start) | async-done | bytes 1179680 | tf_op jit(solution)/shard_map/all_to_all | solution.py:250
  32.6 0.1 copy.57
  32.7 0.2 copy.58
  32.9 0.2 copy.62
  33.1 0.2 copy.61
  33.2 0.1 slice_reduce_fusion
  33.4 0.1 slice_bitcast_fusion
  33.5 0.1 broadcast_in_dim.38
  33.7 1.9 %concatenate.10 = bf16[32,8,2688]{2,1,0:T(8,128)(2,1)} concatenate(bf16[32,8,1024]{2,1,0:T(8,128)(2,1)S(1)} %get-tuple-element.50, bf16[32,8,1024]{2,1,0:T(8,128)(2,1)S(1)} %get-tuple-element.49, bf16[32,8,512]{2,1,0:T(8,128)(2,1)S(1)} %bitcast.65, bf16[32,8,1]{2,1,0:T(8,128)(2,1)S(1)} %broadcast_in_dim.38, bf16[32,8,1]{2,1,0:T(8,128)(2,1)S(1)} %copy.61, ...), dimensions={2} | concatenate | bytes 2752512 | tf_op jit(solution)/shard_map/concatenate | solution.py:265
  35.6 7.3 %all-to-all-start.1 = ((bf16[32,8,2688]{2,1,0:T(8,128)(2,1)}), bf16[32,8,2688]{2,1,0:T(8,128)(2,1)S(1)}, u32[]{:S(2)}, u32[]{:S(2)}) async-start(bf16[32,8,2688]{2,1,0:T(8,128)(2,1)} %concatenate.10), calls=%async_computation.1 | async-start | bytes 2752512 | tf_op jit(solution)/shard_map/all_to_all | solution.py:266
  42.9 26.7 %all-to-all-done.1 = bf16[32,8,2688]{2,1,0:T(8,128)(2,1)S(1)} async-done(((bf16[32,8,2688]{2,1,0:T(8,128)(2,1)}), bf16[32,8,2688]{2,1,0:T(8,128)(2,1)S(1)}, u32[]{:S(2)}, u32[]{:S(2)}) %all-to-all-start.1) | async-done | bytes 1376288 | tf_op jit(solution)/shard_map/all_to_all | solution.py:266
  69.6 0.1 collective-permute-start.3
  69.6 2.0 %collective-permute-start.1 = (bf16[128,512]{1,0:T(8,128)(2,1)S(1)}, bf16[128,512]{1,0:T(8,128)(2,1)S(1)}, u32[]{:S(2)}, u32[]{:S(2)}) collective-permute-start(bf16[128,512]{1,0:T(8,128)(2,1)S(1)} %get-tuple-element.45), channel_id=1, source_target_pairs={{0,32},{32,64},{64,96},{96,0},{1,33},{33,65},{65,97},{97,1},{2,34}... | collective-permute-start | bytes 393224 | tf_op jit(solution)/shard_map/ppermute | solution.py:280
  71.7 1.3 collective-permute-start.2
  73.0 0.7 collective-permute-start
  73.7 1.6 collective-permute-done.3
  75.4 1.0 collective-permute-start.5
  76.3 2.8 %collective-permute-done = bf16[128,512]{1,0:T(8,128)(2,1)S(1)} collective-permute-done((bf16[128,512]{1,0:T(8,128)(2,1)S(1)}, bf16[128,512]{1,0:T(8,128)(2,1)S(1)}, u32[]{:S(2)}, u32[]{:S(2)}) %collective-permute-start) | collective-permute-done | bytes 131104 | tf_op jit(solution)/shard_map/ppermute | solution.py:280
  79.1 0.0 collective-permute-start.4
  79.1 0.0 collective-permute-done.1
  79.2 0.0 collective-permute-done.2
  79.2 1.1 collective-permute-done.5
  80.3 5.0 %collective-permute-done.4 = bf16[128,512]{1,0:T(8,128)(2,1)S(1)} collective-permute-done((bf16[128,512]{1,0:T(8,128)(2,1)S(1)}, bf16[128,512]{1,0:T(8,128)(2,1)S(1)}, u32[]{:S(2)}, u32[]{:S(2)}) %collective-permute-start.4) | collective-permute-done | bytes 131104 | tf_op jit(solution)/shard_map/ppermute | solution.py:282
  85.3 0.0 copy-start.2
  85.4 0.1 collective-permute-start.6
  85.5 1.0 fusion.3
  86.5 0.0 collective-permute-start.10
  86.5 2.0 %collective-permute-start.8 = (bf16[128,2048]{1,0:T(8,128)(2,1)S(1)}, bf16[128,2048]{1,0:T(8,128)(2,1)}, u32[]{:S(2)}, u32[]{:S(2)}) collective-permute-start(bf16[128,2048]{1,0:T(8,128)(2,1)S(1)} %get-tuple-element.43.own1_ref), channel_id=1, source_target_pairs={{0,32},{32,64},{64,96},{96,0},{1,33},{33,65},{65,97},{97,1},{2,34}... | collective-permute-start | bytes 1572872 | tf_op jit(solution)/shard_map/ppermute | solution.py:288
  88.5 1.2 collective-permute-start.9
  89.7 0.8 collective-permute-start.7
  90.6 0.6 pad_add_fusion.where_ref
  91.2 0.1 copy.64
  91.3 0.6 slice.102.nug_ref
  91.9 0.0 collective-permute-done.6.theirs_ref
  91.9 18.9 %shard_map.37 = (bf16[256,4096]{1,0:T(8,128)(2,1)}, f32[1,256]{1,0:T(1,128)}, f32[256,256]{1,0:T(8,128)}, f32[256,256]{1,0:T(8,128)}, f32[256,256]{1,0:T(8,128)}) custom-call(s32[2]{0:T(128)} %pad_add_fusion.where_ref, bf16[1024,512]{1,0:T(8,128)(2,1)} %copy-done.2, bf16[1024,512]{1,0:T(8,128)(2,1)} %collective-permute-done.6.theirs_ref, ...), custom_call_target="tpu_custom_call" | custom-call | flops 1 | bytes 1 | tf_op jit(solution)/shard_map/pallas_call | solution.py:290
  110.8 0.0 collective-permute-done.10.above1_ref
  110.8 0.0 collective-permute-done.8.below1_ref
  110.8 1.2 collective-permute-done.9.above0_ref
  112.0 1.2 collective-permute-done.7.below0_ref
  113.3 0.5 collective-permute-start.11
  113.8 2.7 %collective-permute-start.12 = (bf16[128,2048]{1,0:T(8,128)(2,1)}, bf16[128,2048]{1,0:T(8,128)(2,1)S(1)}, u32[]{:S(2)}, u32[]{:S(2)}) collective-permute-start(bf16[128,2048]{1,0:T(8,128)(2,1)} %collective-permute-done.10.above1_ref), channel_id=1, source_target_pairs={{0,96},{32,0},{64,32},{96,64},{1,97},{33,1},{65,33},{97,65},{2,98}... | collective-permute-start | bytes 1572872 | tf_op jit(solution)/shard_map/ppermute | solution.py:301
  116.5 0.1 slice.94
  116.6 0.1 copy.63
  116.7 2.0 %copy.68 = f32[1,4096]{0,1:T(8,128)} copy(f32[1,4096]{1,0:T(1,128)S(1)} %bitcast.70) | data formatting | bytes 32768
  118.7 7.1 %shard_map.38 = (bf16[512,4096]{1,0:T(8,128)(2,1)}, f32[512,1]{1,0:T(8,128)}, f32[512,256]{1,0:T(8,128)}) custom-call(s32[2]{0:T(128)} %pad_add_fusion.where_ref, bf16[128,2048]{1,0:T(8,128)(2,1)} %get-tuple-element.44.own0_ref, bf16[128,2048]{1,0:T(8,128)(2,1)} %copy-done.1, bf16[128,2048]{1,0:T(8,128)(2,1)} %collective-permute-done.7.below0_ref, ...), custom_call_target="tpu_custom_call" | custom-call | flops 1 | bytes 1 | tf_op jit(solution)/shard_map/pallas_call | solution.py:304
  125.8 2.3 %collective-permute-done.11.far0_ref = bf16[128,2048]{1,0:T(8,128)(2,1)S(1)} collective-permute-done((bf16[128,2048]{1,0:T(8,128)(2,1)}, bf16[128,2048]{1,0:T(8,128)(2,1)S(1)}, u32[]{:S(2)}, u32[]{:S(2)}) %collective-permute-start.11) | collective-permute-done | bytes 524320 | tf_op jit(solution)/shard_map/ppermute | solution.py:301
  128.1 0.0 collective-permute-done.12.far1_ref
  128.1 0.8 copy-done.3
  128.9 0.2 copy-done.4
  129.1 5.7 %shard_map.39 = (bf16[512,4096]{1,0:T(8,128)(2,1)}, f32[1,768]{1,0:T(1,128)}, bf16[768,512]{1,0:T(8,128)(2,1)}) custom-call(s32[2]{0:T(128)} %pad_add_fusion.where_ref, bf16[128,2048]{1,0:T(8,128)(2,1)} %copy-done.3, bf16[128,2048]{1,0:T(8,128)(2,1)} %copy-done.4, f32[1,4096]{1,0:T(1,128)} %bitcast.68, ...), custom_call_target="tpu_custom_call", output_to_operand_aliasing={{0}: (10, {})} | custom-call | flops 1 | bytes 1 | tf_op jit(solution)/shard_map/pallas_call | solution.py:314
  134.8 0.0 all-gather.2.cloned.1.call-done
  134.8 37.9 %shard_map.40 = f32[16384,128]{1,0:T(8,128)} custom-call(s32[2]{0:T(128)} %pad_add_fusion.where_ref, bf16[4096,4096]{1,0:T(8,128)(2,1)} %bitcast.77, f32[4096,1]{1,0:T(8,128)} %bitcast.64, bf16[256,4096]{1,0:T(8,128)(2,1)} %get-tuple-element.26.scaled0_ref.w0_ref, bf16[512,4096]{1,0:T(8,128)(2,1)} %get-tuple-element.39.wc_ref, ...), custom_call_target="tpu_custom_call" | custom-call | flops 30000001024 | bytes 50331648 | tf_op jit(solution)/shard_map/pallas_call | solution.py:333
  (36 shorter events, 0.3 us)
Async XLA Ops:
  6.5 1.2 copy-start
  6.5 2.0 %copy-start.7 = (bf16[16,1,1,8]{0,3,2,1:T(8,128)(2,1)S(1)}, bf16[16,1,1,8]{0,3,2,1:T(8,128)(2,1)}, u32[]{:S(2)}) copy-start(bf16[16,1,1,8]{0,3,2,1:T(8,128)(2,1)} %param.5) | copy-start | bytes 772
  6.5 128.3 %all-gather.2.cloned.1.call-start = ((), (), s32[]{:S(2)}) async-start(), calls=%async_computation.2 | async-start | bytes 34603008 | tf_op jit(solution)/shard_map/all_gather | solution.py:239
  10.6 5.5 %copy-start.5 = (f32[4096]{0:T(1024)S(1)}, f32[4096]{0:T(1024)}, u32[]{:S(2)}) copy-start(f32[4096]{0:T(1024)} %param.4) | copy-start | bytes 49156
  10.6 22.0 %all-to-all-start = ((bf16[4,16,8,1152]{3,2,1,0:T(8,128)(2,1)}), bf16[4,16,8,1152]{3,2,1,0:T(8,128)(2,1)S(1)}, u32[]{:S(2)}, u32[]{:S(2)}) async-start(bf16[4,16,8,1152]{3,2,1,0:T(8,128)(2,1)} %copy.56), calls=%async_computation | async-start | bytes 2359296 | tf_op jit(solution)/shard_map/all_to_all | solution.py:250
  35.6 34.0 %all-to-all-start.1 = ((bf16[32,8,2688]{2,1,0:T(8,128)(2,1)}), bf16[32,8,2688]{2,1,0:T(8,128)(2,1)S(1)}, u32[]{:S(2)}, u32[]{:S(2)}) async-start(bf16[32,8,2688]{2,1,0:T(8,128)(2,1)} %concatenate.10), calls=%async_computation.1 | async-start | bytes 2752512 | tf_op jit(solution)/shard_map/all_to_all | solution.py:266
  69.6 5.8 %collective-permute-start.3 = (bf16[128,512]{1,0:T(8,128)(2,1)S(1)}, bf16[128,512]{1,0:T(8,128)(2,1)S(1)}, u32[]{:S(2)}, u32[]{:S(2)}) collective-permute-start(bf16[128,512]{1,0:T(8,128)(2,1)S(1)} %get-tuple-element.45), channel_id=1, source_target_pairs={{0,96},{32,0},{64,32},{96,64},{1,97},{33,1},{65,33},{97,65},{2,98}... | collective-permute-start | bytes 393224 | tf_op jit(solution)/shard_map/ppermute | solution.py:281
  69.6 9.5 %collective-permute-start.1 = (bf16[128,512]{1,0:T(8,128)(2,1)S(1)}, bf16[128,512]{1,0:T(8,128)(2,1)S(1)}, u32[]{:S(2)}, u32[]{:S(2)}) collective-permute-start(bf16[128,512]{1,0:T(8,128)(2,1)S(1)} %get-tuple-element.45), channel_id=1, source_target_pairs={{0,32},{32,64},{64,96},{96,0},{1,33},{33,65},{65,97},{97,1},{2,34}... | collective-permute-start | bytes 393224 | tf_op jit(solution)/shard_map/ppermute | solution.py:280
  71.7 7.5 %collective-permute-start.2 = (bf16[128,512]{1,0:T(8,128)(2,1)S(1)}, bf16[128,512]{1,0:T(8,128)(2,1)S(1)}, u32[]{:S(2)}, u32[]{:S(2)}) collective-permute-start(bf16[128,512]{1,0:T(8,128)(2,1)S(1)} %get-tuple-element.46), channel_id=1, source_target_pairs={{0,96},{32,0},{64,32},{96,64},{1,97},{33,1},{65,33},{97,65},{2,98}... | collective-permute-start | bytes 393224 | tf_op jit(solution)/shard_map/ppermute | solution.py:281
  73.0 6.2 %collective-permute-start = (bf16[128,512]{1,0:T(8,128)(2,1)S(1)}, bf16[128,512]{1,0:T(8,128)(2,1)S(1)}, u32[]{:S(2)}, u32[]{:S(2)}) collective-permute-start(bf16[128,512]{1,0:T(8,128)(2,1)S(1)} %get-tuple-element.46), channel_id=1, source_target_pairs={{0,32},{32,64},{64,96},{96,0},{1,33},{33,65},{65,97},{97,1},{2,34}... | collective-permute-start | bytes 393224 | tf_op jit(solution)/shard_map/ppermute | solution.py:280
  75.4 5.0 %collective-permute-start.5 = (bf16[128,512]{1,0:T(8,128)(2,1)S(1)}, bf16[128,512]{1,0:T(8,128)(2,1)S(1)}, u32[]{:S(2)}, u32[]{:S(2)}) collective-permute-start(bf16[128,512]{1,0:T(8,128)(2,1)S(1)} %collective-permute-done.3), channel_id=1, source_target_pairs={{0,96},{32,0},{64,32},{96,64},{1,97},{33,1},{65,33},{97,65},{2,98}... | collective-permute-start | bytes 393224 | tf_op jit(solution)/shard_map/ppermute | solution.py:282
  79.1 6.2 %collective-permute-start.4 = (bf16[128,512]{1,0:T(8,128)(2,1)S(1)}, bf16[128,512]{1,0:T(8,128)(2,1)S(1)}, u32[]{:S(2)}, u32[]{:S(2)}) collective-permute-start(bf16[128,512]{1,0:T(8,128)(2,1)S(1)} %collective-permute-done), channel_id=1, source_target_pairs={{0,32},{32,64},{64,96},{96,0},{1,33},{33,65},{65,97},{97,1},{2,34}... | collective-permute-start | bytes 393224 | tf_op jit(solution)/shard_map/ppermute | solution.py:282
  85.3 5.8 %copy-start.2 = (bf16[1024,512]{1,0:T(8,128)(2,1)}, bf16[1024,512]{1,0:T(8,128)(2,1)S(1)}, u32[]{:S(2)}) copy-start(bf16[1024,512]{1,0:T(8,128)(2,1)S(1)} %constant_dynamic-update-slice_fusion.mine_ref) | copy-start | bytes 3145732
  85.4 6.5 %collective-permute-start.6 = (bf16[1024,512]{1,0:T(8,128)(2,1)S(1)}, bf16[1024,512]{1,0:T(8,128)(2,1)}, u32[]{:S(2)}, u32[]{:S(2)}) collective-permute-start(bf16[1024,512]{1,0:T(8,128)(2,1)S(1)} %constant_dynamic-update-slice_fusion.mine_ref), channel_id=1, source_target_pairs={{0,1},{1,0},{2,3},{3,2},{4,5},{5,4},{6,7},{7,6},{8,9},{9,8},{10,11... | collective-permute-start | bytes 3145736 | tf_op jit(solution)/shard_map/ppermute | solution.py:285
  86.5 30.1 %copy-start.1 = (bf16[128,2048]{1,0:T(8,128)(2,1)}, bf16[128,2048]{1,0:T(8,128)(2,1)S(1)}, u32[]{:S(2)}) copy-start(bf16[128,2048]{1,0:T(8,128)(2,1)S(1)} %get-tuple-element.43.own1_ref) | copy-start | bytes 1572868
  86.5 24.3 %collective-permute-start.10 = (bf16[128,2048]{1,0:T(8,128)(2,1)S(1)}, bf16[128,2048]{1,0:T(8,128)(2,1)}, u32[]{:S(2)}, u32[]{:S(2)}) collective-permute-start(bf16[128,2048]{1,0:T(8,128)(2,1)S(1)} %get-tuple-element.43.own1_ref), channel_id=1, source_target_pairs={{0,96},{32,0},{64,32},{96,64},{1,97},{33,1},{65,33},{97,65},{2,98}... | collective-permute-start | bytes 1572872 | tf_op jit(solution)/shard_map/ppermute | solution.py:289
  86.5 24.3 %collective-permute-start.8 = (bf16[128,2048]{1,0:T(8,128)(2,1)S(1)}, bf16[128,2048]{1,0:T(8,128)(2,1)}, u32[]{:S(2)}, u32[]{:S(2)}) collective-permute-start(bf16[128,2048]{1,0:T(8,128)(2,1)S(1)} %get-tuple-element.43.own1_ref), channel_id=1, source_target_pairs={{0,32},{32,64},{64,96},{96,0},{1,33},{33,65},{65,97},{97,1},{2,34}... | collective-permute-start | bytes 1572872 | tf_op jit(solution)/shard_map/ppermute | solution.py:288
  88.5 23.5 %collective-permute-start.9 = (bf16[128,2048]{1,0:T(8,128)(2,1)}, bf16[128,2048]{1,0:T(8,128)(2,1)}, u32[]{:S(2)}, u32[]{:S(2)}) collective-permute-start(bf16[128,2048]{1,0:T(8,128)(2,1)} %get-tuple-element.44.own0_ref), channel_id=1, source_target_pairs={{0,96},{32,0},{64,32},{96,64},{1,97},{33,1},{65,33},{97,65},{2,98}... | collective-permute-start | bytes 1572872 | tf_op jit(solution)/shard_map/ppermute | solution.py:289
  89.7 23.5 %collective-permute-start.7 = (bf16[128,2048]{1,0:T(8,128)(2,1)}, bf16[128,2048]{1,0:T(8,128)(2,1)}, u32[]{:S(2)}, u32[]{:S(2)}) collective-permute-start(bf16[128,2048]{1,0:T(8,128)(2,1)} %get-tuple-element.44.own0_ref), channel_id=1, source_target_pairs={{0,32},{32,64},{64,96},{96,0},{1,33},{33,65},{65,97},{97,1},{2,34}... | collective-permute-start | bytes 1572872 | tf_op jit(solution)/shard_map/ppermute | solution.py:288
  91.3 27.5 %copy-start.6 = (f32[1,1,3,256]{3,1,2,0:T(1,128)}, f32[1,1,3,256]{3,1,2,0:T(1,128)S(1)}, u32[]{:S(2)}) copy-start(f32[1,1,3,256]{3,1,2,0:T(1,128)S(1)} %copy.69) | copy-start | bytes 9220
  113.3 14.8 %collective-permute-start.11 = (bf16[128,2048]{1,0:T(8,128)(2,1)}, bf16[128,2048]{1,0:T(8,128)(2,1)S(1)}, u32[]{:S(2)}, u32[]{:S(2)}) collective-permute-start(bf16[128,2048]{1,0:T(8,128)(2,1)} %collective-permute-done.7.below0_ref), channel_id=1, source_target_pairs={{0,32},{32,64},{64,96},{96,0},{1,33},{33,65},{65,97},{97,1},{2,34}... | collective-permute-start | bytes 1572872 | tf_op jit(solution)/shard_map/ppermute | solution.py:301
  113.8 14.3 %collective-permute-start.12 = (bf16[128,2048]{1,0:T(8,128)(2,1)}, bf16[128,2048]{1,0:T(8,128)(2,1)S(1)}, u32[]{:S(2)}, u32[]{:S(2)}) collective-permute-start(bf16[128,2048]{1,0:T(8,128)(2,1)} %collective-permute-done.10.above1_ref), channel_id=1, source_target_pairs={{0,96},{32,0},{64,32},{96,64},{1,97},{33,1},{65,33},{97,65},{2,98}... | collective-permute-start | bytes 1572872 | tf_op jit(solution)/shard_map/ppermute | solution.py:301
  128.1 0.8 copy-start.3
  128.1 1.0 copy-start.4
Sparse Core Ops, SparseCore 0:
  9.7 122.5 all-gather.1
